TPU v7x, 32 devices: a whole 2x2x4 slice. The times are simulated.
32 devices in a mesh: grp: 2 (over y), row: 4 (over z), col: 4 (over x, core).
Axes of the slice: x: 2, y: 2, z: 4, core: 2. Of those that a mesh axis runs over, the one named last changes fastest.
Arguments:
- sky_cube: bfloat16 [1024, 512, 512], P(('grp', 'row'), 'col'), parts along dimension 0, may hold values from -40 to 40
- half_widths: int32 [512], replicated, may hold values from 1 to 16, as said below
- pixel_mask: int32 [1024, 512], P(('grp', 'row'), 'col'), parts along dimension 0, may hold values 0 or 1
- foreground_modes: float32 [32, 512], P('grp'), parts along dimension 0, may hold values from -6 to 6
Outputs:
- spectrum: float32 [512, 2, 512, 512], P(('grp', 'row', 'col')), parts along dimension 0
- channel_weights: float32 [1024], P('grp'), parts along dimension 0
There are 2 independent parts, one for each index of `grp`. A program takes and returns all parts, laid end to end along the dimension named above; an argument that names none is the same for every part. Nothing has to cross between parts.
Inputs may be any that keep to these rules, and one draw needn't show every extreme that they name: `half_widths`: some channel has half-width exactly 16 and some exactly 1.
All inputs are finite; a program needn't handle non-finite values. No bound on the sum of `pixel_mask` on one device may be relied on, other than what follows from the above.
Results may differ from a plain program's by a relative error of at most 0.0087.
Values may be sent and summed in bfloat16 or wider, within the bound.
No kernel may reach another device: no remote copies, remote signals or barrier semaphores. Data moves between devices by JAX's collectives and lax.ppermute only.
A program may use at most 192 MiB of HBM per device.

v0:
```python
import math

import jax
import jax.numpy as jnp
from jax import lax
from jax.sharding import PartitionSpec as P

NR = 512
NC = 512
HALF = 16


highest = lax.Precision.HIGHEST


def padded(x, sides, width):
    for axis, dim in sides:
        size, length = (lax.axis_size(axis), x.shape[dim])
        up = [(i, (i + 1) % size) for i in range(size - 1)]
        down = [(j, i) for i, j in up]
        last = lax.slice_in_dim(x, length - width, length, axis=dim)
        initial = lax.slice_in_dim(x, 0, width, axis=dim)
        before = lax.ppermute(last, axis, up)
        after = lax.ppermute(initial, axis, down)
        x = jnp.concatenate([before, x, after], axis=dim)
    return x


def make_taps(half_widths):
    offsets = jnp.arange(2 * HALF + 1, dtype=jnp.int32) - HALF
    distance = offsets.astype(jnp.float32)[:, None]
    spread = half_widths.astype(jnp.float32)[None, :] * 0.5
    inside = jnp.abs(offsets)[:, None] <= half_widths[None, :]
    profile = jnp.where(
        inside, jnp.exp(-distance * distance / (2.0 * spread * spread)), jnp.float32(0.0)
    )
    return (profile / jnp.sum(profile, axis=0, keepdims=True)).astype(jnp.bfloat16)


def banded_taps(outputs, beam_taps):
    offsets = (
        jnp.arange(outputs + 2 * HALF, dtype=jnp.int32)[None, :]
        - jnp.arange(outputs, dtype=jnp.int32)[:, None]
    )
    one_hot = (
        offsets[:, :, None] == jnp.arange(2 * HALF + 1, dtype=jnp.int32)[None, None, :]
    ).astype(jnp.bfloat16)
    return jnp.einsum("oit,tf->oif", one_hot, beam_taps, preferred_element_type=jnp.float32).astype(
        jnp.bfloat16
    )


def window_taper(length):
    angles = 2.0 * math.pi * jnp.arange(length, dtype=jnp.int32).astype(jnp.float32) / (length - 1)
    return (
        0.35875
        - 0.48829 * jnp.cos(angles)
        + 0.14128 * jnp.cos(2.0 * angles)
        - 0.01168 * jnp.cos(3.0 * angles)
    )


def dft_table(length):
    indices = jnp.arange(length, dtype=jnp.int32)
    product = indices[:, None] * indices[None, :] % length
    angles = 2.0 * math.pi * product.astype(jnp.float32) / length
    cosine = jnp.cos(angles) / math.sqrt(length)
    sine_part = -jnp.sin(angles) / math.sqrt(length)
    table = jnp.stack([jnp.stack([cosine, -sine_part]), jnp.stack([sine_part, cosine])])
    return table.astype(jnp.bfloat16)


def tile_delay_table(channels, peers):
    per_device = channels // 2 // peers
    slot_index = jnp.arange(channels, dtype=jnp.int32)
    item_index = slot_index // (2 * peers)
    peer_index = slot_index // 2 % peers
    component = slot_index % 2
    delay_index = peer_index * per_device + item_index
    channel_index = jnp.arange(channels, dtype=jnp.int32)
    product = delay_index[:, None] * channel_index[None, :] % channels
    angles = 2.0 * math.pi * product.astype(jnp.float32) / channels
    rows_out = jnp.where(component[:, None] == 0, jnp.cos(angles), -jnp.sin(angles))
    return rows_out * (window_taper(channels) / math.sqrt(channels))[None, :]


def spatial_transform(regrouped):
    items = regrouped.shape[0]
    row_count = lax.axis_size("row")
    col_count = lax.axis_size("col")
    tile_rows = NR // row_count
    tile_cols = NC // col_count
    delay_slab = regrouped.reshape(items, 2, row_count, col_count, tile_rows, tile_cols)
    delay_slab = delay_slab.transpose(0, 1, 2, 4, 3, 5).reshape(items, 2, NR, NC)
    halfway = jnp.einsum(
        "kmrc,nmcd->knrd", delay_slab, dft_table(NC), preferred_element_type=jnp.float32
    )
    halfway = halfway.astype(jnp.bfloat16)
    return jnp.einsum("nmsr,kmrd->knsd", dft_table(NR), halfway, preferred_element_type=jnp.float32)


def body(sky_cube, half_widths, pixel_mask, foreground_modes):
    tile_rows, tile_cols, channels = sky_cube.shape
    beam_taps = make_taps(half_widths)
    row_band = banded_taps(tile_rows, beam_taps)
    extended = padded(sky_cube, (("row", 0),), HALF)
    row_part = jnp.einsum(
        "oif,icf->ocf", row_band, extended, preferred_element_type=jnp.float32
    ).astype(jnp.bfloat16)
    row_smoothed = padded(row_part, (("col", 1),), HALF)
    column_band = banded_taps(tile_cols, beam_taps)
    smoothed = jnp.einsum(
        "oif,rif->rof", column_band, row_smoothed, preferred_element_type=jnp.float32
    )
    masked = pixel_mask.astype(jnp.float32)[:, :, None] * smoothed
    pixels = masked.reshape(tile_rows * tile_cols, channels)
    peers = lax.axis_size("row") * lax.axis_size("col")
    delay_table = tile_delay_table(channels, peers)
    power_sum = lax.psum(jnp.sum(masked * masked, axis=(0, 1)), ("row", "col"))
    weights = 1.0 / (power_sum / (NR * NC) + 1e-05)
    channel_weights = weights / jnp.mean(weights)
    weighted_modes = foreground_modes * weights[None, :]
    normal_matrix = jnp.dot(
        weighted_modes, foreground_modes.T, precision=highest, preferred_element_type=jnp.float32
    )
    projected = jnp.dot(
        pixels, weighted_modes.T, precision=highest, preferred_element_type=jnp.float32
    )
    factor = jnp.linalg.cholesky(normal_matrix)
    amplitude = jax.scipy.linalg.cho_solve((factor, True), projected.T)
    cleaned = pixels - jnp.dot(
        amplitude.T, foreground_modes, precision=highest, preferred_element_type=jnp.float32
    )
    delay_tile = lax.dot_general(
        delay_table,
        cleaned,
        (((1,), (1,)), ((), ())),
        precision=highest,
        preferred_element_type=jnp.float32,
    )
    per_device = channels // 2 // peers
    sendable = delay_tile.astype(jnp.bfloat16).reshape(
        per_device, peers, 2, 1, 1, tile_rows * tile_cols
    )
    spectrum = spatial_transform(
        lax.all_to_all(sendable, ("row", "col"), split_axis=1, concat_axis=3, tiled=True)
    )
    return (spectrum, channel_weights)


def solution(mesh):
    return jax.shard_map(
        body,
        mesh=mesh,
        in_specs=(P(("grp", "row"), "col", None), P(), P(("grp", "row"), "col"), P("grp", None)),
        out_specs=(P(("grp", "row", "col"), None, None, None), P("grp")),
        check_vma=False,
    )
```

profile of v0, /device:TPU:11, one launch (start us, length us, event | category | flops | bytes accessed | tf_op | source)
XLA Modules:
  0.0 972.8 jit_solution(2164666601690065361)
XLA Ops:
  0.6 23.7 %copy.31 = bf16[128,128,512]{1,0,2:T(8,128)(2,1)} copy(bf16[128,128,512]{2,1,0:T(8,128)(2,1)} %param.4) | data formatting | bytes 33554432 | tf_op args[0]
  24.3 4.3 fusion.115
  28.6 3.2 collective-permute-start
  31.8 3.4 collective-permute-start.1
  35.4 10.5 %convolution_convert_fusion = bf16[128,160,512]{2,0,1:T(8,128)(2,1)} fusion(s32[128,160]{0,1:T(8,128)S(1)} %iota_subtract_fusion, f32[512]{0:T(512)S(1)} %fusion.70, f32[512]{0:T(512)S(1)} %multiply_multiply_fusion, f32[33]{0:T(128)S(1)} %negate_multiply_fusion.1, s32[512]{0:T(512)S(1)} %copy-done.2, s32[33]{0:T(128)S(1)} %fusion.102), kind=kOutput, calls=%fused_computation.25 | convolution fusion | flops 703306240 | bytes 21059848 | tf_op jit(solution)/shard_map/oit,tf->oif/dot_general | solution.py:48
  45.9 27.2 %copy.34 = bf16[128,160,512]{0,1,2:T(8,128)(2,1)} copy(bf16[128,160,512]{2,0,1:T(8,128)(2,1)} %convolution_convert_fusion) | data formatting | bytes 41943040 | tf_op jit(solution)/shard_map/convert_element_type | solution.py:48
  73.0 4.3 collective-permute-done
  77.3 2.7 collective-permute-done.1
  80.0 21.3 %convert_bitcast_fusion = bf16[128,128,512]{0,1,2:T(8,128)(2,1)} fusion(bf16[128,160,512]{0,1,2:T(8,128)(2,1)} %copy.34, bf16[16,128,512]{1,0,2:T(8,128)(2,1)} %collective-permute-done.1, bf16[128,128,512]{1,0,2:T(8,128)(2,1)} %copy.31, bf16[16,128,512]{1,0,2:T(8,128)(2,1)} %collective-permute-done), kind=kOutput, calls=%fused_computation.23 | convolution fusion | flops 2755657728 | bytes 58720256 | tf_op jit(solution)/shard_map/oif,icf->ocf/dot_general | solution.py:107
  101.3 3.0 fusion.114
  105.6 5.9 collective-permute-start.3
  111.6 4.3 fusion.136
  117.3 28.2 %fusion = (f32[512]{0:T(512)S(1)}, f32[512,128,128]{2,1,0:T(8,128)}) fusion(bf16[128,160,512]{0,1,2:T(8,128)(2,1)} %copy.34, bf16[128,16,512]{0,1,2:T(8,128)(2,1)} %collective-permute-done.3, bf16[128,128,512]{0,1,2:T(8,128)(2,1)} %convert_bitcast_fusion, bf16[128,16,512]{0,1,2:T(8,128)(2,1)} %copy-done.3, f32[128,128]{1,0:T(8,128)S(1)} %convert_element_type.77), kind=kOutput, calls=%fused_computation.3 | convolution fusion | flops 2772434432 | bytes 75565056 | tf_op jit(solution)/shard_map/oif,rif->rof/dot_general | solution.py:112
  145.5 40.3 %psum.7 = f32[512]{0:T(512)S(1)} all-reduce(f32[512]{0:T(512)S(1)} %get-tuple-element.18), channel_id=1, replica_groups=mesh['grp'=2,'row'=4,'col'=4] {'row','col'}, use_global_device_ids=true, to_apply=%region_2.3 | all-reduce | flops 512 | bytes 4096 | tf_op jit(solution)/shard_map/psum | solution.py:119
  186.6 43.2 %fusion.71 = f32[16,16384]{1,0:T(8,128)S(1)} fusion(f32[16,512]{1,0:T(8,128)S(1)} %copy-done, f32[512]{0:T(512)S(1)} %get-tuple-element.11, f32[64,8,128,128]{3,2,1,0:T(8,128)} %bitcast.104), kind=kOutput, calls=%fused_computation.73 | convolution fusion | flops 1610620928 | bytes 34637824 | tf_op jit(solution)/shard_map/dot_general | solution.py:126
  229.8 33.2 %copy.54 = f32[64,8,128,128]{3,1,2,0:T(8,128)} copy(f32[64,8,128,128]{3,2,1,0:T(8,128)} %bitcast.105) | data formatting | bytes 67108864
  263.1 1.5 cholesky.16
  267.1 33.4 %copy.37 = f32[16384,512]{1,0:T(8,128)} copy(f32[16384,512]{0,1:T(8,128)} %bitcast.106) | data formatting | bytes 67108864 | tf_op jit(solution)/shard_map/reshape | solution.py:116
  302.6 30.6 %fusion.116 = f32[16384,512]{1,0:T(8,128)} fusion(f32[16,16384]{1,0:T(8,128)S(1)} %fusion.86, f32[16,512]{1,0:T(8,128)S(1)} %copy-done), kind=kOutput, calls=%fused_computation.138 | convolution fusion | flops 1610612736 | bytes 34635776 | tf_op jit(solution)/shard_map/dot_general | solution.py:131
  333.2 59.7 %fusion.3 = bf16[512,16384]{1,0:T(8,128)(2,1)} fusion(f32[16384,512]{1,0:T(8,128)} %copy.37, f32[16384,512]{1,0:T(8,128)} %fusion.116, f32[512,512]{1,0:T(8,128)S(1)} %fusion.136), kind=kOutput, calls=%fused_computation.6 | convolution fusion | flops 51556384768 | bytes 84934656 | tf_op jit(solution)/shard_map/dot_general | solution.py:134
  392.9 27.0 %reshape.212 = bf16[16,16,2,1,1,16384]{5,2,1,0,4,3:T(2,128)(2,1)} reshape(bf16[512,16384]{1,0:T(8,128)(2,1)} %fusion.3) | data formatting | bytes 33554432 | tf_op jit(solution)/shard_map/reshape | solution.py:142
  419.9 14.3 %copy.38 = bf16[16,16,2,1,1,16384]{5,2,0,4,3,1:T(2,128)(2,1)} copy(bf16[16,16,2,1,1,16384]{5,2,1,0,4,3:T(2,128)(2,1)} %reshape.212) | data formatting | bytes 33554432 | tf_op jit(solution)/shard_map/reshape | solution.py:142
  434.1 15.8 %all-to-all-start = ((bf16[16,16,2,1,1,16384]{5,2,0,4,3,1:T(2,128)(2,1)}), bf16[16,16,2,1,1,16384]{5,2,0,4,3,1:T(2,128)(2,1)}, u32[]{:S(2)}, u32[]{:S(2)}) async-start(bf16[16,16,2,1,1,16384]{5,2,0,4,3,1:T(2,128)(2,1)} %copy.38), calls=%async_computation | async-start | bytes 33554432 | tf_op jit(solution)/shard_map/all_to_all | solution.py:146
  450.0 4.0 fusion.61
  454.0 4.4 negate_convert_fusion
  459.8 352.1 %all-to-all-done = bf16[16,16,2,1,1,16384]{5,2,0,4,3,1:T(2,128)(2,1)} async-done(((bf16[16,16,2,1,1,16384]{5,2,0,4,3,1:T(2,128)(2,1)}), bf16[16,16,2,1,1,16384]{5,2,0,4,3,1:T(2,128)(2,1)}, u32[]{:S(2)}, u32[]{:S(2)}) %all-to-all-start) | async-done | bytes 16777248 | tf_op jit(solution)/shard_map/all_to_all | solution.py:146
  812.0 27.9 %reshape.222 = bf16[16,2,4,4,128,128]{5,4,1,0,3,2:T(8,128)(2,1)} reshape(bf16[16,1,2,16,1,1,16384]{6,2,0,3,5,4,1:T(2,128)(2,1)} %bitcast.10) | data formatting | bytes 33554432 | tf_op jit(solution)/shard_map/reshape | solution.py:93
  839.8 20.0 %copy.40 = bf16[16,2,4,128,4,128]{5,4,3,2,1,0:T(4,128)(2,1)} copy(bf16[16,2,4,128,4,128]{5,3,1,0,4,2:T(8,128)(2,1)} %bitcast.107) | data formatting | bytes 33554432 | tf_op jit(solution)/shard_map/transpose | solution.py:94
  859.8 24.8 %reshape.217 = bf16[16,2,512,512,1]{3,2,1,0,4:T(8,128)(2,1)} reshape(bf16[16,2,4,128,4,128]{5,4,3,2,1,0:T(4,128)(2,1)} %copy.40) | data formatting | bytes 33554432 | tf_op jit(solution)/shard_map/reshape | solution.py:94
  884.7 25.9 %fusion.139 = bf16[16,2,512,512,1]{2,3,1,4,0:T(8,128)(2,1)} fusion(bf16[16,2,512,512,1]{3,2,1,0,4:T(8,128)(2,1)} %reshape.217, bf16[1,2,512,512]{2,3,1,0:T(8,128)(2,1)S(1)} %get-tuple-element.17, bf16[1,2,512,512]{2,3,1,0:T(8,128)(2,1)S(1)} %get-tuple-element.16), kind=kOutput, calls=%fused_computation.19.clone.clone.clone.clone.2 | convolution fusion | flops 17192452096 | bytes 35651584 | tf_op jit(solution)/shard_map/kmrc,nmcd->knrd/dot_general | solution.py:95
  910.6 27.1 %fusion.27 = f32[16,2,512,512]{2,3,1,0:T(8,128)} fusion(bf16[1,2,512,512]{2,3,1,0:T(8,128)(2,1)S(1)} %get-tuple-element.17, bf16[1,2,512,512]{2,3,1,0:T(8,128)(2,1)S(1)} %get-tuple-element.16, bf16[16,2,512,512,1]{2,3,1,4,0:T(8,128)(2,1)} %fusion.139), kind=kOutput, calls=%fused_computation.26 | convolution fusion | flops 17184063488 | bytes 52428800 | tf_op jit(solution)/shard_map/nmsr,kmrd->knsd/dot_general | solution.py:99
  937.7 34.8 %copy.42 = f32[16,2,512,512]{3,2,1,0:T(8,128)} copy(f32[16,2,512,512]{2,3,1,0:T(8,128)} %fusion.27) | data formatting | bytes 67108864
  (32 shorter events, 9.0 us)
Async XLA Ops:
  0.6 34.6 %copy-start.2 = (s32[512]{0:T(512)S(1)}, s32[512]{0:T(512)}, u32[]{:S(2)}) copy-start(s32[512]{0:T(512)} %param.5) | copy-start | bytes 6148
  28.6 48.7 %collective-permute-start = (bf16[16,128,512]{1,0,2:T(8,128)(2,1)}, bf16[16,128,512]{1,0,2:T(8,128)(2,1)}, u32[]{:S(2)}, u32[]{:S(2)}) collective-permute-start(bf16[16,128,512]{1,0,2:T(8,128)(2,1)} %get-tuple-element.14), channel_id=1, source_target_pairs={{0,4},{4,8},{8,12},{1,5},{5,9},{9,13},{2,6},{6,10},{10,14},{3,7},{... | collective-permute-start | bytes 6291464 | tf_op jit(solution)/shard_map/ppermute | solution.py:23
  31.8 48.2 %collective-permute-start.1 = (bf16[16,128,512]{1,0,2:T(8,128)(2,1)S(1)}, bf16[16,128,512]{1,0,2:T(8,128)(2,1)}, u32[]{:S(2)}, u32[]{:S(2)}) collective-permute-start(bf16[16,128,512]{1,0,2:T(8,128)(2,1)S(1)} %get-tuple-element.15), channel_id=1, source_target_pairs={{4,0},{8,4},{12,8},{5,1},{9,5},{13,9},{6,2},{10,6},{14,10},{7,3},{... | collective-permute-start | bytes 6291464 | tf_op jit(solution)/shard_map/ppermute | solution.py:24
  73.0 38.5 %copy-start.1 = (s32[128,128]{1,0:T(8,128)S(1)}, s32[128,128]{1,0:T(8,128)}, u32[]{:S(2)}) copy-start(s32[128,128]{1,0:T(8,128)} %param.6) | copy-start | bytes 196612
  104.3 11.7 %collective-permute-start.2 = (bf16[128,16,512]{0,1,2:T(8,128)(2,1)S(1)}, bf16[128,16,512]{0,1,2:T(8,128)(2,1)S(1)}, u32[]{:S(2)}, u32[]{:S(2)}) collective-permute-start(bf16[128,16,512]{0,1,2:T(8,128)(2,1)S(1)} %get-tuple-element.12), channel_id=1, source_target_pairs={{0,1},{1,2},{2,3},{4,5},{5,6},{6,7},{8,9},{9,10},{10,11},{12,13},{... | collective-permute-start | bytes 6291464 | tf_op jit(solution)/shard_map/ppermute | solution.py:23
  105.6 11.7 %collective-permute-start.3 = (bf16[128,16,512]{0,1,2:T(8,128)(2,1)S(1)}, bf16[128,16,512]{0,1,2:T(8,128)(2,1)}, u32[]{:S(2)}, u32[]{:S(2)}) collective-permute-start(bf16[128,16,512]{0,1,2:T(8,128)(2,1)S(1)} %get-tuple-element.13), channel_id=1, source_target_pairs={{1,0},{2,1},{3,2},{5,4},{6,5},{7,6},{9,8},{10,9},{11,10},{13,12},{... | collective-permute-start | bytes 6291464 | tf_op jit(solution)/shard_map/ppermute | solution.py:24
  115.9 70.5 %copy-start = (f32[16,512]{1,0:T(8,128)S(1)}, f32[16,512]{1,0:T(8,128)}, u32[]{:S(2)}) copy-start(f32[16,512]{1,0:T(8,128)} %param.7) | copy-start | bytes 98308
  115.9 1.3 copy-start.3
  434.1 377.8 %all-to-all-start = ((bf16[16,16,2,1,1,16384]{5,2,0,4,3,1:T(2,128)(2,1)}), bf16[16,16,2,1,1,16384]{5,2,0,4,3,1:T(2,128)(2,1)}, u32[]{:S(2)}, u32[]{:S(2)}) async-start(bf16[16,16,2,1,1,16384]{5,2,0,4,3,1:T(2,128)(2,1)} %copy.38), calls=%async_computation | async-start | bytes 33554432 | tf_op jit(solution)/shard_map/all_to_all | solution.py:146
where the time goes:
time: 983 us; the launch traced here: 973 us
  waiting for transfers between devices  359 us (37%)
  local copies, waits for them, and re-layouts  275 us (28%)
  matrix products  249 us (25%)
  blocking collectives  40.3 us (4%)
  starting transfers between devices  29.6 us (3%)
  other arithmetic  18.3 us (2%)
    all_to_all x1, waiting for transfers between devices, body(): lax.all_to_all(sendable, ('row', 'col'), split_axis=1, concat_axis=3, til...  352 us
    unnamed x11, local copies, waits for them, and re-layouts  93 us
    dot_general x1, matrix products, body(): lax.dot_general(delay_table, cleaned, (((1,), (1,)), ((), ())), precision...  59.7 us
    dot_general x1, matrix products, body(): jnp.dot(pixels, weighted_modes.T, precision=highest, preferred_element_ty...  43.2 us
    reshape x2, local copies, waits for them, and re-layouts, body(): delay_tile.astype(jnp.bfloat16)  41.3 us
    psum x1, blocking collectives, body(): power_sum = lax.psum(jnp.sum(masked * masked, axis=(0, 1)), ('row', 'col'))  40.3 us
    reshape x1, local copies, waits for them, and re-layouts, body(): pixels = masked.reshape(tile_rows * tile_cols, channels)  33.4 us
    dot_general x1, matrix products, body(): jnp.dot(amplitude.T, foreground_modes, precision=highest, preferred_eleme...  30.6 us
  transfers between devices with their start and end apart: 5, of which 3 were waited for; matrix products, arithmetic and copies ran while one was open for 5% of the time, Pallas kernels for 0%

commit v1 on v0

v1 whole, which is shorter than its diff:
```python
import functools
import math

import jax
import jax.numpy as jnp
import numpy as np
from jax import lax
from jax.experimental import pallas as pl
from jax.experimental.pallas import tpu as pltpu
from jax.sharding import PartitionSpec as P

HALF = 16
VMEM_LIMIT = 48 * 1024 * 1024
CHUNKS = 4

highest = lax.Precision.HIGHEST


def padded(x, sides, width):
    for axis, dim in sides:
        size, length = (lax.axis_size(axis), x.shape[dim])
        up = [(i, (i + 1) % size) for i in range(size - 1)]
        down = [(j, i) for i, j in up]
        last = lax.slice_in_dim(x, length - width, length, axis=dim)
        initial = lax.slice_in_dim(x, 0, width, axis=dim)
        before = lax.ppermute(last, axis, up)
        after = lax.ppermute(initial, axis, down)
        x = jnp.concatenate([before, x, after], axis=dim)
    return x


def make_taps(half_widths):
    offsets = jnp.arange(2 * HALF + 1, dtype=jnp.int32) - HALF
    distance = offsets.astype(jnp.float32)[:, None]
    spread = half_widths.astype(jnp.float32)[None, :] * 0.5
    inside = jnp.abs(offsets)[:, None] <= half_widths[None, :]
    profile = jnp.where(
        inside, jnp.exp(-distance * distance / (2.0 * spread * spread)), jnp.float32(0.0)
    )
    return (profile / jnp.sum(profile, axis=0, keepdims=True)).astype(jnp.bfloat16)


def banded_taps(outputs, beam_taps):
    offsets = (
        jnp.arange(outputs + 2 * HALF, dtype=jnp.int32)[None, :]
        - jnp.arange(outputs, dtype=jnp.int32)[:, None]
    )
    one_hot = (
        offsets[:, :, None] == jnp.arange(2 * HALF + 1, dtype=jnp.int32)[None, None, :]
    ).astype(jnp.bfloat16)
    return jnp.einsum("oit,tf->oif", one_hot, beam_taps, preferred_element_type=jnp.float32).astype(
        jnp.bfloat16
    )


def window_taper(length):
    angles = 2.0 * math.pi * np.arange(length) / (length - 1)
    return (
        0.35875
        - 0.48829 * np.cos(angles)
        + 0.14128 * np.cos(2.0 * angles)
        - 0.01168 * np.cos(3.0 * angles)
    )


def dft_parts(length):
    indices = np.arange(length)
    angles = 2.0 * math.pi * (indices[:, None] * indices[None, :] % length) / length
    scale = 1.0 / math.sqrt(length)
    return (
        (np.cos(angles) * scale).astype(jnp.bfloat16),
        (-np.sin(angles) * scale).astype(jnp.bfloat16),
    )


def delay_rows(channels, peers, sizes):
    per_device = channels // 2 // peers
    order, start = [], 0
    for size in sizes:
        for peer in range(peers):
            order.extend(peer * per_device + start + item for item in range(size))
        start += size
    delays = np.asarray(order)
    channel = np.arange(channels)
    angles = 2.0 * math.pi * (delays[:, None] * channel[None, :] % channels) / channels
    rows = np.stack([np.cos(angles), -np.sin(angles)], axis=1).reshape(channels, channels)
    return (rows * (window_taper(channels) / math.sqrt(channels))[None, :]).astype(np.float32)


def tap_table():
    distance = np.arange(HALF + 1, dtype=np.float32)
    table = np.zeros((HALF, HALF + 1), np.float32)
    for width in range(1, HALF + 1):
        spread = np.float32(width) * np.float32(0.5)
        profile = np.exp(-distance * distance / (np.float32(2.0) * spread * spread))
        profile = np.where(distance <= width, profile, np.float32(0.0)).astype(np.float32)
        total = profile[0] + np.float32(2.0) * np.sum(profile[1:], dtype=np.float32)
        table[width - 1] = profile / total
    return table


def band_table(out_places, in_places):
    taps = np.concatenate([tap_table(), np.zeros((HALF, 1), np.float32)], axis=1)
    distance = np.abs(np.asarray(out_places)[:, None] - np.asarray(in_places)[None, :])
    return taps[:, np.minimum(distance, HALF + 1)].astype(jnp.bfloat16)


def smooth_kernel(row_pieces, side_pieces, widths, mask, row_band, side_band, col_band, *refs):
    rows, sides = refs[:row_pieces], refs[row_pieces : row_pieces + side_pieces]
    high, low, power, staged = refs[row_pieces + side_pieces :]
    block = rows[0].shape[0]
    outputs, columns = mask.shape
    first = pl.program_id(0) * block
    kept = mask[...]
    for j in range(block):
        width = widths[first + j] - 1
        data = jnp.concatenate([piece[j] for piece in rows], axis=0)
        side = jnp.concatenate([piece[j] for piece in sides], axis=1)
        centre = jnp.dot(row_band[width], data, preferred_element_type=jnp.float32)
        edge = jnp.dot(side, side_band[width], preferred_element_type=jnp.float32)
        smoothed_rows = jnp.concatenate(
            [centre.astype(jnp.bfloat16), edge.T.astype(jnp.bfloat16)], axis=1
        )
        smoothed = jnp.dot(smoothed_rows, col_band[width], preferred_element_type=jnp.float32)
        staged[pl.ds(j, outputs, stride=block), :] = smoothed * kept

    group = 8

    def split(step, total):
        start = pl.multiple_of(step * group, group)
        value = staged[pl.ds(pl.multiple_of(start * block, group * block), group * block), :]
        rounded = value.astype(jnp.bfloat16)
        rest = (value - rounded.astype(jnp.float32)).astype(jnp.bfloat16)
        high[pl.ds(start, group)] = rounded.reshape(group, block, columns)
        low[pl.ds(start, group)] = rest.reshape(group, block, columns)
        return total + jnp.sum((value * value).reshape(group, block, columns), axis=0)

    power[...] = lax.fori_loop(
        0, outputs // group, split, jnp.zeros((block, columns), jnp.float32)
    )


def smooth(half_widths, mask, rows, sides, tables, block=16):
    channels, _, columns = rows[0].shape
    outputs = mask.shape[0]
    whole = lambda shape: pl.BlockSpec(shape, lambda i: (0,) * len(shape))
    piece = lambda x: pl.BlockSpec((block,) + x.shape[1:], lambda i: (i, 0, 0))
    split_spec = pl.BlockSpec((outputs, block, columns), lambda i: (0, i, 0))
    split_shape = jax.ShapeDtypeStruct((outputs, channels, columns), jnp.bfloat16)
    return pl.pallas_call(
        functools.partial(smooth_kernel, len(rows), len(sides)),
        grid=(channels // block,),
        in_specs=[pl.BlockSpec(memory_space=pltpu.SMEM), whole(mask.shape)]
        + [whole(t.shape) for t in tables]
        + [piece(x) for x in rows + sides],
        out_specs=[split_spec, split_spec, pl.BlockSpec((block, columns), lambda i: (i, 0))],
        out_shape=[
            split_shape,
            split_shape,
            jax.ShapeDtypeStruct((channels, columns), jnp.float32),
        ],
        scratch_shapes=[pltpu.VMEM((outputs * block, columns), jnp.float32)],
        compiler_params=pltpu.CompilerParams(vmem_limit_bytes=VMEM_LIMIT),
        cost_estimate=pl.CostEstimate(
            flops=4 * channels * outputs * columns * 160, bytes_accessed=80_000_000, transcendentals=0
        ),
        name="smooth",
    )(half_widths, mask, *tables, *rows, *sides)


def delay_kernel(modes, high, low, out, staged):
    rows = high.shape[0]
    count, _, columns = out.shape
    for pair in range(rows // 2):
        first, second = 2 * pair, 2 * pair + 1
        coarse = jnp.concatenate([high[first], high[second]], axis=1)
        fine = jnp.concatenate([low[first], low[second]], axis=1)
        both = jnp.dot(modes[...], coarse, preferred_element_type=jnp.float32)
        value = both[:count] + both[count:]
        value = value + jnp.dot(modes[:count], fine, preferred_element_type=jnp.float32)
        staged[pl.ds(first, count, stride=rows), :] = value[:, :columns]
        staged[pl.ds(second, count, stride=rows), :] = value[:, columns:]
    out[...] = staged[...].reshape(count, rows, columns).astype(jnp.bfloat16)


def delay_chunk(matrix, high, low, block=16):
    tile_rows, channels, columns = high.shape
    count = matrix.shape[0] // 2
    spec = pl.BlockSpec((block, channels, columns), lambda i: (i, 0, 0))
    return pl.pallas_call(
        delay_kernel,
        grid=(tile_rows // block,),
        in_specs=[pl.BlockSpec(matrix.shape, lambda i: (0, 0)), spec, spec],
        out_specs=pl.BlockSpec((count, block, columns), lambda i: (0, i, 0)),
        out_shape=jax.ShapeDtypeStruct((count, tile_rows, columns), jnp.bfloat16),
        scratch_shapes=[pltpu.VMEM((count * block, columns), jnp.float32)],
        compiler_params=pltpu.CompilerParams(vmem_limit_bytes=VMEM_LIMIT),
        cost_estimate=pl.CostEstimate(
            flops=6 * count * channels * tile_rows * columns,
            bytes_accessed=40_000_000,
            transcendentals=0,
        ),
        name="delays",
    )(matrix, high, low)


def spatial_kernel(row_count, col_count, has_previous, slab, col_table, row_table, *refs):
    out, halfway = refs[-2:]
    _, _, tile_rows, _ = slab.shape
    side = row_count * tile_rows
    for a in range(row_count):
        line = jnp.concatenate(
            [slab[a * col_count + b, k] for k in range(2) for b in range(col_count)], axis=1
        )
        part = jnp.dot(line, col_table[...], preferred_element_type=jnp.float32)
        part = part.astype(jnp.bfloat16)
        columns = part.shape[1] // 2
        halfway[pl.ds(a * tile_rows, tile_rows), :] = part[:, :columns]
        halfway[pl.ds(side + a * tile_rows, tile_rows), :] = part[:, columns:]
    step = side // 2
    for k in range(2):
        for s in range(side // step):
            rows = row_table[pl.ds(k * side + s * step, step), :]
            out[0, k, pl.ds(s * step, step), :] = jnp.dot(
                rows, halfway[...], preferred_element_type=jnp.float32
            )


def spatial_chunk(received, col_table, row_table, shape, start, previous):
    peers, parts, tile_rows, tile_cols = received.shape
    items = parts // 2
    side, columns = shape[2], shape[3]
    in_specs = [
        pl.BlockSpec((peers, 2, tile_rows, tile_cols), lambda i: (0, i, 0, 0)),
        pl.BlockSpec(col_table.shape, lambda i: (0, 0)),
        pl.BlockSpec(row_table.shape, lambda i: (0, 0)),
    ]
    operands = [received, col_table, row_table]
    aliases = {}
    if previous is not None:
        in_specs.append(pl.BlockSpec(memory_space=pl.ANY))
        operands.append(previous)
        aliases = {3: 0}
    return pl.pallas_call(
        functools.partial(
            spatial_kernel, side // tile_rows, columns // tile_cols, previous is not None
        ),
        grid=(items,),
        in_specs=in_specs,
        out_specs=pl.BlockSpec((1, 2, side, columns), lambda i: (start + i, 0, 0, 0)),
        out_shape=jax.ShapeDtypeStruct(shape, jnp.float32),
        scratch_shapes=[pltpu.VMEM((2 * side, columns), jnp.bfloat16)],
        input_output_aliases=aliases,
        compiler_params=pltpu.CompilerParams(vmem_limit_bytes=VMEM_LIMIT),
        cost_estimate=pl.CostEstimate(
            flops=16 * items * side * side * columns,
            bytes_accessed=items * 12 * side * columns,
            transcendentals=0,
        ),
        name="spatial",
    )(*operands)


def shifted(x, steps):
    axes = tuple(axis for axis, _ in steps)
    sizes = [lax.axis_size(axis) for axis in axes]
    pairs = []
    for place in np.ndindex(*sizes):
        target = [p + s for p, (_, s) in zip(place, steps)]
        if all(0 <= t < n for t, n in zip(target, sizes)):
            pairs.append(
                (int(np.ravel_multi_index(place, sizes)), int(np.ravel_multi_index(target, sizes)))
            )
    return lax.ppermute(x, axes if len(axes) > 1 else axes[0], pairs)


def split_high_low(x):
    rounded = x.astype(jnp.bfloat16)
    return rounded, (x - rounded.astype(jnp.float32)).astype(jnp.bfloat16)


def tiled_body(sky_cube, half_widths, pixel_mask, foreground_modes):
    tile_rows, tile_cols, channels = sky_cube.shape
    row_count, col_count = lax.axis_size("row"), lax.axis_size("col")
    peers = row_count * col_count
    per_device = channels // 2 // peers
    sides, columns = row_count * tile_rows, col_count * tile_cols

    top = shifted(sky_cube[-HALF:], (("row", 1),))
    bottom = shifted(sky_cube[:HALF], (("row", -1),))
    left = shifted(sky_cube[:, -HALF:], (("col", 1),))
    right = shifted(sky_cube[:, :HALF], (("col", -1),))
    corners = [
        [
            shifted(
                sky_cube[(slice(-HALF, None) if v > 0 else slice(0, HALF))][
                    :, (slice(-HALF, None) if h > 0 else slice(0, HALF))
                ],
                (("row", v), ("col", h)),
            )
            for h in (1, -1)
        ]
        for v in (1, -1)
    ]
    centre_t = jnp.transpose(sky_cube, (2, 0, 1))
    caps_t = jnp.transpose(jnp.concatenate([top, bottom], axis=0), (2, 0, 1))
    flank_t = jnp.transpose(jnp.concatenate([left, right], axis=1), (2, 1, 0))
    corner = jnp.concatenate([jnp.concatenate(line, axis=1) for line in corners], axis=0)
    corner_t = jnp.transpose(corner, (2, 1, 0))

    def places(length):
        return list(range(length)) + list(range(-HALF, 0)) + list(range(length, length + HALF))

    out_rows = list(range(tile_rows))
    row_band = band_table(out_rows, places(tile_rows))
    side_band = np.swapaxes(row_band, 1, 2)
    col_band = np.swapaxes(band_table(list(range(tile_cols)), places(tile_cols)), 1, 2)
    high, low, power = smooth(
        half_widths,
        pixel_mask.astype(jnp.float32),
        [centre_t, caps_t],
        [flank_t, corner_t],
        [row_band, side_band, col_band],
    )

    chunks = math.gcd(CHUNKS, per_device)
    sizes = [per_device // chunks] * chunks
    delay_table = delay_rows(channels, peers, sizes)
    mode_delays = jnp.dot(
        delay_table, foreground_modes.T, precision=highest, preferred_element_type=jnp.float32
    )
    power_sum = lax.psum(jnp.sum(power, axis=1), ("row", "col"))
    weights = 1.0 / (power_sum / (sides * columns) + 1e-05)
    channel_weights = weights / jnp.mean(weights)
    weighted_modes = foreground_modes * weights[None, :]
    normal_matrix = jnp.dot(
        weighted_modes, foreground_modes.T, precision=highest, preferred_element_type=jnp.float32
    )
    factor = jnp.linalg.cholesky(normal_matrix)
    solved = jax.scipy.linalg.cho_solve((factor, True), weighted_modes)
    matrix = delay_table - jnp.dot(
        mode_delays, solved, precision=highest, preferred_element_type=jnp.float32
    )
    matrix_high, matrix_low = split_high_low(matrix)

    cos_c, sin_c = dft_parts(columns)
    col_table = np.block([[cos_c, sin_c], [-sin_c, cos_c]])
    cos_r, sin_r = dft_parts(sides)
    row_table = np.block([[cos_r, -sin_r], [sin_r, cos_r]])

    spectrum = None
    start = 0
    for size in sizes:
        begin, count = 2 * start * peers, 2 * size * peers
        both = jnp.concatenate(
            [matrix_high[begin : begin + count], matrix_low[begin : begin + count]], axis=0
        )
        delays = delay_chunk(both, high, low)
        delays = delays.reshape(peers, 2 * size, tile_rows, tile_cols)
        received = lax.all_to_all(delays, ("row", "col"), split_axis=0, concat_axis=0, tiled=True)
        spectrum = spatial_chunk(
            received, col_table, row_table, (per_device, 2, sides, columns), start, spectrum
        )
        start += size
    return (spectrum, channel_weights)


def small_tile_body(sky_cube, half_widths, pixel_mask, foreground_modes):
    tile_rows, tile_cols, channels = sky_cube.shape
    row_count, col_count = lax.axis_size("row"), lax.axis_size("col")
    peers = row_count * col_count
    per_device = channels // 2 // peers
    sides, columns = row_count * tile_rows, col_count * tile_cols
    beam_taps = make_taps(half_widths)
    extended = padded(sky_cube, (("row", 0),), HALF)
    row_part = jnp.einsum(
        "oif,icf->ocf",
        banded_taps(tile_rows, beam_taps),
        extended,
        preferred_element_type=jnp.float32,
    ).astype(jnp.bfloat16)
    row_smoothed = padded(row_part, (("col", 1),), HALF)
    smoothed = jnp.einsum(
        "oif,rif->rof",
        banded_taps(tile_cols, beam_taps),
        row_smoothed,
        preferred_element_type=jnp.float32,
    )
    masked = pixel_mask.astype(jnp.float32)[:, :, None] * smoothed
    pixels = masked.reshape(tile_rows * tile_cols, channels)
    power_sum = lax.psum(jnp.sum(masked * masked, axis=(0, 1)), ("row", "col"))
    weights = 1.0 / (power_sum / (sides * columns) + 1e-05)
    channel_weights = weights / jnp.mean(weights)
    weighted_modes = foreground_modes * weights[None, :]
    normal_matrix = jnp.dot(
        weighted_modes, foreground_modes.T, precision=highest, preferred_element_type=jnp.float32
    )
    projected = jnp.dot(
        pixels, weighted_modes.T, precision=highest, preferred_element_type=jnp.float32
    )
    factor = jnp.linalg.cholesky(normal_matrix)
    amplitude = jax.scipy.linalg.cho_solve((factor, True), projected.T)
    cleaned = pixels - jnp.dot(
        amplitude.T, foreground_modes, precision=highest, preferred_element_type=jnp.float32
    )
    delay_tile = lax.dot_general(
        delay_rows(channels, peers, [per_device]),
        cleaned,
        (((1,), (1,)), ((), ())),
        precision=highest,
        preferred_element_type=jnp.float32,
    )
    sendable = delay_tile.astype(jnp.bfloat16).reshape(
        peers, per_device, 2, tile_rows, tile_cols
    )
    regrouped = lax.all_to_all(sendable, ("row", "col"), split_axis=0, concat_axis=0, tiled=True)
    slab = regrouped.reshape(row_count, col_count, per_device, 2, tile_rows, tile_cols)
    slab = slab.transpose(2, 3, 0, 4, 1, 5).reshape(per_device, 2, sides, columns)
    cos_c, sin_c = dft_parts(columns)
    col_table = np.stack([np.stack([cos_c, -sin_c]), np.stack([sin_c, cos_c])])
    cos_r, sin_r = dft_parts(sides)
    row_table = np.stack([np.stack([cos_r, -sin_r]), np.stack([sin_r, cos_r])])
    halfway = jnp.einsum(
        "kmrc,nmcd->knrd", slab, col_table, preferred_element_type=jnp.float32
    ).astype(jnp.bfloat16)
    spectrum = jnp.einsum(
        "nmsr,kmrd->knsd", row_table, halfway, preferred_element_type=jnp.float32
    )
    return (spectrum, channel_weights)


def body(sky_cube, half_widths, pixel_mask, foreground_modes):
    tile_rows, tile_cols, channels = sky_cube.shape
    fits = tile_rows % 128 == 0 and tile_cols % 128 == 0 and channels % 128 == 0
    run = tiled_body if fits else small_tile_body
    return run(sky_cube, half_widths, pixel_mask, foreground_modes)


def solution(mesh):
    return jax.shard_map(
        body,
        mesh=mesh,
        in_specs=(P(("grp", "row"), "col", None), P(), P(("grp", "row"), "col"), P("grp", None)),
        out_specs=(P(("grp", "row", "col"), None, None, None), P("grp")),
        check_vma=False,
    )
```

time: 983 us -> 736 us (0.75)
  matrix products: 249 us -> 2.49 us
  Pallas kernels: 0 us -> 237 us
  local copies, waits for them, and re-layouts: 275 us -> 61.1 us
  starting transfers between devices: 29.6 us -> 53.4 us
  waiting for transfers between devices: 359 us -> 339 us
  blocking collectives: 40.3 us -> 24.3 us
    dot_general x9 -> x3, matrix products: 247 us -> 2.1 us  [the longest x1 1 us: tiled_body(): jnp.dot(mode_delays, solved, precision=highest, preferred_element_type=jn...]
    pallas_call x0 -> x9, Pallas kernels: none -> 237 us  [the longest x1 127 us: smooth(): pl.pallas_call(functools.partial(smooth_kernel, len(rows), len(sides)), g...]
    reshape x5 -> x0, local copies, waits for them, and re-layouts: 127 us -> none  [the longest x2 41.3 us: body(): delay_tile.astype(jnp.bfloat16)]
    all_to_all x1 -> x4, waiting for transfers between devices: 352 us -> 279 us  [tiled_body(): lax.all_to_all(delays, ('row', 'col'), split_axis=0, concat_axis=0, tiled...]
    ppermute x4 -> x8, waiting for transfers between devices: 6.98 us -> 60.1 us  [shifted(): return lax.ppermute(x, axes if len(axes) > 1 else axes[0], pairs)]
    unnamed x11 -> x29, local copies, waits for them, and re-layouts: 93 us -> 43.6 us
    convert_element_type x1 -> x0, local copies, waits for them, and re-layouts: 27.2 us -> none  [banded_taps(): jnp.einsum('oit,tf->oif', one_hot, beam_taps, preferred_element_type=jnp....]
    transpose x1 -> x0, local copies, waits for them, and re-layouts: 20 us -> none  [spatial_transform(): delay_slab.transpose(0, 1, 2, 4, 3, 5).reshape(items, 2, NR, NC)]
  transfers between devices with their start and end apart: 5 -> 12, of which waited for: 3 -> 8; matrix products, arithmetic and copies ran while one was open for 5% -> 6% of each run, Pallas kernels for 0% -> 11%
where the time goes in v1:
time: 736 us; the launch traced here: 734 us
  waiting for transfers between devices  339 us (46%)
  Pallas kernels  237 us (32%)
  local copies, waits for them, and re-layouts  61.1 us (8%)
  starting transfers between devices  53.4 us (7%)
  blocking collectives  24.3 us (3%)
  other arithmetic  15.5 us (2%)
    all_to_all x4, waiting for transfers between devices, tiled_body(): lax.all_to_all(delays, ('row', 'col'), split_axis=0, concat_axis=0, tiled...  279 us
    pallas_call x1, Pallas kernels, smooth(): pl.pallas_call(functools.partial(smooth_kernel, len(rows), len(sides)), g...  127 us
    pallas_call x4, Pallas kernels, delay_chunk(): pl.pallas_call(delay_kernel, grid=(tile_rows // block,), in_specs=[pl.Blo...  61.5 us
    ppermute x8, waiting for transfers between devices, shifted(): return lax.ppermute(x, axes if len(axes) > 1 else axes[0], pairs)  60.1 us
    pallas_call x4, Pallas kernels, spatial_chunk(): pl.pallas_call(functools.partial(spatial_kernel, side // tile_rows, colum...  48.1 us
    unnamed x29, local copies, waits for them, and re-layouts  43.6 us
    all_to_all x4, starting transfers between devices, tiled_body(): lax.all_to_all(delays, ('row', 'col'), split_axis=0, concat_axis=0, tiled...  30.2 us
    psum x1, blocking collectives, tiled_body(): power_sum = lax.psum(jnp.sum(power, axis=1), ('row', 'col'))  24.3 us
  transfers between devices with their start and end apart: 12, of which 8 were waited for; matrix products, arithmetic and copies ran while one was open for 6% of the time, Pallas kernels for 11%

profile of v1, /device:TPU:11, one launch (start us, length us, event | category | flops | bytes accessed | tf_op | source)
XLA Modules:
  0.0 734.3 jit_solution(8188824023810874707)
XLA Ops:
  0.6 4.0 fusion.15
  4.6 5.1 copy.33
  9.7 3.9 collective-permute-start.3
  13.7 3.9 copy.32
  18.9 23.5 %copy.25 = bf16[128,128,512]{1,0,2:T(8,128)(2,1)} copy(bf16[128,128,512]{2,1,0:T(8,128)(2,1)} %param.10) | data formatting | bytes 33554432 | tf_op args[0]
  42.3 5.1 fusion.16
  56.6 43.5 %collective-permute-done.4 = bf16[16,16,512]{2,1,0:T(8,128)(2,1)S(1)} collective-permute-done((bf16[16,16,512]{2,1,0:T(8,128)(2,1)S(1)}, bf16[16,16,512]{2,1,0:T(8,128)(2,1)S(1)}, u32[]{:S(2)}, u32[]{:S(2)}) %collective-permute-start.4) | collective-permute-done | bytes 262176 | tf_op jit(solution)/shard_map/ppermute | solution.py:274
  100.1 5.4 collective-permute-start.5
  105.5 4.9 collective-permute-done.5
  113.9 5.9 collective-permute-done.7
  122.2 5.8 collective-permute-done.6
  128.1 6.9 copy.30
  135.0 4.9 maximum_bitcast_fusion.1.refs_2_
  139.9 5.0 maximum_bitcast_fusion.refs_1_
  144.9 127.4 %smooth.1 = (bf16[128,512,128]{2,1,0:T(8,128)(2,1)}, bf16[128,512,128]{2,1,0:T(8,128)(2,1)}, f32[512,128]{1,0:T(8,128)S(1)}) custom-call(s32[512]{0:T(512)S(1)} %copy-done.9, f32[128,128]{1,0:T(8,128)S(1)} %convert_element_type.12.mask, bf16[16,128,160]{2,1,0:T(8,128)(2,1)S(1)} %copy-done.8, bf16[16,160,128]{2,1,0:T(8,128)(2,1)S(1)} %copy-done.7, ...), custom_call_target="tpu_custom_call" | custom-call | flops 5368709120 | bytes 80000000 | tf_op jit(solution)/shard_map/smooth/pallas_call | solution.py:150
  272.5 24.3 %psum.7 = f32[512]{0:T(512)S(1)} all-reduce(f32[512]{0:T(512)S(1)} %reduce_sum.18), channel_id=1, replica_groups=mesh['grp'=2,'row'=4,'col'=4] {'row','col'}, use_global_device_ids=true, to_apply=%region_1.0 | all-reduce | flops 512 | bytes 4096 | tf_op jit(solution)/shard_map/psum | solution.py:332
  303.2 15.4 %delays.5 = bf16[128,128,128]{2,1,0:T(8,128)(2,1)S(1)} custom-call(bf16[256,512]{1,0:T(8,128)(2,1)S(1)} %pad_maximum_fusion.1.modes, bf16[128,512,128]{2,1,0:T(8,128)(2,1)} %get-tuple-element.6.high, bf16[128,512,128]{2,1,0:T(8,128)(2,1)} %get-tuple-element.7.low), custom_call_target="tpu_custom_call" | custom-call | flops 6442450944 | bytes 40000000 | tf_op jit(solution)/shard_map/delays/pallas_call | solution.py:190
  320.6 15.3 %all-to-all-start.1 = ((bf16[16,8,128,128]{3,2,1,0:T(8,128)(2,1)}), bf16[16,8,128,128]{3,2,1,0:T(8,128)(2,1)}, u32[]{:S(2)}, u32[]{:S(2)}) async-start(bf16[16,8,128,128]{3,2,1,0:T(8,128)(2,1)} %bitcast.30), calls=%async_computation.1 | async-start | bytes 8388608 | tf_op jit(solution)/shard_map/all_to_all | solution.py:360
  335.9 15.4 %delays.6 = bf16[128,128,128]{2,1,0:T(8,128)(2,1)S(1)} custom-call(bf16[256,512]{1,0:T(8,128)(2,1)S(1)} %pad_maximum_fusion.2.modes, bf16[128,512,128]{2,1,0:T(8,128)(2,1)} %get-tuple-element.6.high, bf16[128,512,128]{2,1,0:T(8,128)(2,1)} %get-tuple-element.7.low), custom_call_target="tpu_custom_call" | custom-call | flops 6442450944 | bytes 40000000 | tf_op jit(solution)/shard_map/delays/pallas_call | solution.py:190
  353.3 75.1 %all-to-all-done.1.slab = bf16[16,8,128,128]{3,2,1,0:T(8,128)(2,1)} async-done(((bf16[16,8,128,128]{3,2,1,0:T(8,128)(2,1)}), bf16[16,8,128,128]{3,2,1,0:T(8,128)(2,1)}, u32[]{:S(2)}, u32[]{:S(2)}) %all-to-all-start.1) | async-done | bytes 4194336 | tf_op jit(solution)/shard_map/all_to_all | solution.py:360
  428.4 4.9 all-to-all-start.2
  433.3 15.4 %delays.7 = bf16[128,128,128]{2,1,0:T(8,128)(2,1)S(1)} custom-call(bf16[256,512]{1,0:T(8,128)(2,1)S(1)} %pad_maximum_fusion.3.modes, bf16[128,512,128]{2,1,0:T(8,128)(2,1)} %get-tuple-element.6.high, bf16[128,512,128]{2,1,0:T(8,128)(2,1)} %get-tuple-element.7.low), custom_call_target="tpu_custom_call" | custom-call | flops 6442450944 | bytes 40000000 | tf_op jit(solution)/shard_map/delays/pallas_call | solution.py:190
  450.7 75.0 %all-to-all-done.2.slab = bf16[16,8,128,128]{3,2,1,0:T(8,128)(2,1)} async-done(((bf16[16,8,128,128]{3,2,1,0:T(8,128)(2,1)}), bf16[16,8,128,128]{3,2,1,0:T(8,128)(2,1)}, u32[]{:S(2)}, u32[]{:S(2)}) %all-to-all-start.2) | async-done | bytes 4194336 | tf_op jit(solution)/shard_map/all_to_all | solution.py:360
  525.8 4.9 all-to-all-start.3
  530.7 15.4 %delays.4 = bf16[128,128,128]{2,1,0:T(8,128)(2,1)S(1)} custom-call(bf16[256,512]{1,0:T(8,128)(2,1)S(1)} %pad_maximum_fusion.modes, bf16[128,512,128]{2,1,0:T(8,128)(2,1)} %get-tuple-element.6.high, bf16[128,512,128]{2,1,0:T(8,128)(2,1)} %get-tuple-element.7.low), custom_call_target="tpu_custom_call" | custom-call | flops 6442450944 | bytes 40000000 | tf_op jit(solution)/shard_map/delays/pallas_call | solution.py:190
  548.1 75.1 %all-to-all-done.3.slab = bf16[16,8,128,128]{3,2,1,0:T(8,128)(2,1)} async-done(((bf16[16,8,128,128]{3,2,1,0:T(8,128)(2,1)}), bf16[16,8,128,128]{3,2,1,0:T(8,128)(2,1)}, u32[]{:S(2)}, u32[]{:S(2)}) %all-to-all-start.3) | async-done | bytes 4194336 | tf_op jit(solution)/shard_map/all_to_all | solution.py:360
  623.1 5.0 all-to-all-start
  631.0 12.0 %spatial.4.refs_0_ = f32[16,2,512,512]{3,2,1,0:T(8,128)} custom-call(bf16[16,8,128,128]{3,2,1,0:T(8,128)(2,1)} %all-to-all-done.3.slab, bf16[1024,1024]{1,0:T(8,128)(2,1)S(1)} %copy-done.1, bf16[1024,1024]{1,0:T(8,128)(2,1)S(1)} %copy-done), custom_call_target="tpu_custom_call" | custom-call | flops 8589934592 | bytes 12582912 | tf_op jit(solution)/shard_map/spatial/pallas_call | solution.py:244
  643.0 12.0 %spatial.5.refs_0_ = f32[16,2,512,512]{3,2,1,0:T(8,128)} custom-call(bf16[16,8,128,128]{3,2,1,0:T(8,128)(2,1)} %all-to-all-done.2.slab, bf16[1024,1024]{1,0:T(8,128)(2,1)S(1)} %copy-done.1, bf16[1024,1024]{1,0:T(8,128)(2,1)S(1)} %copy-done, f32[16,2,512,512]{3,2,1,0:T(8,128)} %spatial.4.refs_0_), custom_call_target="tpu_custom_call", output_to_operand_aliasing={{}: (3, {})} | custom-call | flops 8589934592 | bytes 12582912 | tf_op jit(solution)/shard_map/spatial/pallas_call | solution.py:244
  655.1 12.0 %spatial.6.refs_0_ = f32[16,2,512,512]{3,2,1,0:T(8,128)} custom-call(bf16[16,8,128,128]{3,2,1,0:T(8,128)(2,1)} %all-to-all-done.1.slab, bf16[1024,1024]{1,0:T(8,128)(2,1)S(1)} %copy-done.1, bf16[1024,1024]{1,0:T(8,128)(2,1)S(1)} %copy-done, f32[16,2,512,512]{3,2,1,0:T(8,128)} %spatial.5.refs_0_), custom_call_target="tpu_custom_call", output_to_operand_aliasing={{}: (3, {})} | custom-call | flops 8589934592 | bytes 12582912 | tf_op jit(solution)/shard_map/spatial/pallas_call | solution.py:244
  667.1 53.5 %all-to-all-done.slab = bf16[16,8,128,128]{3,2,1,0:T(8,128)(2,1)} async-done(((bf16[16,8,128,128]{3,2,1,0:T(8,128)(2,1)}), bf16[16,8,128,128]{3,2,1,0:T(8,128)(2,1)}, u32[]{:S(2)}, u32[]{:S(2)}) %all-to-all-start) | async-done | bytes 4194336 | tf_op jit(solution)/shard_map/all_to_all | solution.py:360
  722.2 12.0 %spatial.7 = f32[16,2,512,512]{3,2,1,0:T(8,128)} custom-call(bf16[16,8,128,128]{3,2,1,0:T(8,128)(2,1)} %all-to-all-done.slab, bf16[1024,1024]{1,0:T(8,128)(2,1)S(1)} %copy-done.2, bf16[1024,1024]{1,0:T(8,128)(2,1)S(1)} %copy-done, f32[16,2,512,512]{3,2,1,0:T(8,128)} %spatial.6.refs_0_), custom_call_target="tpu_custom_call", output_to_operand_aliasing={{}: (3, {})} | custom-call | flops 8589934592 | bytes 12582912 | tf_op jit(solution)/shard_map/spatial/pallas_call | solution.py:244
  (59 shorter events, 34.6 us)
Async XLA Ops:
  9.7 125.2 %collective-permute-start.3 = (bf16[128,16,512]{0,1,2:T(8,128)(2,1)}, bf16[128,16,512]{0,1,2:T(8,128)(2,1)}, u32[]{:S(2)}, u32[]{:S(2)}) collective-permute-start(bf16[128,16,512]{0,1,2:T(8,128)(2,1)} %copy.33), channel_id=1, source_target_pairs={{1,0},{2,1},{3,2},{5,4},{6,5},{7,6},{9,8},{10,9},{11,10},{13,12},{... | collective-permute-start | bytes 6291464 | tf_op jit(solution)/shard_map/ppermute | solution.py:274
  17.6 117.4 %collective-permute-start.2 = (bf16[128,16,512]{0,1,2:T(8,128)(2,1)}, bf16[128,16,512]{0,1,2:T(8,128)(2,1)}, u32[]{:S(2)}, u32[]{:S(2)}) collective-permute-start(bf16[128,16,512]{0,1,2:T(8,128)(2,1)} %copy.32), channel_id=1, source_target_pairs={{0,1},{1,2},{2,3},{4,5},{5,6},{6,7},{8,9},{9,10},{10,11},{12,13},{... | collective-permute-start | bytes 6291464 | tf_op jit(solution)/shard_map/ppermute | solution.py:274
  42.3 78.9 %copy-start.12 = (s32[128,128]{1,0:T(8,128)S(1)}, s32[128,128]{1,0:T(8,128)}, u32[]{:S(2)}) copy-start(s32[128,128]{1,0:T(8,128)} %param.12) | copy-start | bytes 196612
  42.3 78.9 %copy-start.10 = (f32[512,512]{1,0:T(8,128)S(1)}, f32[512,512]{1,0:T(8,128)}, u32[]{:S(2)}) copy-start(f32[512,512]{1,0:T(8,128)} %constant.72.clone) | copy-start | bytes 3145732
  42.3 78.9 %copy-start.11 = (f32[16,512]{1,0:T(8,128)S(1)}, f32[16,512]{1,0:T(8,128)}, u32[]{:S(2)}) copy-start(f32[16,512]{1,0:T(8,128)} %param.13) | copy-start | bytes 98308
  47.5 92.4 %collective-permute-start = (bf16[16,128,512]{1,0,2:T(8,128)(2,1)}, bf16[16,128,512]{1,0,2:T(8,128)(2,1)}, u32[]{:S(2)}, u32[]{:S(2)}) collective-permute-start(bf16[16,128,512]{1,0,2:T(8,128)(2,1)} %get-tuple-element.18), channel_id=1, source_target_pairs={{0,4},{4,8},{8,12},{1,5},{5,9},{9,13},{2,6},{6,10},{10,14},{3,7},{... | collective-permute-start | bytes 6291464 | tf_op jit(solution)/shard_map/ppermute | solution.py:274
  50.7 89.2 %collective-permute-start.1 = (bf16[16,128,512]{1,0,2:T(8,128)(2,1)}, bf16[16,128,512]{1,0,2:T(8,128)(2,1)}, u32[]{:S(2)}, u32[]{:S(2)}) collective-permute-start(bf16[16,128,512]{1,0,2:T(8,128)(2,1)} %get-tuple-element.19), channel_id=1, source_target_pairs={{4,0},{8,4},{12,8},{5,1},{9,5},{13,9},{6,2},{10,6},{14,10},{7,3},{... | collective-permute-start | bytes 6291464 | tf_op jit(solution)/shard_map/ppermute | solution.py:274
  55.3 44.8 %collective-permute-start.4 = (bf16[16,16,512]{2,1,0:T(8,128)(2,1)S(1)}, bf16[16,16,512]{2,1,0:T(8,128)(2,1)S(1)}, u32[]{:S(2)}, u32[]{:S(2)}) collective-permute-start(bf16[16,16,512]{2,1,0:T(8,128)(2,1)S(1)} %get-tuple-element.12), channel_id=1, source_target_pairs={{0,5},{1,6},{2,7},{4,9},{5,10},{6,11},{8,13},{9,14},{10,15},{16,21... | collective-permute-start | bytes 786440 | tf_op jit(solution)/shard_map/ppermute | solution.py:274
  100.1 10.2 %collective-permute-start.5 = (bf16[16,16,512]{2,1,0:T(8,128)(2,1)S(1)}, bf16[16,16,512]{2,1,0:T(8,128)(2,1)S(1)}, u32[]{:S(2)}, u32[]{:S(2)}) collective-permute-start(bf16[16,16,512]{2,1,0:T(8,128)(2,1)S(1)} %get-tuple-element.13), channel_id=1, source_target_pairs={{1,4},{2,5},{3,6},{5,8},{6,9},{7,10},{9,12},{10,13},{11,14},{17,20... | collective-permute-start | bytes 786440 | tf_op jit(solution)/shard_map/ppermute | solution.py:274
  110.3 9.5 %collective-permute-start.7 = (bf16[16,16,512]{2,1,0:T(8,128)(2,1)S(1)}, bf16[16,16,512]{2,1,0:T(8,128)(2,1)S(1)}, u32[]{:S(2)}, u32[]{:S(2)}) collective-permute-start(bf16[16,16,512]{2,1,0:T(8,128)(2,1)S(1)} %get-tuple-element.14), channel_id=1, source_target_pairs={{5,0},{6,1},{7,2},{9,4},{10,5},{11,6},{13,8},{14,9},{15,10},{21,16... | collective-permute-start | bytes 786440 | tf_op jit(solution)/shard_map/ppermute | solution.py:274
  119.9 8.1 %collective-permute-start.6 = (bf16[16,16,512]{2,1,0:T(8,128)(2,1)S(1)}, bf16[16,16,512]{2,1,0:T(8,128)(2,1)S(1)}, u32[]{:S(2)}, u32[]{:S(2)}) collective-permute-start(bf16[16,16,512]{2,1,0:T(8,128)(2,1)S(1)} %get-tuple-element.15), channel_id=1, source_target_pairs={{4,1},{5,2},{6,3},{8,5},{9,6},{10,7},{12,9},{13,10},{14,11},{20,17... | collective-permute-start | bytes 786440 | tf_op jit(solution)/shard_map/ppermute | solution.py:274
  139.9 5.0 copy-start.7
  139.9 5.0 copy-start.8
  139.9 5.0 copy-start.9
  318.6 2.0 copy-start.6
  320.6 107.8 %all-to-all-start.1 = ((bf16[16,8,128,128]{3,2,1,0:T(8,128)(2,1)}), bf16[16,8,128,128]{3,2,1,0:T(8,128)(2,1)}, u32[]{:S(2)}, u32[]{:S(2)}) async-start(bf16[16,8,128,128]{3,2,1,0:T(8,128)(2,1)} %bitcast.30), calls=%async_computation.1 | async-start | bytes 8388608 | tf_op jit(solution)/shard_map/all_to_all | solution.py:360
  351.3 1.9 copy-start.5
  428.4 97.4 %all-to-all-start.2 = ((bf16[16,8,128,128]{3,2,1,0:T(8,128)(2,1)}), bf16[16,8,128,128]{3,2,1,0:T(8,128)(2,1)}, u32[]{:S(2)}, u32[]{:S(2)}) async-start(bf16[16,8,128,128]{3,2,1,0:T(8,128)(2,1)} %bitcast.29), calls=%async_computation.2 | async-start | bytes 8388608 | tf_op jit(solution)/shard_map/all_to_all | solution.py:360
  448.7 2.0 copy-start.4
  525.8 97.4 %all-to-all-start.3 = ((bf16[16,8,128,128]{3,2,1,0:T(8,128)(2,1)}), bf16[16,8,128,128]{3,2,1,0:T(8,128)(2,1)}, u32[]{:S(2)}, u32[]{:S(2)}) async-start(bf16[16,8,128,128]{3,2,1,0:T(8,128)(2,1)} %bitcast.28), calls=%async_computation.3 | async-start | bytes 8388608 | tf_op jit(solution)/shard_map/all_to_all | solution.py:360
  546.1 2.0 copy-start.3
  623.1 6.3 copy-start
  623.1 97.5 %all-to-all-start = ((bf16[16,8,128,128]{3,2,1,0:T(8,128)(2,1)}), bf16[16,8,128,128]{3,2,1,0:T(8,128)(2,1)}, u32[]{:S(2)}, u32[]{:S(2)}) async-start(bf16[16,8,128,128]{3,2,1,0:T(8,128)(2,1)} %bitcast.27), calls=%async_computation | async-start | bytes 8388608 | tf_op jit(solution)/shard_map/all_to_all | solution.py:360
  629.4 1.6 copy-start.1
  720.6 1.6 copy-start.2

commit v2 on v1

--- a/solution.py
+++ b/solution.py
@@ -6,12 +6,15 @@
 import numpy as np
 from jax import lax
 from jax.experimental import pallas as pl
+from jax.experimental.layout import Layout, with_layout_constraint
 from jax.experimental.pallas import tpu as pltpu
 from jax.sharding import PartitionSpec as P
 
 HALF = 16
 VMEM_LIMIT = 48 * 1024 * 1024
-CHUNKS = 4
+PACK = 4
+FIRST, LAST = slice(0, HALF), slice(-HALF, None)
+END_DELAYS = 2
 
 highest = lax.Precision.HIGHEST
 
@@ -105,54 +108,60 @@
     return taps[:, np.minimum(distance, HALF + 1)].astype(jnp.bfloat16)
 
 
-def smooth_kernel(row_pieces, side_pieces, widths, mask, row_band, side_band, col_band, *refs):
-    rows, sides = refs[:row_pieces], refs[row_pieces : row_pieces + side_pieces]
-    high, low, power, staged = refs[row_pieces + side_pieces :]
-    block = rows[0].shape[0]
+def smooth_kernel(widths, mask, row_band, col_band, centre, top, bottom, left, right, corners, *outs):
+    high, low, power, staged = outs
+    block = centre.shape[0]
     outputs, columns = mask.shape
     first = pl.program_id(0) * block
     kept = mask[...]
-    for j in range(block):
-        width = widths[first + j] - 1
-        data = jnp.concatenate([piece[j] for piece in rows], axis=0)
-        side = jnp.concatenate([piece[j] for piece in sides], axis=1)
-        centre = jnp.dot(row_band[width], data, preferred_element_type=jnp.float32)
-        edge = jnp.dot(side, side_band[width], preferred_element_type=jnp.float32)
-        smoothed_rows = jnp.concatenate(
-            [centre.astype(jnp.bfloat16), edge.T.astype(jnp.bfloat16)], axis=1
-        )
-        smoothed = jnp.dot(smoothed_rows, col_band[width], preferred_element_type=jnp.float32)
-        staged[pl.ds(j, outputs, stride=block), :] = smoothed * kept
-
-    group = 8
-
-    def split(step, total):
-        start = pl.multiple_of(step * group, group)
-        value = staged[pl.ds(pl.multiple_of(start * block, group * block), group * block), :]
+    for group in range(0, block, PACK):
+        members = range(group, group + PACK)
+        chosen = pl.ds(group, PACK)
+        flank = [left[chosen], right[chosen]]
+        flank = jnp.concatenate([x.reshape(PACK * HALF, outputs) for x in flank], axis=0)
+        corner = [corners[chosen, :HALF], corners[chosen, HALF:]]
+        corner = jnp.concatenate([x.reshape(PACK * HALF, 2 * HALF) for x in corner], axis=0)
+        flank = jnp.concatenate([flank, corner], axis=1).T
+        half_smoothed = []
+        for j in members:
+            data = jnp.concatenate([centre[j], top[j], bottom[j]], axis=0)
+            data = jnp.concatenate([data, flank], axis=1)
+            band = row_band[widths[first + j] - 1]
+            half_smoothed.append(
+                jnp.dot(band, data, preferred_element_type=jnp.float32).astype(jnp.bfloat16)
+            )
+        for j, rows in zip(members, half_smoothed):
+            band = col_band[(widths[first + j] - 1) * PACK + j % PACK]
+            smoothed = jnp.dot(rows, band, preferred_element_type=jnp.float32)
+            staged[pl.ds(j, outputs, stride=block), :] = smoothed * kept
+
+    step = 8
+    total = jnp.zeros((block, columns), jnp.float32)
+    for start in range(0, outputs, step):
+        value = staged[pl.ds(start * block, step * block), :]
         rounded = value.astype(jnp.bfloat16)
         rest = (value - rounded.astype(jnp.float32)).astype(jnp.bfloat16)
-        high[pl.ds(start, group)] = rounded.reshape(group, block, columns)
-        low[pl.ds(start, group)] = rest.reshape(group, block, columns)
-        return total + jnp.sum((value * value).reshape(group, block, columns), axis=0)
-
-    power[...] = lax.fori_loop(
-        0, outputs // group, split, jnp.zeros((block, columns), jnp.float32)
-    )
-
-
-def smooth(half_widths, mask, rows, sides, tables, block=16):
-    channels, _, columns = rows[0].shape
+        high[pl.ds(start, step)] = rounded.reshape(step, block, columns)
+        low[pl.ds(start, step)] = rest.reshape(step, block, columns)
+        total = total + jnp.sum((value * value).reshape(step, block, columns), axis=0)
+    power[...] = total
+
+
+def smooth(half_widths, mask, pieces, row_band, col_band, block=32):
+    centre = pieces[0]
+    channels, _, columns = centre.shape
     outputs = mask.shape[0]
     whole = lambda shape: pl.BlockSpec(shape, lambda i: (0,) * len(shape))
     piece = lambda x: pl.BlockSpec((block,) + x.shape[1:], lambda i: (i, 0, 0))
     split_spec = pl.BlockSpec((outputs, block, columns), lambda i: (0, i, 0))
     split_shape = jax.ShapeDtypeStruct((outputs, channels, columns), jnp.bfloat16)
+    tables = [mask, row_band, col_band]
     return pl.pallas_call(
-        functools.partial(smooth_kernel, len(rows), len(sides)),
+        smooth_kernel,
         grid=(channels // block,),
-        in_specs=[pl.BlockSpec(memory_space=pltpu.SMEM), whole(mask.shape)]
+        in_specs=[pl.BlockSpec(memory_space=pltpu.SMEM)]
         + [whole(t.shape) for t in tables]
-        + [piece(x) for x in rows + sides],
+        + [piece(x) for x in pieces],
         out_specs=[split_spec, split_spec, pl.BlockSpec((block, columns), lambda i: (i, 0))],
         out_shape=[
             split_shape,
@@ -162,10 +171,10 @@
         scratch_shapes=[pltpu.VMEM((outputs * block, columns), jnp.float32)],
         compiler_params=pltpu.CompilerParams(vmem_limit_bytes=VMEM_LIMIT),
         cost_estimate=pl.CostEstimate(
-            flops=4 * channels * outputs * columns * 160, bytes_accessed=80_000_000, transcendentals=0
+            flops=4 * channels * outputs * columns * 256, bytes_accessed=80_000_000, transcendentals=0
         ),
         name="smooth",
-    )(half_widths, mask, *tables, *rows, *sides)
+    )(half_widths, *tables, *pieces)
 
 
 def delay_kernel(modes, high, low, out, staged):
@@ -261,22 +270,23 @@
     )(*operands)
 
 
-def shifted(x, steps):
-    axes = tuple(axis for axis, _ in steps)
-    sizes = [lax.axis_size(axis) for axis in axes]
-    pairs = []
-    for place in np.ndindex(*sizes):
-        target = [p + s for p, (_, s) in zip(place, steps)]
-        if all(0 <= t < n for t, n in zip(target, sizes)):
-            pairs.append(
-                (int(np.ravel_multi_index(place, sizes)), int(np.ravel_multi_index(target, sizes)))
-            )
-    return lax.ppermute(x, axes if len(axes) > 1 else axes[0], pairs)
+def shifted(x, axis, step):
+    size = lax.axis_size(axis)
+    pairs = [(i, i + step) for i in range(size) if 0 <= i + step < size]
+    order = Layout(major_to_minor=tuple(range(x.ndim)))
+    x = with_layout_constraint(x, order)
+    return with_layout_constraint(lax.ppermute(x, axis, pairs), order)
 
 
 def split_high_low(x):
-    rounded = x.astype(jnp.bfloat16)
-    return rounded, (x - rounded.astype(jnp.float32)).astype(jnp.bfloat16)
+    rounded = lax.reduce_precision(x, exponent_bits=8, mantissa_bits=7)
+    return rounded.astype(jnp.bfloat16), (x - rounded).astype(jnp.bfloat16)
+
+
+def chunk_sizes(per_device):
+    if per_device <= 4 * END_DELAYS:
+        return [per_device]
+    return [END_DELAYS, per_device - 2 * END_DELAYS, END_DELAYS]
 
 
 def tiled_body(sky_cube, half_widths, pixel_mask, foreground_modes):
@@ -286,50 +296,43 @@
     per_device = channels // 2 // peers
     sides, columns = row_count * tile_rows, col_count * tile_cols
 
-    top = shifted(sky_cube[-HALF:], (("row", 1),))
-    bottom = shifted(sky_cube[:HALF], (("row", -1),))
-    left = shifted(sky_cube[:, -HALF:], (("col", 1),))
-    right = shifted(sky_cube[:, :HALF], (("col", -1),))
-    corners = [
-        [
-            shifted(
-                sky_cube[(slice(-HALF, None) if v > 0 else slice(0, HALF))][
-                    :, (slice(-HALF, None) if h > 0 else slice(0, HALF))
-                ],
-                (("row", v), ("col", h)),
-            )
-            for h in (1, -1)
-        ]
-        for v in (1, -1)
-    ]
-    centre_t = jnp.transpose(sky_cube, (2, 0, 1))
-    caps_t = jnp.transpose(jnp.concatenate([top, bottom], axis=0), (2, 0, 1))
-    flank_t = jnp.transpose(jnp.concatenate([left, right], axis=1), (2, 1, 0))
-    corner = jnp.concatenate([jnp.concatenate(line, axis=1) for line in corners], axis=0)
-    corner_t = jnp.transpose(corner, (2, 1, 0))
+    top = shifted(sky_cube[LAST], "row", 1)
+    bottom = shifted(sky_cube[FIRST], "row", -1)
+    left = shifted(sky_cube[:, LAST], "col", 1)
+    right = shifted(sky_cube[:, FIRST], "col", -1)
+    centre = jnp.transpose(sky_cube, (2, 0, 1))
+    left, right, centre = lax.optimization_barrier((left, right, centre))
+    ends = [jnp.concatenate([left[rows], right[rows]], axis=1) for rows in (LAST, FIRST)]
+    corner = jnp.concatenate([shifted(ends[0], "row", 1), shifted(ends[1], "row", -1)], axis=0)
+    pieces = [centre] + [jnp.transpose(x, (2, 0, 1)) for x in (top, bottom)]
+    pieces += [jnp.transpose(x, (2, 1, 0)) for x in (left, right, corner)]
 
     def places(length):
         return list(range(length)) + list(range(-HALF, 0)) + list(range(length, length + HALF))
 
-    out_rows = list(range(tile_rows))
-    row_band = band_table(out_rows, places(tile_rows))
-    side_band = np.swapaxes(row_band, 1, 2)
-    col_band = np.swapaxes(band_table(list(range(tile_cols)), places(tile_cols)), 1, 2)
+    row_band = band_table(list(range(tile_rows)), places(tile_rows))
+    narrow = np.swapaxes(band_table(list(range(tile_cols)), places(tile_cols)), 1, 2)
+    col_band = np.zeros((HALF, PACK, tile_cols + PACK * 2 * HALF, tile_cols), narrow.dtype)
+    col_band[:, :, :tile_cols] = narrow[:, None, :tile_cols]
+    for member in range(PACK):
+        for part in range(2):
+            to = tile_cols + (part * PACK + member) * HALF
+            begin = tile_cols + part * HALF
+            col_band[:, member, to : to + HALF] = narrow[:, begin : begin + HALF]
+    col_band = col_band.reshape((HALF * PACK,) + col_band.shape[2:])
     high, low, power = smooth(
-        half_widths,
-        pixel_mask.astype(jnp.float32),
-        [centre_t, caps_t],
-        [flank_t, corner_t],
-        [row_band, side_band, col_band],
-    )
-
-    chunks = math.gcd(CHUNKS, per_device)
-    sizes = [per_device // chunks] * chunks
+        half_widths, pixel_mask.astype(jnp.float32), pieces, row_band, col_band
+    )
+
+    sizes = chunk_sizes(per_device)
     delay_table = delay_rows(channels, peers, sizes)
     mode_delays = jnp.dot(
         delay_table, foreground_modes.T, precision=highest, preferred_element_type=jnp.float32
     )
-    power_sum = lax.psum(jnp.sum(power, axis=1), ("row", "col"))
+    tile_power = jnp.broadcast_to(jnp.sum(power, axis=1)[None], (peers, channels))
+    power_sum = jnp.sum(
+        lax.all_to_all(tile_power, ("row", "col"), split_axis=0, concat_axis=0, tiled=True), axis=0
+    )
     weights = 1.0 / (power_sum / (sides * columns) + 1e-05)
     channel_weights = weights / jnp.mean(weights)
     weighted_modes = foreground_modes * weights[None, :]
@@ -350,18 +353,33 @@
 
     spectrum = None
     start = 0
-    for size in sizes:
+    for index, size in enumerate(sizes):
         begin, count = 2 * start * peers, 2 * size * peers
         both = jnp.concatenate(
             [matrix_high[begin : begin + count], matrix_low[begin : begin + count]], axis=0
         )
         delays = delay_chunk(both, high, low)
         delays = delays.reshape(peers, 2 * size, tile_rows, tile_cols)
+        if index == 2:
+            delays, spectrum = lax.optimization_barrier((delays, spectrum))
         received = lax.all_to_all(delays, ("row", "col"), split_axis=0, concat_axis=0, tiled=True)
+        if index == 1:
+            held = received
+            spectrum = spatial_chunk(
+                first_received, col_table, row_table, (per_device, 2, sides, columns), 0, None
+            )
+        elif index == 2:
+            spectrum = spatial_chunk(
+                held, col_table, row_table, spectrum.shape, sizes[0], spectrum
+            )
+            spectrum = spatial_chunk(received, col_table, row_table, spectrum.shape, start, spectrum)
+        else:
+            first_received = received
+        start += size
+    if len(sizes) == 1:
         spectrum = spatial_chunk(
-            received, col_table, row_table, (per_device, 2, sides, columns), start, spectrum
+            first_received, col_table, row_table, (per_device, 2, sides, columns), 0, None
         )
-        start += size
     return (spectrum, channel_weights)
 
 

time: 736 us -> 577 us (0.78)
  Pallas kernels: 237 us -> 163 us
  waiting for transfers between devices: 339 us -> 291 us
  blocking collectives: 24.3 us -> 0 us
  starting transfers between devices: 53.4 us -> 41.9 us
  other arithmetic: 15.5 us -> 7.83 us
    pallas_call x1, Pallas kernels: 127 us -> 57.8 us  [smooth(): pl.pallas_call(smooth_kernel, grid=(channels // block,), in_specs=[pl.Blo...]
    ppermute x8 -> x6, waiting for transfers between devices: 60.1 us -> 7.66 us  [shifted(): return with_layout_constraint(lax.ppermute(x, axis, pairs), order)]
    psum x1 -> x0, blocking collectives: 24.3 us -> none  [tiled_body(): power_sum = lax.psum(jnp.sum(power, axis=1), ('row', 'col'))]
    all_to_all x4 -> x3, starting transfers between devices: 30.2 us -> 15.9 us  [tiled_body(): lax.all_to_all(delays, ('row', 'col'), split_axis=0, concat_axis=0, tiled...]
    unnamed x29 -> x25, local copies, waits for them, and re-layouts: 43.6 us -> 29.6 us
    all_to_all x0 -> x1, starting transfers between devices: none -> 10.3 us  [tiled_body(): lax.all_to_all(tile_power, ('row', 'col'), split_axis=0, concat_axis=0, t...]
    transpose x2 -> x0, other arithmetic: 9.93 us -> none  [the longest x1 5 us: tiled_body(): caps_t = jnp.transpose(jnp.concatenate([top, bottom], axis=0), (2, 0, 1))]
    optimization_barrier x0 -> x2, local copies, waits for them, and re-layouts: none -> 9.05 us  [tiled_body(): left, right, centre = lax.optimization_barrier((left, right, centre))]
  transfers between devices with their start and end apart: 12 -> 10, of which waited for: 8 -> 7; matrix products, arithmetic and copies ran while one was open for 6% -> 9% of each run, Pallas kernels for 11% -> 14%
where the time goes in v2:
time: 577 us; the launch traced here: 576 us
  waiting for transfers between devices  291 us (50%)
  Pallas kernels  163 us (28%)
  local copies, waits for them, and re-layouts  66.6 us (12%)
  starting transfers between devices  41.9 us (7%)
  other arithmetic  7.83 us (1%)
    all_to_all x3, waiting for transfers between devices, tiled_body(): lax.all_to_all(delays, ('row', 'col'), split_axis=0, concat_axis=0, tiled...  281 us
    pallas_call x1, Pallas kernels, smooth(): pl.pallas_call(smooth_kernel, grid=(channels // block,), in_specs=[pl.Blo...  57.8 us
    pallas_call x3, Pallas kernels, delay_chunk(): pl.pallas_call(delay_kernel, grid=(tile_rows // block,), in_specs=[pl.Blo...  57.7 us
    pallas_call x3, Pallas kernels, spatial_chunk(): pl.pallas_call(functools.partial(spatial_kernel, side // tile_rows, colum...  47.4 us
    unnamed x25, local copies, waits for them, and re-layouts  29.6 us
    all_to_all x3, starting transfers between devices, tiled_body(): lax.all_to_all(delays, ('row', 'col'), split_axis=0, concat_axis=0, tiled...  15.9 us
    ppermute x6, starting transfers between devices, shifted(): return with_layout_constraint(lax.ppermute(x, axis, pairs), order)  15.8 us
  transfers between devices with their start and end apart: 10, of which 7 were waited for; matrix products, arithmetic and copies ran while one was open for 9% of the time, Pallas kernels for 14%

profile of v2, /device:TPU:11, one launch (start us, length us, event | category | flops | bytes accessed | tf_op | source)
XLA Modules:
  0.0 575.8 jit_solution(1872603009150671437)
XLA Ops:
  0.6 4.8 fusion.16
  5.4 2.7 collective-permute-start.1
  9.4 4.6 fusion.15
  14.0 2.1 collective-permute-start.3
  16.1 3.2 collective-permute-start.2
  19.3 23.5 %copy.35 = bf16[128,128,512]{1,0,2:T(8,128)(2,1)} copy(bf16[128,128,512]{2,1,0:T(8,128)(2,1)} %param.9) | data formatting | bytes 33554432 | tf_op args[0]
  44.0 3.4 collective-permute-start.5
  47.4 3.1 collective-permute-start.4
  50.6 4.0 copy.39
  54.5 5.1 copy.38
  59.6 2.6 collective-permute-done.3
  62.2 3.4 copy.37
  65.7 4.5 copy.36
  70.2 3.2 collective-permute-done.5
  75.3 2.3 pad_maximum_fusion
  77.5 8.7 %copy.40 = bf16[32,32,512]{0,1,2:T(8,128)(2,1)} copy(bf16[32,32,512]{2,1,0:T(8,128)(2,1)} %pad_maximum_fusion) | data formatting | bytes 2097152 | tf_op jit(solution)/shard_map/concatenate | solution.py:306
  87.8 57.8 %smooth.1 = (bf16[128,512,128]{2,1,0:T(8,128)(2,1)}, bf16[128,512,128]{2,1,0:T(8,128)(2,1)}, f32[512,128]{1,0:T(8,128)S(1)}) custom-call(s32[512]{0:T(512)S(1)} %copy-done.8, f32[128,128]{1,0:T(8,128)S(1)} %convert_element_type.9.mask, bf16[16,128,160]{2,1,0:T(8,128)(2,1)S(1)} %copy-done.7, bf16[64,256,128]{2,1,0:T(8,128)(2,1)} %constant.71.clone.col_band, ...), custom_call_target="tpu_custom_call" | custom-call | flops 8589934592 | bytes 80000000 | tf_op jit(solution)/shard_map/smooth/pallas_call | solution.py:159
  146.4 10.3 %all-to-all-start = ((f32[16,1,512]{2,1,0:T(1,128)}), f32[16,1,512]{2,1,0:T(1,128)S(1)}, u32[]{:S(2)}, u32[]{:S(2)}) async-start(f32[16,1,512]{2,1,0:T(1,128)} %broadcast_in_dim.3), calls=%async_computation | async-start | bytes 65536 | tf_op jit(solution)/shard_map/all_to_all | solution.py:334
  156.7 2.2 fusion.21
  158.9 1.9 all-to-all-done
  167.3 14.4 %delays.4 = bf16[64,128,128]{2,1,0:T(8,128)(2,1)S(1)} custom-call(bf16[128,512]{1,0:T(8,128)(2,1)S(1)} %pad_maximum_fusion.5.modes, bf16[128,512,128]{2,1,0:T(8,128)(2,1)} %get-tuple-element.14.high, bf16[128,512,128]{2,1,0:T(8,128)(2,1)} %get-tuple-element.15.low), custom_call_target="tpu_custom_call" | custom-call | flops 3221225472 | bytes 40000000 | tf_op jit(solution)/shard_map/delays/pallas_call | solution.py:199
  183.1 6.1 %all-to-all-start.1 = ((bf16[16,4,128,128]{3,2,1,0:T(8,128)(2,1)}), bf16[16,4,128,128]{3,2,1,0:T(8,128)(2,1)S(1)}, u32[]{:S(2)}, u32[]{:S(2)}) async-start(bf16[16,4,128,128]{3,2,1,0:T(8,128)(2,1)} %bitcast.29), calls=%async_computation.1 | async-start | bytes 4194304 | tf_op jit(solution)/shard_map/all_to_all | solution.py:365
  189.3 28.7 %delays.5 = bf16[384,128,128]{2,1,0:T(8,128)(2,1)} custom-call(bf16[768,512]{1,0:T(8,128)(2,1)S(1)} %pad_maximum_fusion.1.modes, bf16[128,512,128]{2,1,0:T(8,128)(2,1)} %get-tuple-element.14.high, bf16[128,512,128]{2,1,0:T(8,128)(2,1)} %get-tuple-element.15.low), custom_call_target="tpu_custom_call" | custom-call | flops 19327352832 | bytes 40000000 | tf_op jit(solution)/shard_map/delays/pallas_call | solution.py:199
  218.1 18.6 %all-to-all-done.1.slab = bf16[16,4,128,128]{3,2,1,0:T(8,128)(2,1)S(1)} async-done(((bf16[16,4,128,128]{3,2,1,0:T(8,128)(2,1)}), bf16[16,4,128,128]{3,2,1,0:T(8,128)(2,1)S(1)}, u32[]{:S(2)}, u32[]{:S(2)}) %all-to-all-start.1) | async-done | bytes 2097184 | tf_op jit(solution)/shard_map/all_to_all | solution.py:365
  236.6 4.9 all-to-all-start.3
  241.6 14.6 %delays.3 = bf16[64,128,128]{2,1,0:T(8,128)(2,1)S(1)} custom-call(bf16[128,512]{1,0:T(8,128)(2,1)S(1)} %pad_maximum_fusion.4.modes, bf16[128,512,128]{2,1,0:T(8,128)(2,1)} %get-tuple-element.14.high, bf16[128,512,128]{2,1,0:T(8,128)(2,1)} %get-tuple-element.15.low), custom_call_target="tpu_custom_call" | custom-call | flops 3221225472 | bytes 40000000 | tf_op jit(solution)/shard_map/delays/pallas_call | solution.py:199
  256.2 8.4 %spatial.3.refs_0_ = f32[16,2,512,512]{3,2,1,0:T(8,128)} custom-call(bf16[16,4,128,128]{3,2,1,0:T(8,128)(2,1)S(1)} %all-to-all-done.1.slab, bf16[1024,1024]{1,0:T(8,128)(2,1)S(1)} %copy-done.1, bf16[1024,1024]{1,0:T(8,128)(2,1)} %constant.74.clone.row_table), custom_call_target="tpu_custom_call" | custom-call | flops 4294967296 | bytes 6291456 | tf_op jit(solution)/shard_map/spatial/pallas_call | solution.py:253
  264.6 249.2 %all-to-all-done.3.slab = bf16[16,24,128,128]{3,2,1,0:T(8,128)(2,1)} async-done(((bf16[16,24,128,128]{3,2,1,0:T(8,128)(2,1)}), bf16[16,24,128,128]{3,2,1,0:T(8,128)(2,1)}, u32[]{:S(2)}, u32[]{:S(2)}) %all-to-all-start.3) | async-done | bytes 12582944 | tf_op jit(solution)/shard_map/all_to_all | solution.py:365
  513.8 4.9 all-to-all-start.2
  521.5 31.1 %spatial.4.refs_0_ = f32[16,2,512,512]{3,2,1,0:T(8,128)} custom-call(bf16[16,24,128,128]{3,2,1,0:T(8,128)(2,1)} %all-to-all-done.3.slab, bf16[1024,1024]{1,0:T(8,128)(2,1)S(1)} %copy-done.2, bf16[1024,1024]{1,0:T(8,128)(2,1)S(1)} %copy-done, f32[16,2,512,512]{3,2,1,0:T(8,128)} %spatial.3.refs_0_), custom_call_target="tpu_custom_call", output_to_operand_aliasing={{}: (3, {})} | custom-call | flops 25769803776 | bytes 37748736 | tf_op jit(solution)/shard_map/spatial/pallas_call | solution.py:253
  552.6 13.6 %all-to-all-done.2.slab = bf16[16,4,128,128]{3,2,1,0:T(8,128)(2,1)} async-done(((bf16[16,4,128,128]{3,2,1,0:T(8,128)(2,1)}), bf16[16,4,128,128]{3,2,1,0:T(8,128)(2,1)}, u32[]{:S(2)}, u32[]{:S(2)}) %all-to-all-start.2) | async-done | bytes 2097184 | tf_op jit(solution)/shard_map/all_to_all | solution.py:365
  567.8 8.0 %spatial.5 = f32[16,2,512,512]{3,2,1,0:T(8,128)} custom-call(bf16[16,4,128,128]{3,2,1,0:T(8,128)(2,1)} %all-to-all-done.2.slab, bf16[1024,1024]{1,0:T(8,128)(2,1)S(1)} %copy-done.3, bf16[1024,1024]{1,0:T(8,128)(2,1)} %constant.74.clone.row_table, f32[16,2,512,512]{3,2,1,0:T(8,128)} %spatial.4.refs_0_), custom_call_target="tpu_custom_call", output_to_operand_aliasing={{}: (3, {})} | custom-call | flops 4294967296 | bytes 6291456 | tf_op jit(solution)/shard_map/spatial/pallas_call | solution.py:253
  (56 shorter events, 18.4 us)
Async XLA Ops:
  5.4 37.4 %collective-permute-start.1 = (bf16[128,16,512]{2,1,0:T(8,128)(2,1)}, bf16[128,16,512]{2,1,0:T(8,128)(2,1)S(1)}, u32[]{:S(2)}, u32[]{:S(2)}) collective-permute-start(bf16[128,16,512]{2,1,0:T(8,128)(2,1)} %get-tuple-element.22), channel_id=1, source_target_pairs={{1,0},{2,1},{3,2},{5,4},{6,5},{7,6},{9,8},{10,9},{11,10},{13,12},{... | collective-permute-start | bytes 6291464 | tf_op jit(solution)/shard_map/ppermute | solution.py:278
  8.1 34.7 %collective-permute-start = (bf16[128,16,512]{2,1,0:T(8,128)(2,1)}, bf16[128,16,512]{2,1,0:T(8,128)(2,1)}, u32[]{:S(2)}, u32[]{:S(2)}) collective-permute-start(bf16[128,16,512]{2,1,0:T(8,128)(2,1)} %get-tuple-element.23), channel_id=1, source_target_pairs={{0,1},{1,2},{2,3},{4,5},{5,6},{6,7},{8,9},{9,10},{10,11},{12,13},{... | collective-permute-start | bytes 6291464 | tf_op jit(solution)/shard_map/ppermute | solution.py:278
  14.0 48.2 %collective-permute-start.3 = (bf16[16,128,512]{2,1,0:T(8,128)(2,1)}, bf16[16,128,512]{2,1,0:T(8,128)(2,1)}, u32[]{:S(2)}, u32[]{:S(2)}) collective-permute-start(bf16[16,128,512]{2,1,0:T(8,128)(2,1)} %get-tuple-element.20), channel_id=1, source_target_pairs={{4,0},{8,4},{12,8},{5,1},{9,5},{13,9},{6,2},{10,6},{14,10},{7,3},{... | collective-permute-start | bytes 6291464 | tf_op jit(solution)/shard_map/ppermute | solution.py:278
  16.1 49.6 %collective-permute-start.2 = (bf16[16,128,512]{2,1,0:T(8,128)(2,1)}, bf16[16,128,512]{2,1,0:T(8,128)(2,1)}, u32[]{:S(2)}, u32[]{:S(2)}) collective-permute-start(bf16[16,128,512]{2,1,0:T(8,128)(2,1)} %get-tuple-element.21), channel_id=1, source_target_pairs={{0,4},{4,8},{8,12},{1,5},{5,9},{9,13},{2,6},{6,10},{10,14},{3,7},{... | collective-permute-start | bytes 6291464 | tf_op jit(solution)/shard_map/ppermute | solution.py:278
  42.8 7.7 %copy-start.11 = (s32[128,128]{1,0:T(8,128)S(1)}, s32[128,128]{1,0:T(8,128)}, u32[]{:S(2)}) copy-start(s32[128,128]{1,0:T(8,128)} %param.11) | copy-start | bytes 196612
  44.0 29.5 %collective-permute-start.5 = (bf16[16,32,512]{2,1,0:T(8,128)(2,1)S(1)}, bf16[16,32,512]{2,1,0:T(8,128)(2,1)}, u32[]{:S(2)}, u32[]{:S(2)}) collective-permute-start(bf16[16,32,512]{2,1,0:T(8,128)(2,1)S(1)} %pad_maximum_fusion.3), channel_id=1, source_target_pairs={{4,0},{8,4},{12,8},{5,1},{9,5},{13,9},{6,2},{10,6},{14,10},{7,3},{... | collective-permute-start | bytes 1572872 | tf_op jit(solution)/shard_map/ppermute | solution.py:278
  47.4 27.9 %collective-permute-start.4 = (bf16[16,32,512]{2,1,0:T(8,128)(2,1)S(1)}, bf16[16,32,512]{2,1,0:T(8,128)(2,1)}, u32[]{:S(2)}, u32[]{:S(2)}) collective-permute-start(bf16[16,32,512]{2,1,0:T(8,128)(2,1)S(1)} %pad_maximum_fusion.2), channel_id=1, source_target_pairs={{0,4},{4,8},{8,12},{1,5},{5,9},{9,13},{2,6},{6,10},{10,14},{3,7},{... | collective-permute-start | bytes 1572872 | tf_op jit(solution)/shard_map/ppermute | solution.py:278
  77.5 8.7 %copy-start.7 = (bf16[16,128,160]{2,1,0:T(8,128)(2,1)S(1)}, bf16[16,128,160]{2,1,0:T(8,128)(2,1)}, u32[]{:S(2)}) copy-start(bf16[16,128,160]{2,1,0:T(8,128)(2,1)} %constant.70.clone.row_band) | copy-start | bytes 1966084
  77.5 8.7 %copy-start.8 = (s32[512]{0:T(512)S(1)}, s32[512]{0:T(512)}, u32[]{:S(2)}) copy-start(s32[512]{0:T(512)} %widths.1) | copy-start | bytes 6148
  86.2 1.6 copy-start.4
  87.8 68.9 %copy-start.10 = (f32[16,512]{1,0:T(8,128)S(1)}, f32[16,512]{1,0:T(8,128)}, u32[]{:S(2)}) copy-start(f32[16,512]{1,0:T(8,128)} %param.12) | copy-start | bytes 98308
  145.6 20.5 %copy-start.9 = (f32[512,512]{1,0:T(8,128)S(1)}, f32[512,512]{1,0:T(8,128)}, u32[]{:S(2)}) copy-start(f32[512,512]{1,0:T(8,128)} %constant.72.clone) | copy-start | bytes 3145732
  146.4 14.4 %all-to-all-start = ((f32[16,1,512]{2,1,0:T(1,128)}), f32[16,1,512]{2,1,0:T(1,128)S(1)}, u32[]{:S(2)}, u32[]{:S(2)}) async-start(f32[16,1,512]{2,1,0:T(1,128)} %broadcast_in_dim.3), calls=%async_computation | async-start | bytes 65536 | tf_op jit(solution)/shard_map/all_to_all | solution.py:334
  181.8 1.3 copy-start.6
  183.1 53.6 %all-to-all-start.1 = ((bf16[16,4,128,128]{3,2,1,0:T(8,128)(2,1)}), bf16[16,4,128,128]{3,2,1,0:T(8,128)(2,1)S(1)}, u32[]{:S(2)}, u32[]{:S(2)}) async-start(bf16[16,4,128,128]{3,2,1,0:T(8,128)(2,1)} %bitcast.29), calls=%async_computation.1 | async-start | bytes 4194304 | tf_op jit(solution)/shard_map/all_to_all | solution.py:365
  236.6 277.1 %all-to-all-start.3 = ((bf16[16,24,128,128]{3,2,1,0:T(8,128)(2,1)}), bf16[16,24,128,128]{3,2,1,0:T(8,128)(2,1)}, u32[]{:S(2)}, u32[]{:S(2)}) async-start(bf16[16,24,128,128]{3,2,1,0:T(8,128)(2,1)} %bitcast.32), calls=%async_computation.3 | async-start | bytes 25165824 | tf_op jit(solution)/shard_map/all_to_all | solution.py:365
  241.5 14.6 %copy-start.1 = (bf16[1024,1024]{1,0:T(8,128)(2,1)S(1)}, bf16[1024,1024]{1,0:T(8,128)(2,1)}, u32[]{:S(2)}) copy-start(bf16[1024,1024]{1,0:T(8,128)(2,1)} %constant.73.clone.col_table) | copy-start | bytes 6291460
  256.1 8.4 %copy-start.5 = (bf16[64,128,128]{2,1,0:T(8,128)(2,1)}, bf16[64,128,128]{2,1,0:T(8,128)(2,1)S(1)}, u32[]{:S(2)}) copy-start(bf16[64,128,128]{2,1,0:T(8,128)(2,1)S(1)} %delays.3) | copy-start | bytes 6291460
  264.6 255.4 %copy-start = (bf16[1024,1024]{1,0:T(8,128)(2,1)S(1)}, bf16[1024,1024]{1,0:T(8,128)(2,1)}, u32[]{:S(2)}) copy-start(bf16[1024,1024]{1,0:T(8,128)(2,1)} %constant.74.clone.row_table) | copy-start | bytes 6291460
  513.8 52.4 %all-to-all-start.2 = ((bf16[16,4,128,128]{3,2,1,0:T(8,128)(2,1)}), bf16[16,4,128,128]{3,2,1,0:T(8,128)(2,1)}, u32[]{:S(2)}, u32[]{:S(2)}) async-start(bf16[16,4,128,128]{3,2,1,0:T(8,128)(2,1)} %bitcast.28), calls=%async_computation.2 | async-start | bytes 4194304 | tf_op jit(solution)/shard_map/all_to_all | solution.py:365
  519.9 1.6 copy-start.2
  566.2 1.6 copy-start.3

commit v3 on v2

--- a/solution.py
+++ b/solution.py
@@ -13,6 +13,8 @@
 HALF = 16
 VMEM_LIMIT = 48 * 1024 * 1024
 PACK = 4
+TURN = 8
+HEAD_ROWS = 16
 FIRST, LAST = slice(0, HALF), slice(-HALF, None)
 END_DELAYS = 2
 
@@ -108,23 +110,24 @@
     return taps[:, np.minimum(distance, HALF + 1)].astype(jnp.bfloat16)
 
 
-def smooth_kernel(widths, mask, row_band, col_band, centre, top, bottom, left, right, corners, *outs):
+def smooth_kernel(widths, mask, row_band, col_band, centre, top, bottom, left, right, *outs):
     high, low, power, staged = outs
     block = centre.shape[0]
     outputs, columns = mask.shape
     first = pl.program_id(0) * block
     kept = mask[...]
+    done = []
     for group in range(0, block, PACK):
         members = range(group, group + PACK)
         chosen = pl.ds(group, PACK)
-        flank = [left[chosen], right[chosen]]
-        flank = jnp.concatenate([x.reshape(PACK * HALF, outputs) for x in flank], axis=0)
-        corner = [corners[chosen, :HALF], corners[chosen, HALF:]]
-        corner = jnp.concatenate([x.reshape(PACK * HALF, 2 * HALF) for x in corner], axis=0)
-        flank = jnp.concatenate([flank, corner], axis=1).T
+        flank = jnp.concatenate([left[chosen], right[chosen]], axis=1)
+        flank = flank.reshape(PACK * 2 * HALF, outputs).T
+        caps = [jnp.concatenate([top[j], bottom[j]], axis=0) for j in members]
+        corner = jnp.concatenate([x[:, columns:] for x in caps], axis=1)
+        flank = jnp.concatenate([flank, corner], axis=0)
         half_smoothed = []
-        for j in members:
-            data = jnp.concatenate([centre[j], top[j], bottom[j]], axis=0)
+        for j, cap in zip(members, caps):
+            data = jnp.concatenate([centre[j], cap[:, :columns]], axis=0)
             data = jnp.concatenate([data, flank], axis=1)
             band = row_band[widths[first + j] - 1]
             half_smoothed.append(
@@ -133,17 +136,20 @@
         for j, rows in zip(members, half_smoothed):
             band = col_band[(widths[first + j] - 1) * PACK + j % PACK]
             smoothed = jnp.dot(rows, band, preferred_element_type=jnp.float32)
-            staged[pl.ds(j, outputs, stride=block), :] = smoothed * kept
+            done.append(smoothed * kept)
+        if len(done) == TURN:
+            begin = group + PACK - TURN
+            staged[:, pl.ds(begin, TURN), :] = jnp.swapaxes(jnp.stack(done), 0, 1)
+            done = []
 
     step = 8
     total = jnp.zeros((block, columns), jnp.float32)
     for start in range(0, outputs, step):
-        value = staged[pl.ds(start * block, step * block), :]
+        value = staged[pl.ds(start, step)]
         rounded = value.astype(jnp.bfloat16)
-        rest = (value - rounded.astype(jnp.float32)).astype(jnp.bfloat16)
-        high[pl.ds(start, step)] = rounded.reshape(step, block, columns)
-        low[pl.ds(start, step)] = rest.reshape(step, block, columns)
-        total = total + jnp.sum((value * value).reshape(step, block, columns), axis=0)
+        high[pl.ds(start, step)] = rounded
+        low[pl.ds(start, step)] = (value - rounded.astype(jnp.float32)).astype(jnp.bfloat16)
+        total = total + jnp.sum(value * value, axis=0)
     power[...] = total
 
 
@@ -168,7 +174,7 @@
             split_shape,
             jax.ShapeDtypeStruct((channels, columns), jnp.float32),
         ],
-        scratch_shapes=[pltpu.VMEM((outputs * block, columns), jnp.float32)],
+        scratch_shapes=[pltpu.VMEM((outputs, block, columns), jnp.float32)],
         compiler_params=pltpu.CompilerParams(vmem_limit_bytes=VMEM_LIMIT),
         cost_estimate=pl.CostEstimate(
             flops=4 * channels * outputs * columns * 256, bytes_accessed=80_000_000, transcendentals=0
@@ -192,34 +198,40 @@
     out[...] = staged[...].reshape(count, rows, columns).astype(jnp.bfloat16)
 
 
-def delay_chunk(matrix, high, low, block=16):
-    tile_rows, channels, columns = high.shape
+def delay_chunk(matrix, high, low, begin, rows, block=16):
+    _, channels, columns = high.shape
     count = matrix.shape[0] // 2
-    spec = pl.BlockSpec((block, channels, columns), lambda i: (i, 0, 0))
+    spec = pl.BlockSpec((block, channels, columns), lambda i: (begin // block + i, 0, 0))
     return pl.pallas_call(
         delay_kernel,
-        grid=(tile_rows // block,),
+        grid=(rows // block,),
         in_specs=[pl.BlockSpec(matrix.shape, lambda i: (0, 0)), spec, spec],
         out_specs=pl.BlockSpec((count, block, columns), lambda i: (0, i, 0)),
-        out_shape=jax.ShapeDtypeStruct((count, tile_rows, columns), jnp.bfloat16),
+        out_shape=jax.ShapeDtypeStruct((count, rows, columns), jnp.bfloat16),
         scratch_shapes=[pltpu.VMEM((count * block, columns), jnp.float32)],
         compiler_params=pltpu.CompilerParams(vmem_limit_bytes=VMEM_LIMIT),
         cost_estimate=pl.CostEstimate(
-            flops=6 * count * channels * tile_rows * columns,
-            bytes_accessed=40_000_000,
+            flops=6 * count * channels * rows * columns,
+            bytes_accessed=(4 * channels + 2 * count) * rows * columns,
             transcendentals=0,
         ),
         name="delays",
     )(matrix, high, low)
 
 
-def spatial_kernel(row_count, col_count, has_previous, slab, col_table, row_table, *refs):
+def spatial_kernel(row_count, col_count, head, tail, col_table, row_table, *refs):
     out, halfway = refs[-2:]
-    _, _, tile_rows, _ = slab.shape
+    tile_rows = head.shape[2] + tail.shape[2]
     side = row_count * tile_rows
     for a in range(row_count):
         line = jnp.concatenate(
-            [slab[a * col_count + b, k] for k in range(2) for b in range(col_count)], axis=1
+            [
+                jnp.concatenate(
+                    [slab[a * col_count + b, k] for k in range(2) for b in range(col_count)], axis=1
+                )
+                for slab in (head, tail)
+            ],
+            axis=0,
         )
         part = jnp.dot(line, col_table[...], preferred_element_type=jnp.float32)
         part = part.astype(jnp.bfloat16)
@@ -235,25 +247,25 @@
             )
 
 
-def spatial_chunk(received, col_table, row_table, shape, start, previous):
-    peers, parts, tile_rows, tile_cols = received.shape
-    items = parts // 2
+def spatial_chunk(head, tail, col_table, row_table, shape, start, previous):
+    peers, parts, tail_rows, tile_cols = tail.shape
+    items, head_rows = parts // 2, head.shape[2]
     side, columns = shape[2], shape[3]
+    row_count, col_count = side // (head_rows + tail_rows), columns // tile_cols
     in_specs = [
-        pl.BlockSpec((peers, 2, tile_rows, tile_cols), lambda i: (0, i, 0, 0)),
+        pl.BlockSpec((peers, 2, head_rows, tile_cols), lambda i: (0, start + i, 0, 0)),
+        pl.BlockSpec((peers, 2, tail_rows, tile_cols), lambda i: (0, i, 0, 0)),
         pl.BlockSpec(col_table.shape, lambda i: (0, 0)),
         pl.BlockSpec(row_table.shape, lambda i: (0, 0)),
     ]
-    operands = [received, col_table, row_table]
+    operands = [head, tail, col_table, row_table]
     aliases = {}
     if previous is not None:
         in_specs.append(pl.BlockSpec(memory_space=pl.ANY))
         operands.append(previous)
-        aliases = {3: 0}
+        aliases = {4: 0}
     return pl.pallas_call(
-        functools.partial(
-            spatial_kernel, side // tile_rows, columns // tile_cols, previous is not None
-        ),
+        functools.partial(spatial_kernel, row_count, col_count),
         grid=(items,),
         in_specs=in_specs,
         out_specs=pl.BlockSpec((1, 2, side, columns), lambda i: (start + i, 0, 0, 0)),
@@ -270,12 +282,14 @@
     )(*operands)
 
 
+def pinned(x):
+    return with_layout_constraint(x, Layout(major_to_minor=tuple(range(x.ndim))))
+
+
 def shifted(x, axis, step):
     size = lax.axis_size(axis)
     pairs = [(i, i + step) for i in range(size) if 0 <= i + step < size]
-    order = Layout(major_to_minor=tuple(range(x.ndim)))
-    x = with_layout_constraint(x, order)
-    return with_layout_constraint(lax.ppermute(x, axis, pairs), order)
+    return pinned(lax.ppermute(pinned(x), axis, pairs))
 
 
 def split_high_low(x):
@@ -286,7 +300,7 @@
 def chunk_sizes(per_device):
     if per_device <= 4 * END_DELAYS:
         return [per_device]
-    return [END_DELAYS, per_device - 2 * END_DELAYS, END_DELAYS]
+    return [per_device - END_DELAYS, END_DELAYS]
 
 
 def tiled_body(sky_cube, half_widths, pixel_mask, foreground_modes):
@@ -296,16 +310,16 @@
     per_device = channels // 2 // peers
     sides, columns = row_count * tile_rows, col_count * tile_cols
 
-    top = shifted(sky_cube[LAST], "row", 1)
-    bottom = shifted(sky_cube[FIRST], "row", -1)
-    left = shifted(sky_cube[:, LAST], "col", 1)
-    right = shifted(sky_cube[:, FIRST], "col", -1)
+    sky_cube, last, initial = lax.optimization_barrier((sky_cube, sky_cube[LAST], sky_cube[FIRST]))
+    top, bottom = shifted(last, "row", 1), shifted(initial, "row", -1)
+    left, right = shifted(sky_cube[:, LAST], "col", 1), shifted(sky_cube[:, FIRST], "col", -1)
     centre = jnp.transpose(sky_cube, (2, 0, 1))
     left, right, centre = lax.optimization_barrier((left, right, centre))
     ends = [jnp.concatenate([left[rows], right[rows]], axis=1) for rows in (LAST, FIRST)]
-    corner = jnp.concatenate([shifted(ends[0], "row", 1), shifted(ends[1], "row", -1)], axis=0)
-    pieces = [centre] + [jnp.transpose(x, (2, 0, 1)) for x in (top, bottom)]
-    pieces += [jnp.transpose(x, (2, 1, 0)) for x in (left, right, corner)]
+    corners = [shifted(ends[0], "row", 1), shifted(ends[1], "row", -1)]
+    caps = [pinned(jnp.concatenate([x, y], axis=1)) for x, y in zip((top, bottom), corners)]
+    pieces = [centre] + [jnp.transpose(x, (2, 0, 1)) for x in caps]
+    pieces += [jnp.transpose(x, (2, 1, 0)) for x in (left, right)]
 
     def places(length):
         return list(range(length)) + list(range(-HALF, 0)) + list(range(length, length + HALF))
@@ -315,17 +329,14 @@
     col_band = np.zeros((HALF, PACK, tile_cols + PACK * 2 * HALF, tile_cols), narrow.dtype)
     col_band[:, :, :tile_cols] = narrow[:, None, :tile_cols]
     for member in range(PACK):
-        for part in range(2):
-            to = tile_cols + (part * PACK + member) * HALF
-            begin = tile_cols + part * HALF
-            col_band[:, member, to : to + HALF] = narrow[:, begin : begin + HALF]
+        begin = tile_cols + member * 2 * HALF
+        col_band[:, member, begin : begin + 2 * HALF] = narrow[:, tile_cols:]
     col_band = col_band.reshape((HALF * PACK,) + col_band.shape[2:])
     high, low, power = smooth(
         half_widths, pixel_mask.astype(jnp.float32), pieces, row_band, col_band
     )
 
-    sizes = chunk_sizes(per_device)
-    delay_table = delay_rows(channels, peers, sizes)
+    delay_table = delay_rows(channels, peers, [per_device])
     mode_delays = jnp.dot(
         delay_table, foreground_modes.T, precision=highest, preferred_element_type=jnp.float32
     )
@@ -351,35 +362,26 @@
     cos_r, sin_r = dft_parts(sides)
     row_table = np.block([[cos_r, -sin_r], [sin_r, cos_r]])
 
+    def send(begin, end, first_row, rows):
+        parts = [
+            x.reshape(peers, per_device, 2, channels)[:, begin:end].reshape(-1, channels)
+            for x in (matrix_high, matrix_low)
+        ]
+        delays = delay_chunk(jnp.concatenate(parts, axis=0), high, low, first_row, rows)
+        return delays.reshape(peers, 2 * (end - begin), rows, tile_cols)
+
+    def exchange(x):
+        return lax.all_to_all(x, ("row", "col"), split_axis=0, concat_axis=0, tiled=True)
+
+    shape = (per_device, 2, sides, columns)
+    head = exchange(send(0, per_device, 0, HEAD_ROWS))
+    tail_rows = tile_rows - HEAD_ROWS
     spectrum = None
     start = 0
-    for index, size in enumerate(sizes):
-        begin, count = 2 * start * peers, 2 * size * peers
-        both = jnp.concatenate(
-            [matrix_high[begin : begin + count], matrix_low[begin : begin + count]], axis=0
-        )
-        delays = delay_chunk(both, high, low)
-        delays = delays.reshape(peers, 2 * size, tile_rows, tile_cols)
-        if index == 2:
-            delays, spectrum = lax.optimization_barrier((delays, spectrum))
-        received = lax.all_to_all(delays, ("row", "col"), split_axis=0, concat_axis=0, tiled=True)
-        if index == 1:
-            held = received
-            spectrum = spatial_chunk(
-                first_received, col_table, row_table, (per_device, 2, sides, columns), 0, None
-            )
-        elif index == 2:
-            spectrum = spatial_chunk(
-                held, col_table, row_table, spectrum.shape, sizes[0], spectrum
-            )
-            spectrum = spatial_chunk(received, col_table, row_table, spectrum.shape, start, spectrum)
-        else:
-            first_received = received
+    for size in chunk_sizes(per_device):
+        tail = exchange(send(start, start + size, HEAD_ROWS, tail_rows))
+        spectrum = spatial_chunk(head, tail, col_table, row_table, shape, start, spectrum)
         start += size
-    if len(sizes) == 1:
-        spectrum = spatial_chunk(
-            first_received, col_table, row_table, (per_device, 2, sides, columns), 0, None
-        )
     return (spectrum, channel_weights)
 
 

time: 577 us -> 563 us (0.976)
  Pallas kernels: 163 us -> 138 us
  other arithmetic: 7.83 us -> 14 us
    optimization_barrier x0 -> x1, local copies, waits for them, and re-layouts: none -> 23.5 us  [tiled_body(): lax.optimization_barrier((sky_cube, sky_cube[LAST], sky_cube[FIRST]))]
    unnamed x25 -> x22, local copies, waits for them, and re-layouts: 29.6 us -> 7.34 us
    pallas_call x1, Pallas kernels: 57.8 us -> 44 us  [smooth(): pl.pallas_call(smooth_kernel, grid=(channels // block,), in_specs=[pl.Blo...]
    pallas_call x6 -> x5, Pallas kernels: 105 us -> 93.6 us  [the longest x3 49 us: delay_chunk(): pl.pallas_call(delay_kernel, grid=(rows // block,), in_specs=[pl.BlockSpe...]
    concatenate x1 -> x0, local copies, waits for them, and re-layouts: 8.67 us -> none  [tiled_body(): jnp.concatenate([shifted(ends[0], 'row', 1), shifted(ends[1], 'row', -1)]...]
    another operation x2, local copies, waits for them, and re-layouts: 7.97 us -> 15.4 us  [pinned(): with_layout_constraint(x, Layout(major_to_minor=tuple(range(x.ndim))))]
  transfers between devices with their start and end apart: 10 -> 10, of which waited for: 7 -> 6; matrix products, arithmetic and copies ran while one was open for 9% -> 9% of each run, Pallas kernels for 14% -> 14%
where the time goes in v3:
time: 563 us; the launch traced here: 561 us
  waiting for transfers between devices  294 us (52%)
  Pallas kernels  138 us (25%)
  local copies, waits for them, and re-layouts  70.5 us (13%)
  starting transfers between devices  39.5 us (7%)
  other arithmetic  14 us (2%)
    all_to_all x3, waiting for transfers between devices, exchange(): lax.all_to_all(x, ('row', 'col'), split_axis=0, concat_axis=0, tiled=True)  281 us
    pallas_call x3, Pallas kernels, delay_chunk(): pl.pallas_call(delay_kernel, grid=(rows // block,), in_specs=[pl.BlockSpe...  49 us
    pallas_call x2, Pallas kernels, spatial_chunk(): pl.pallas_call(functools.partial(spatial_kernel, row_count, col_count), g...  44.6 us
    pallas_call x1, Pallas kernels, smooth(): pl.pallas_call(smooth_kernel, grid=(channels // block,), in_specs=[pl.Blo...  44 us
    optimization_barrier x1, local copies, waits for them, and re-layouts, tiled_body(): lax.optimization_barrier((sky_cube, sky_cube[LAST], sky_cube[FIRST]))  23.5 us
    all_to_all x3, starting transfers between devices, exchange(): lax.all_to_all(x, ('row', 'col'), split_axis=0, concat_axis=0, tiled=True)  16.2 us
    ppermute x6, starting transfers between devices, shifted(): return pinned(lax.ppermute(pinned(x), axis, pairs))  15.7 us
    another operation x2, local copies, waits for them, and re-layouts, pinned(): with_layout_constraint(x, Layout(major_to_minor=tuple(range(x.ndim))))  15.4 us
  transfers between devices with their start and end apart: 10, of which 6 were waited for; matrix products, arithmetic and copies ran while one was open for 9% of the time, Pallas kernels for 14%

profile of v3, /device:TPU:11, one launch (start us, length us, event | category | flops | bytes accessed | tf_op | source)
XLA Modules:
  0.0 560.8 jit_solution(14125789843438605059)
XLA Ops:
  0.6 4.6 fusion.16
  5.3 4.7 fusion.15
  10.0 2.7 collective-permute-start.1
  14.0 2.1 collective-permute-start.4
  16.1 3.2 collective-permute-start.2
  19.3 23.5 %copy.24 = bf16[128,128,512]{1,0,2:T(8,128)(2,1)} copy(bf16[128,128,512]{2,1,0:T(8,128)(2,1)} %param.9) | data formatting | bytes 33554432 | tf_op jit(solution)/shard_map/optimization_barrier | solution.py:313
  45.2 3.4 collective-permute-start.5
  49.5 3.0 collective-permute-start.3
  52.5 4.2 copy.28
  56.8 5.2 copy.27
  62.2 11.1 %collective-permute-done.5 = bf16[16,32,512]{2,1,0:T(8,128)(2,1)S(1)} collective-permute-done((bf16[16,32,512]{2,1,0:T(8,128)(2,1)}, bf16[16,32,512]{2,1,0:T(8,128)(2,1)S(1)}, u32[]{:S(2)}, u32[]{:S(2)}) %collective-permute-start.5) | collective-permute-done | bytes 524320 | tf_op jit(solution)/shard_map/ppermute | solution.py:292
  73.3 3.3 pad_maximum_fusion.1
  76.6 7.6 %copy.26 = bf16[16,160,512]{1,0,2:T(8,128)(2,1)} copy(bf16[16,160,512]{2,1,0:T(8,128)(2,1)} %pad_maximum_fusion.1) | data formatting | bytes 5242880 | tf_op jit(solution)/shard_map/layout_constraint | solution.py:286
  84.3 3.3 pad_maximum_fusion
  87.6 7.8 %copy.25 = bf16[16,160,512]{1,0,2:T(8,128)(2,1)} copy(bf16[16,160,512]{2,1,0:T(8,128)(2,1)} %pad_maximum_fusion) | data formatting | bytes 5242880 | tf_op jit(solution)/shard_map/layout_constraint | solution.py:286
  97.0 44.0 %smooth.1 = (bf16[128,512,128]{2,1,0:T(8,128)(2,1)}, bf16[128,512,128]{2,1,0:T(8,128)(2,1)}, f32[512,128]{1,0:T(8,128)S(1)}) custom-call(s32[512]{0:T(512)S(1)} %copy-done.6, f32[128,128]{1,0:T(8,128)S(1)} %convert_element_type.9.mask, bf16[16,128,160]{2,1,0:T(8,128)(2,1)S(1)} %copy-done.5, bf16[64,256,128]{2,1,0:T(8,128)(2,1)} %constant.71.clone.col_band, ...), custom_call_target="tpu_custom_call" | custom-call | flops 8589934592 | bytes 80000000 | tf_op jit(solution)/shard_map/smooth/pallas_call | solution.py:165
  141.8 7.6 %all-to-all-start = ((f32[16,1,512]{2,1,0:T(1,128)}), f32[16,1,512]{2,1,0:T(1,128)S(1)}, u32[]{:S(2)}, u32[]{:S(2)}) async-start(f32[16,1,512]{2,1,0:T(1,128)} %broadcast_in_dim.3), calls=%async_computation | async-start | bytes 65536 | tf_op jit(solution)/shard_map/all_to_all | solution.py:345
  149.4 2.2 fusion.19
  151.6 1.9 all-to-all-done
  160.1 6.5 %delays.3 = bf16[512,16,128]{2,1,0:T(8,128)(2,1)S(1)} custom-call(bf16[1024,512]{1,0:T(8,128)(2,1)S(1)} %pad_maximum_fusion.2.modes, bf16[128,512,128]{2,1,0:T(8,128)(2,1)} %get-tuple-element.18.high, bf16[128,512,128]{2,1,0:T(8,128)(2,1)} %get-tuple-element.19.low), custom_call_target="tpu_custom_call" | custom-call | flops 3221225472 | bytes 6291456 | tf_op jit(solution)/shard_map/delays/pallas_call | solution.py:205
  167.9 6.3 %all-to-all-start.1 = ((bf16[16,32,16,128]{3,2,1,0:T(8,128)(2,1)}), bf16[16,32,16,128]{3,2,1,0:T(8,128)(2,1)S(1)}, u32[]{:S(2)}, u32[]{:S(2)}) async-start(bf16[16,32,16,128]{3,2,1,0:T(8,128)(2,1)} %bitcast.27), calls=%async_computation.1 | async-start | bytes 4194304 | tf_op jit(solution)/shard_map/all_to_all | solution.py:374
  177.5 29.6 %delays.5 = bf16[448,112,128]{2,1,0:T(8,128)(2,1)} custom-call(bf16[896,512]{1,0:T(8,128)(2,1)S(1)} %pad_maximum_fusion.3.modes, bf16[128,512,128]{2,1,0:T(8,128)(2,1)} %get-tuple-element.18.high, bf16[128,512,128]{2,1,0:T(8,128)(2,1)} %get-tuple-element.19.low), custom_call_target="tpu_custom_call" | custom-call | flops 19730006016 | bytes 42205184 | tf_op jit(solution)/shard_map/delays/pallas_call | solution.py:205
  207.1 14.5 %all-to-all-done.1.head = bf16[16,32,16,128]{3,2,1,0:T(8,128)(2,1)S(1)} async-done(((bf16[16,32,16,128]{3,2,1,0:T(8,128)(2,1)}), bf16[16,32,16,128]{3,2,1,0:T(8,128)(2,1)S(1)}, u32[]{:S(2)}, u32[]{:S(2)}) %all-to-all-start.1) | async-done | bytes 2097184 | tf_op jit(solution)/shard_map/all_to_all | solution.py:374
  221.6 5.0 all-to-all-start.3
  226.7 12.9 %delays.4 = bf16[64,112,128]{2,1,0:T(8,128)(2,1)S(1)} custom-call(bf16[128,512]{1,0:T(8,128)(2,1)S(1)} %pad_maximum_fusion.6.modes, bf16[128,512,128]{2,1,0:T(8,128)(2,1)} %get-tuple-element.18.high, bf16[128,512,128]{2,1,0:T(8,128)(2,1)} %get-tuple-element.19.low), custom_call_target="tpu_custom_call" | custom-call | flops 2818572288 | bytes 31195136 | tf_op jit(solution)/shard_map/delays/pallas_call | solution.py:205
  240.9 263.6 %all-to-all-done.3.tail = bf16[16,28,112,128]{3,2,1,0:T(8,128)(2,1)} async-done(((bf16[16,28,112,128]{3,2,1,0:T(8,128)(2,1)}), bf16[16,28,112,128]{3,2,1,0:T(8,128)(2,1)}, u32[]{:S(2)}, u32[]{:S(2)}) %all-to-all-start.3) | async-done | bytes 12845088 | tf_op jit(solution)/shard_map/all_to_all | solution.py:374
  504.5 4.9 all-to-all-start.2
  510.6 1.6 copy-done.3
  512.2 36.6 %spatial.2.refs_0_ = f32[16,2,512,512]{3,2,1,0:T(8,128)} custom-call(bf16[16,32,16,128]{3,2,1,0:T(8,128)(2,1)S(1)} %all-to-all-done.1.head, bf16[16,28,112,128]{3,2,1,0:T(8,128)(2,1)} %all-to-all-done.3.tail, bf16[1024,1024]{1,0:T(8,128)(2,1)S(1)} %copy-done.3, bf16[1024,1024]{1,0:T(8,128)(2,1)} %constant.74.clone.row_table), custom_call_target="tpu_custom_call" | custom-call | flops 30064771072 | bytes 44040192 | tf_op jit(solution)/shard_map/spatial/pallas_call | solution.py:267
  548.8 2.5 all-to-all-done.2.tail
  551.3 1.6 copy-done.4
  552.9 8.0 %spatial.3 = f32[16,2,512,512]{3,2,1,0:T(8,128)} custom-call(bf16[16,32,16,128]{3,2,1,0:T(8,128)(2,1)S(1)} %all-to-all-done.1.head, bf16[16,4,112,128]{3,2,1,0:T(8,128)(2,1)} %all-to-all-done.2.tail, bf16[1024,1024]{1,0:T(8,128)(2,1)S(1)} %copy-done.4, bf16[1024,1024]{1,0:T(8,128)(2,1)} %constant.74.clone.row_table, ...), custom_call_target="tpu_custom_call", output_to_operand_aliasing={{}: (4, {})} | custom-call | flops 4294967296 | bytes 6291456 | tf_op jit(solution)/shard_map/spatial/pallas_call | solution.py:267
  (63 shorter events, 20.2 us)
Async XLA Ops:
  10.0 32.8 %collective-permute-start.1 = (bf16[128,16,512]{2,1,0:T(8,128)(2,1)}, bf16[128,16,512]{2,1,0:T(8,128)(2,1)S(1)}, u32[]{:S(2)}, u32[]{:S(2)}) collective-permute-start(bf16[128,16,512]{2,1,0:T(8,128)(2,1)} %get-tuple-element.22), channel_id=1, source_target_pairs={{1,0},{2,1},{3,2},{5,4},{6,5},{7,6},{9,8},{10,9},{11,10},{13,12},{... | collective-permute-start | bytes 6291464 | tf_op jit(solution)/shard_map/ppermute | solution.py:292
  12.7 30.1 %collective-permute-start = (bf16[128,16,512]{2,1,0:T(8,128)(2,1)}, bf16[128,16,512]{2,1,0:T(8,128)(2,1)}, u32[]{:S(2)}, u32[]{:S(2)}) collective-permute-start(bf16[128,16,512]{2,1,0:T(8,128)(2,1)} %get-tuple-element.23), channel_id=1, source_target_pairs={{0,1},{1,2},{2,3},{4,5},{5,6},{6,7},{8,9},{9,10},{10,11},{12,13},{... | collective-permute-start | bytes 6291464 | tf_op jit(solution)/shard_map/ppermute | solution.py:292
  14.0 48.2 %collective-permute-start.4 = (bf16[16,128,512]{2,1,0:T(8,128)(2,1)}, bf16[16,128,512]{2,1,0:T(8,128)(2,1)}, u32[]{:S(2)}, u32[]{:S(2)}) collective-permute-start(bf16[16,128,512]{2,1,0:T(8,128)(2,1)} %get-tuple-element.16), channel_id=1, source_target_pairs={{4,0},{8,4},{12,8},{5,1},{9,5},{13,9},{6,2},{10,6},{14,10},{7,3},{... | collective-permute-start | bytes 6291464 | tf_op jit(solution)/shard_map/ppermute | solution.py:292
  16.1 68.2 %collective-permute-start.2 = (bf16[16,128,512]{2,1,0:T(8,128)(2,1)}, bf16[16,128,512]{2,1,0:T(8,128)(2,1)}, u32[]{:S(2)}, u32[]{:S(2)}) collective-permute-start(bf16[16,128,512]{2,1,0:T(8,128)(2,1)} %get-tuple-element.13), channel_id=1, source_target_pairs={{0,4},{4,8},{8,12},{1,5},{5,9},{9,13},{2,6},{6,10},{10,14},{3,7},{... | collective-permute-start | bytes 6291464 | tf_op jit(solution)/shard_map/ppermute | solution.py:292
  42.7 6.7 %copy-start.8 = (bf16[128,16,512]{2,1,0:T(8,128)(2,1)}, bf16[128,16,512]{2,1,0:T(8,128)(2,1)S(1)}, u32[]{:S(2)}) copy-start(bf16[128,16,512]{2,1,0:T(8,128)(2,1)S(1)} %collective-permute-done.1) | copy-start | bytes 6291460
  42.8 9.7 %copy-start.10 = (s32[128,128]{1,0:T(8,128)S(1)}, s32[128,128]{1,0:T(8,128)}, u32[]{:S(2)}) copy-start(s32[128,128]{1,0:T(8,128)} %param.11) | copy-start | bytes 196612
  45.2 28.1 %collective-permute-start.5 = (bf16[16,32,512]{2,1,0:T(8,128)(2,1)}, bf16[16,32,512]{2,1,0:T(8,128)(2,1)S(1)}, u32[]{:S(2)}, u32[]{:S(2)}) collective-permute-start(bf16[16,32,512]{2,1,0:T(8,128)(2,1)} %pad_maximum_fusion.5), channel_id=1, source_target_pairs={{4,0},{8,4},{12,8},{5,1},{9,5},{13,9},{6,2},{10,6},{14,10},{7,3},{... | collective-permute-start | bytes 1572872 | tf_op jit(solution)/shard_map/ppermute | solution.py:292
  49.5 34.8 %collective-permute-start.3 = (bf16[16,32,512]{2,1,0:T(8,128)(2,1)}, bf16[16,32,512]{2,1,0:T(8,128)(2,1)S(1)}, u32[]{:S(2)}, u32[]{:S(2)}) collective-permute-start(bf16[16,32,512]{2,1,0:T(8,128)(2,1)} %pad_maximum_fusion.4), channel_id=1, source_target_pairs={{0,4},{4,8},{8,12},{1,5},{5,9},{9,13},{2,6},{6,10},{10,14},{3,7},{... | collective-permute-start | bytes 1572872 | tf_op jit(solution)/shard_map/ppermute | solution.py:292
  87.6 7.8 %copy-start.5 = (bf16[16,128,160]{2,1,0:T(8,128)(2,1)S(1)}, bf16[16,128,160]{2,1,0:T(8,128)(2,1)}, u32[]{:S(2)}) copy-start(bf16[16,128,160]{2,1,0:T(8,128)(2,1)} %constant.70.clone.row_band) | copy-start | bytes 1966084
  87.6 7.8 %copy-start.6 = (s32[512]{0:T(512)S(1)}, s32[512]{0:T(512)}, u32[]{:S(2)}) copy-start(s32[512]{0:T(512)} %widths.1) | copy-start | bytes 6148
  95.4 1.6 copy-start
  97.0 52.4 %copy-start.9 = (f32[16,512]{1,0:T(8,128)S(1)}, f32[16,512]{1,0:T(8,128)}, u32[]{:S(2)}) copy-start(f32[16,512]{1,0:T(8,128)} %param.12) | copy-start | bytes 98308
  141.0 17.9 %copy-start.7 = (f32[512,512]{1,0:T(8,128)S(1)}, f32[512,512]{1,0:T(8,128)}, u32[]{:S(2)}) copy-start(f32[512,512]{1,0:T(8,128)} %constant.72.clone) | copy-start | bytes 3145732
  141.8 11.8 %all-to-all-start = ((f32[16,1,512]{2,1,0:T(1,128)}), f32[16,1,512]{2,1,0:T(1,128)S(1)}, u32[]{:S(2)}, u32[]{:S(2)}) async-start(f32[16,1,512]{2,1,0:T(1,128)} %broadcast_in_dim.3), calls=%async_computation | async-start | bytes 65536 | tf_op jit(solution)/shard_map/all_to_all | solution.py:345
  166.6 1.3 copy-start.1
  167.9 53.7 %all-to-all-start.1 = ((bf16[16,32,16,128]{3,2,1,0:T(8,128)(2,1)}), bf16[16,32,16,128]{3,2,1,0:T(8,128)(2,1)S(1)}, u32[]{:S(2)}, u32[]{:S(2)}) async-start(bf16[16,32,16,128]{3,2,1,0:T(8,128)(2,1)} %bitcast.27), calls=%async_computation.1 | async-start | bytes 4194304 | tf_op jit(solution)/shard_map/all_to_all | solution.py:374
  175.2 1.0 slice-start
  176.2 1.0 slice-start.2
  221.6 5.0 slice-start.1
  221.6 5.1 slice-start.3
  221.6 282.9 %all-to-all-start.3 = ((bf16[16,28,112,128]{3,2,1,0:T(8,128)(2,1)}), bf16[16,28,112,128]{3,2,1,0:T(8,128)(2,1)}, u32[]{:S(2)}, u32[]{:S(2)}) async-start(bf16[16,28,112,128]{3,2,1,0:T(8,128)(2,1)} %bitcast.32), calls=%async_computation.3 | async-start | bytes 25690112 | tf_op jit(solution)/shard_map/all_to_all | solution.py:374
  239.7 1.2 copy-start.2
  504.5 46.8 %all-to-all-start.2 = ((bf16[16,4,112,128]{3,2,1,0:T(8,128)(2,1)}), bf16[16,4,112,128]{3,2,1,0:T(8,128)(2,1)}, u32[]{:S(2)}, u32[]{:S(2)}) async-start(bf16[16,4,112,128]{3,2,1,0:T(8,128)(2,1)} %bitcast.28), calls=%async_computation.2 | async-start | bytes 3670016 | tf_op jit(solution)/shard_map/all_to_all | solution.py:374
  510.6 1.6 copy-start.3
  551.3 1.6 copy-start.4

commit v4 on v3

--- a/solution.py
+++ b/solution.py
@@ -14,7 +14,8 @@
 VMEM_LIMIT = 48 * 1024 * 1024
 PACK = 4
 TURN = 8
-HEAD_ROWS = 16
+HEAD_ROWS = 48
+LANES = 128
 FIRST, LAST = slice(0, HALF), slice(-HALF, None)
 END_DELAYS = 2
 
@@ -110,105 +111,142 @@
     return taps[:, np.minimum(distance, HALF + 1)].astype(jnp.bfloat16)
 
 
-def smooth_kernel(widths, mask, row_band, col_band, centre, top, bottom, left, right, *outs):
-    high, low, power, staged = outs
+def smooth_kernel(spans, capped, widths, mask, row_band, col_band, centre, left, right, *refs):
+    if capped:
+        top, bottom, top_ends, bottom_ends, *refs = refs
+        high, low, power, staged, sides, caps, corners = refs
+    else:
+        high, low, power, staged, sides = refs
     block = centre.shape[0]
     outputs, columns = mask.shape
-    first = pl.program_id(0) * block
+    rows = sides.shape[2]
+    step = pl.program_id(0)
+    per_turn = LANES // block
+
+    @pl.when(step % per_turn == 0)
+    def _():
+        sides[:, FIRST] = jnp.transpose(left[...], (2, 1, 0))
+        sides[:, HALF : 2 * HALF] = jnp.transpose(right[...], (2, 1, 0))
+        if capped:
+            caps[:, FIRST] = jnp.transpose(top[...], (2, 0, 1))
+            caps[:, HALF : 2 * HALF] = jnp.transpose(bottom[...], (2, 0, 1))
+            corners[:, FIRST] = jnp.transpose(top_ends[...], (2, 0, 1))
+            corners[:, HALF : 2 * HALF] = jnp.transpose(bottom_ends[...], (2, 0, 1))
+
+    first = step * block
+    lane = (step % per_turn) * block
     kept = mask[...]
     done = []
     for group in range(0, block, PACK):
         members = range(group, group + PACK)
-        chosen = pl.ds(group, PACK)
-        flank = jnp.concatenate([left[chosen], right[chosen]], axis=1)
-        flank = flank.reshape(PACK * 2 * HALF, outputs).T
-        caps = [jnp.concatenate([top[j], bottom[j]], axis=0) for j in members]
-        corner = jnp.concatenate([x[:, columns:] for x in caps], axis=1)
-        flank = jnp.concatenate([flank, corner], axis=0)
+        flank = sides[pl.ds(lane + group, PACK)].reshape(PACK * 2 * HALF, rows).T
+        flank = [flank[a:b] for a, b in spans]
+        if capped:
+            corner = [corners[lane + j] for j in members]
+            flank.append(jnp.concatenate(corner, axis=1))
+        flank = jnp.concatenate(flank, axis=0)
         half_smoothed = []
-        for j, cap in zip(members, caps):
-            data = jnp.concatenate([centre[j], cap[:, :columns]], axis=0)
-            data = jnp.concatenate([data, flank], axis=1)
+        for j in members:
+            data = [centre[j, a:b] for a, b in spans]
+            if capped:
+                data.append(caps[lane + j])
+            data = jnp.concatenate([jnp.concatenate(data, axis=0), flank], axis=1)
             band = row_band[widths[first + j] - 1]
             half_smoothed.append(
                 jnp.dot(band, data, preferred_element_type=jnp.float32).astype(jnp.bfloat16)
             )
-        for j, rows in zip(members, half_smoothed):
+        for j, half in zip(members, half_smoothed):
             band = col_band[(widths[first + j] - 1) * PACK + j % PACK]
-            smoothed = jnp.dot(rows, band, preferred_element_type=jnp.float32)
+            smoothed = jnp.dot(half, band, preferred_element_type=jnp.float32)
             done.append(smoothed * kept)
         if len(done) == TURN:
             begin = group + PACK - TURN
             staged[:, pl.ds(begin, TURN), :] = jnp.swapaxes(jnp.stack(done), 0, 1)
             done = []
 
-    step = 8
+    step_rows = 8
     total = jnp.zeros((block, columns), jnp.float32)
-    for start in range(0, outputs, step):
-        value = staged[pl.ds(start, step)]
+    for start in range(0, outputs, step_rows):
+        value = staged[pl.ds(start, step_rows)]
         rounded = value.astype(jnp.bfloat16)
-        high[pl.ds(start, step)] = rounded
-        low[pl.ds(start, step)] = (value - rounded.astype(jnp.float32)).astype(jnp.bfloat16)
+        high[pl.ds(start, step_rows)] = rounded
+        low[pl.ds(start, step_rows)] = (value - rounded.astype(jnp.float32)).astype(jnp.bfloat16)
         total = total + jnp.sum(value * value, axis=0)
     power[...] = total
 
 
-def smooth(half_widths, mask, pieces, row_band, col_band, block=32):
-    centre = pieces[0]
-    channels, _, columns = centre.shape
+def smooth(half_widths, mask, centre, sides, caps, spans, row_band, col_band, block=32):
+    channels, tile_rows, columns = centre.shape
     outputs = mask.shape[0]
+    per_turn = LANES // block
     whole = lambda shape: pl.BlockSpec(shape, lambda i: (0,) * len(shape))
-    piece = lambda x: pl.BlockSpec((block,) + x.shape[1:], lambda i: (i, 0, 0))
+    halo = lambda x: pl.BlockSpec(x.shape[:2] + (LANES,), lambda i: (0, 0, i // per_turn))
     split_spec = pl.BlockSpec((outputs, block, columns), lambda i: (0, i, 0))
     split_shape = jax.ShapeDtypeStruct((outputs, channels, columns), jnp.bfloat16)
     tables = [mask, row_band, col_band]
+    scratch = [
+        pltpu.VMEM((outputs, block, columns), jnp.float32),
+        pltpu.VMEM((LANES, 2 * HALF, tile_rows), jnp.bfloat16),
+    ]
+    if caps:
+        scratch += [
+            pltpu.VMEM((LANES, 2 * HALF, columns), jnp.bfloat16),
+            pltpu.VMEM((LANES, 2 * HALF, 2 * HALF), jnp.bfloat16),
+        ]
     return pl.pallas_call(
-        smooth_kernel,
+        functools.partial(smooth_kernel, spans, bool(caps)),
         grid=(channels // block,),
         in_specs=[pl.BlockSpec(memory_space=pltpu.SMEM)]
         + [whole(t.shape) for t in tables]
-        + [piece(x) for x in pieces],
+        + [pl.BlockSpec((block, tile_rows, columns), lambda i: (i, 0, 0))]
+        + [halo(x) for x in sides + caps],
         out_specs=[split_spec, split_spec, pl.BlockSpec((block, columns), lambda i: (i, 0))],
         out_shape=[
             split_shape,
             split_shape,
             jax.ShapeDtypeStruct((channels, columns), jnp.float32),
         ],
-        scratch_shapes=[pltpu.VMEM((outputs, block, columns), jnp.float32)],
+        scratch_shapes=scratch,
         compiler_params=pltpu.CompilerParams(vmem_limit_bytes=VMEM_LIMIT),
         cost_estimate=pl.CostEstimate(
-            flops=4 * channels * outputs * columns * 256, bytes_accessed=80_000_000, transcendentals=0
+            flops=16 * channels * tile_rows * columns * 256,
+            bytes_accessed=80_000_000,
+            transcendentals=0,
         ),
         name="smooth",
-    )(half_widths, *tables, *pieces)
-
-
-def delay_kernel(modes, high, low, out, staged):
+    )(half_widths, *tables, centre, *sides, *caps)
+
+
+def delay_kernel(matrix, high, low, out, staged):
     rows = high.shape[0]
     count, _, columns = out.shape
+    done = []
     for pair in range(rows // 2):
         first, second = 2 * pair, 2 * pair + 1
         coarse = jnp.concatenate([high[first], high[second]], axis=1)
         fine = jnp.concatenate([low[first], low[second]], axis=1)
-        both = jnp.dot(modes[...], coarse, preferred_element_type=jnp.float32)
+        both = jnp.dot(matrix[...], coarse, preferred_element_type=jnp.float32)
         value = both[:count] + both[count:]
-        value = value + jnp.dot(modes[:count], fine, preferred_element_type=jnp.float32)
-        staged[pl.ds(first, count, stride=rows), :] = value[:, :columns]
-        staged[pl.ds(second, count, stride=rows), :] = value[:, columns:]
-    out[...] = staged[...].reshape(count, rows, columns).astype(jnp.bfloat16)
-
-
-def delay_chunk(matrix, high, low, begin, rows, block=16):
-    _, channels, columns = high.shape
+        value = value + jnp.dot(matrix[:count], fine, preferred_element_type=jnp.float32)
+        done += [value[:, :columns], value[:, columns:]]
+        if len(done) == TURN:
+            begin = second + 1 - TURN
+            staged[:, pl.ds(begin, TURN), :] = jnp.swapaxes(jnp.stack(done), 0, 1)
+            done = []
+    out[...] = staged[...].astype(jnp.bfloat16)
+
+
+def delay_chunk(matrix, high, low, block=16):
+    rows, channels, columns = high.shape
     count = matrix.shape[0] // 2
-    spec = pl.BlockSpec((block, channels, columns), lambda i: (begin // block + i, 0, 0))
+    spec = pl.BlockSpec((block, channels, columns), lambda i: (i, 0, 0))
     return pl.pallas_call(
         delay_kernel,
         grid=(rows // block,),
         in_specs=[pl.BlockSpec(matrix.shape, lambda i: (0, 0)), spec, spec],
         out_specs=pl.BlockSpec((count, block, columns), lambda i: (0, i, 0)),
         out_shape=jax.ShapeDtypeStruct((count, rows, columns), jnp.bfloat16),
-        scratch_shapes=[pltpu.VMEM((count * block, columns), jnp.float32)],
+        scratch_shapes=[pltpu.VMEM((count, block, columns), jnp.float32)],
         compiler_params=pltpu.CompilerParams(vmem_limit_bytes=VMEM_LIMIT),
         cost_estimate=pl.CostEstimate(
             flops=6 * count * channels * rows * columns,
@@ -217,6 +255,38 @@
         ),
         name="delays",
     )(matrix, high, low)
+
+
+def correct_kernel(weights, delays, modes, out):
+    _, count, rows, _ = delays.shape
+    mode_count = modes.shape[1]
+
+    @pl.loop(0, rows // HALF)
+    def _(part):
+        here = pl.ds(pl.multiple_of(part * HALF, HALF), HALF)
+        values = [modes[0, m, here].astype(jnp.float32) for m in range(mode_count)]
+        for d in range(count):
+            total = delays[0, d, here].astype(jnp.float32)
+            for m in range(mode_count):
+                total = total - weights[d, m] * values[m]
+            out[0, d, here] = total.astype(jnp.bfloat16)
+
+
+def correct(weights, delays, modes):
+    peers = delays.shape[0]
+    piece = lambda x: pl.BlockSpec((1,) + x.shape[1:], lambda i: (i, 0, 0, 0))
+    return pl.pallas_call(
+        correct_kernel,
+        grid=(peers,),
+        in_specs=[pl.BlockSpec(memory_space=pltpu.SMEM), piece(delays), piece(modes)],
+        out_specs=piece(delays),
+        out_shape=jax.ShapeDtypeStruct(delays.shape, delays.dtype),
+        compiler_params=pltpu.CompilerParams(vmem_limit_bytes=VMEM_LIMIT),
+        cost_estimate=pl.CostEstimate(
+            flops=32 * delays.size, bytes_accessed=4 * delays.size, transcendentals=0
+        ),
+        name="correct",
+    )(weights, delays, modes)
 
 
 def spatial_kernel(row_count, col_count, head, tail, col_table, row_table, *refs):
@@ -292,6 +362,19 @@
     return pinned(lax.ppermute(pinned(x), axis, pairs))
 
 
+def outside(length):
+    return [*range(-HALF, 0), *range(length, length + HALF)]
+
+
+def exact_dot(x, y):
+    return jnp.dot(x, y, precision=highest, preferred_element_type=jnp.float32)
+
+
+def fit(normal_matrix, modes):
+    factor = jnp.linalg.cholesky(normal_matrix)
+    return jax.scipy.linalg.cho_solve((factor, True), modes)
+
+
 def split_high_low(x):
     rounded = lax.reduce_precision(x, exponent_bits=8, mantissa_bits=7)
     return rounded.astype(jnp.bfloat16), (x - rounded).astype(jnp.bfloat16)
@@ -316,70 +399,91 @@
     centre = jnp.transpose(sky_cube, (2, 0, 1))
     left, right, centre = lax.optimization_barrier((left, right, centre))
     ends = [jnp.concatenate([left[rows], right[rows]], axis=1) for rows in (LAST, FIRST)]
-    corners = [shifted(ends[0], "row", 1), shifted(ends[1], "row", -1)]
-    caps = [pinned(jnp.concatenate([x, y], axis=1)) for x, y in zip((top, bottom), corners)]
-    pieces = [centre] + [jnp.transpose(x, (2, 0, 1)) for x in caps]
-    pieces += [jnp.transpose(x, (2, 1, 0)) for x in (left, right)]
-
-    def places(length):
-        return list(range(length)) + list(range(-HALF, 0)) + list(range(length, length + HALF))
-
-    row_band = band_table(list(range(tile_rows)), places(tile_rows))
-    narrow = np.swapaxes(band_table(list(range(tile_cols)), places(tile_cols)), 1, 2)
+    top_ends, bottom_ends = shifted(ends[0], "row", 1), shifted(ends[1], "row", -1)
+
+    narrow = band_table(range(tile_cols), [*range(tile_cols), *outside(tile_cols)])
+    narrow = np.swapaxes(narrow, 1, 2)
     col_band = np.zeros((HALF, PACK, tile_cols + PACK * 2 * HALF, tile_cols), narrow.dtype)
     col_band[:, :, :tile_cols] = narrow[:, None, :tile_cols]
     for member in range(PACK):
         begin = tile_cols + member * 2 * HALF
         col_band[:, member, begin : begin + 2 * HALF] = narrow[:, tile_cols:]
     col_band = col_band.reshape((HALF * PACK,) + col_band.shape[2:])
-    high, low, power = smooth(
-        half_widths, pixel_mask.astype(jnp.float32), pieces, row_band, col_band
-    )
-
+    mask = pixel_mask.astype(jnp.float32)
+
+    head_end = HALF + HEAD_ROWS
+    head_rows = list(range(HALF, head_end))
+    tail_rows = [*range(HALF), *range(head_end, tile_rows)]
+    head_span = ((0, head_end + HALF),)
+    tail_spans = ((0, 2 * HALF), (HEAD_ROWS, tile_rows))
+
+    modes_t = foreground_modes.T
     delay_table = delay_rows(channels, peers, [per_device])
-    mode_delays = jnp.dot(
-        delay_table, foreground_modes.T, precision=highest, preferred_element_type=jnp.float32
-    )
-    tile_power = jnp.broadcast_to(jnp.sum(power, axis=1)[None], (peers, channels))
-    power_sum = jnp.sum(
-        lax.all_to_all(tile_power, ("row", "col"), split_axis=0, concat_axis=0, tiled=True), axis=0
-    )
+    mode_delays = exact_dot(delay_table, modes_t)
+    plain_fit = fit(exact_dot(foreground_modes, modes_t), foreground_modes)
+
+    def stacked(matrix, begin, end):
+        matrix = matrix.reshape(peers, per_device, 2, channels)[:, begin:end]
+        return jnp.concatenate(split_high_low(matrix.reshape(-1, channels)), axis=0)
+
+    def exchange(delays, items):
+        delays = delays.reshape(peers, 2 * items, -1, tile_cols)
+        return lax.all_to_all(delays, ("row", "col"), split_axis=0, concat_axis=0, tiled=True)
+
+    head_high, head_low, head_power = smooth(
+        half_widths,
+        mask[HALF:head_end],
+        centre,
+        [left, right],
+        [],
+        head_span,
+        band_table(head_rows, range(head_span[0][1])),
+        col_band,
+    )
+    plain = stacked(delay_table - exact_dot(mode_delays, plain_fit), 0, per_device)
+    head_delays = delay_chunk(plain, head_high, head_low)
+    head = exchange(head_delays, per_device)
+
+    _, top = lax.optimization_barrier((head_delays, top))
+    tail_in = [r for a, b in tail_spans for r in range(a, b)] + outside(tile_rows)
+    tail_high, tail_low, tail_power = smooth(
+        half_widths,
+        jnp.concatenate([mask[:HALF], mask[head_end:]], axis=0),
+        centre,
+        [left, right],
+        [top, bottom, top_ends, bottom_ends],
+        tail_spans,
+        band_table(tail_rows, tail_in),
+        col_band,
+    )
+
+    power_sum = lax.psum(jnp.sum(head_power + tail_power, axis=1), ("row", "col"))
     weights = 1.0 / (power_sum / (sides * columns) + 1e-05)
     channel_weights = weights / jnp.mean(weights)
     weighted_modes = foreground_modes * weights[None, :]
-    normal_matrix = jnp.dot(
-        weighted_modes, foreground_modes.T, precision=highest, preferred_element_type=jnp.float32
-    )
-    factor = jnp.linalg.cholesky(normal_matrix)
-    solved = jax.scipy.linalg.cho_solve((factor, True), weighted_modes)
-    matrix = delay_table - jnp.dot(
-        mode_delays, solved, precision=highest, preferred_element_type=jnp.float32
-    )
-    matrix_high, matrix_low = split_high_low(matrix)
+    weighted_fit = fit(exact_dot(weighted_modes, modes_t), weighted_modes)
+    change = jnp.concatenate(split_high_low(weighted_fit - plain_fit), axis=0)
+    amplitude = delay_chunk(change, head_high, head_low)
+    amplitude = lax.all_gather(amplitude, ("row", "col"), axis=0, tiled=False)
+    matrix = delay_table - exact_dot(mode_delays, weighted_fit)
+
+    place = lax.axis_index("row") * col_count + lax.axis_index("col")
+    own = lax.dynamic_slice_in_dim(mode_delays, place * 2 * per_device, 2 * per_device, axis=0)
+    head = correct(own, head, amplitude)
 
     cos_c, sin_c = dft_parts(columns)
     col_table = np.block([[cos_c, sin_c], [-sin_c, cos_c]])
     cos_r, sin_r = dft_parts(sides)
+    order = [a * tile_rows + r for a in range(row_count) for r in head_rows + tail_rows]
+    cos_r, sin_r = cos_r[:, order], sin_r[:, order]
     row_table = np.block([[cos_r, -sin_r], [sin_r, cos_r]])
 
-    def send(begin, end, first_row, rows):
-        parts = [
-            x.reshape(peers, per_device, 2, channels)[:, begin:end].reshape(-1, channels)
-            for x in (matrix_high, matrix_low)
-        ]
-        delays = delay_chunk(jnp.concatenate(parts, axis=0), high, low, first_row, rows)
-        return delays.reshape(peers, 2 * (end - begin), rows, tile_cols)
-
-    def exchange(x):
-        return lax.all_to_all(x, ("row", "col"), split_axis=0, concat_axis=0, tiled=True)
-
     shape = (per_device, 2, sides, columns)
-    head = exchange(send(0, per_device, 0, HEAD_ROWS))
-    tail_rows = tile_rows - HEAD_ROWS
     spectrum = None
     start = 0
     for size in chunk_sizes(per_device):
-        tail = exchange(send(start, start + size, HEAD_ROWS, tail_rows))
+        delays = delay_chunk(stacked(matrix, start, start + size), tail_high, tail_low)
+        tail = exchange(delays, size)
         spectrum = spatial_chunk(head, tail, col_table, row_table, shape, start, spectrum)
         start += size
     return (spectrum, channel_weights)

time: 563 us -> 714 us (1.27)
  Pallas kernels: 138 us -> 225 us
  waiting for transfers between devices: 294 us -> 359 us
  local copies, waits for them, and re-layouts: 70.5 us -> 41.2 us
  blocking collectives: 0 us -> 22 us
  between operations: 1.52 us -> 15.1 us
    all_to_all x4 -> x3, waiting for transfers between devices: 283 us -> 30.1 us  [exchange(): lax.all_to_all(delays, ('row', 'col'), split_axis=0, concat_axis=0, tiled...]
    ppermute x6, waiting for transfers between devices: 11.4 us -> 181 us  [shifted(): return pinned(lax.ppermute(pinned(x), axis, pairs))]
    all_gather x0 -> x1, waiting for transfers between devices: none -> 147 us  [tiled_body(): amplitude = lax.all_gather(amplitude, ('row', 'col'), axis=0, tiled=False)]
    pallas_call x1 -> x3, Pallas kernels: 44 us -> 129 us  [the longest x2 110 us: smooth(): pl.pallas_call(functools.partial(smooth_kernel, spans, bool(caps)), grid=...]
    psum x0 -> x1, blocking collectives: none -> 22 us  [tiled_body(): lax.psum(jnp.sum(head_power + tail_power, axis=1), ('row', 'col'))]
    another operation x2 -> x0, local copies, waits for them, and re-layouts: 15.4 us -> none  [pinned(): with_layout_constraint(x, Layout(major_to_minor=tuple(range(x.ndim))))]
    optimization_barrier x2 -> x0, local copies, waits for them, and re-layouts: 9.42 us -> none  [tiled_body(): left, right, centre = lax.optimization_barrier((left, right, centre))]
    pallas_call x3 -> x4, Pallas kernels: 49 us -> 53 us  [delay_chunk(): pl.pallas_call(delay_kernel, grid=(rows // block,), in_specs=[pl.BlockSpe...]
  transfers between devices with their start and end apart: 10 -> 10, of which waited for: 6 -> 6; matrix products, arithmetic and copies ran while one was open for 9% -> 6% of each run, Pallas kernels for 14% -> 21%
where the time goes in v4:
time: 714 us; the launch traced here: 711 us
  waiting for transfers between devices  359 us (50%)
  Pallas kernels  225 us (32%)
  local copies, waits for them, and re-layouts  41.2 us (6%)
  starting transfers between devices  35.1 us (5%)
  blocking collectives  22 us (3%)
  between operations  15.1 us (2%)
  other arithmetic  9.81 us (1%)
    ppermute x6, waiting for transfers between devices, shifted(): return pinned(lax.ppermute(pinned(x), axis, pairs))  181 us
    all_gather x1, waiting for transfers between devices, tiled_body(): amplitude = lax.all_gather(amplitude, ('row', 'col'), axis=0, tiled=False)  147 us
    pallas_call x2, Pallas kernels, smooth(): pl.pallas_call(functools.partial(smooth_kernel, spans, bool(caps)), grid=...  110 us
    pallas_call x4, Pallas kernels, delay_chunk(): pl.pallas_call(delay_kernel, grid=(rows // block,), in_specs=[pl.BlockSpe...  53 us
    pallas_call x2, Pallas kernels, spatial_chunk(): pl.pallas_call(functools.partial(spatial_kernel, row_count, col_count), g...  42.9 us
    all_to_all x3, waiting for transfers between devices, exchange(): lax.all_to_all(delays, ('row', 'col'), split_axis=0, concat_axis=0, tiled...  30.1 us
    optimization_barrier x1, local copies, waits for them, and re-layouts, tiled_body(): lax.optimization_barrier((sky_cube, sky_cube[LAST], sky_cube[FIRST]))  23.5 us
    psum x1, blocking collectives, tiled_body(): lax.psum(jnp.sum(head_power + tail_power, axis=1), ('row', 'col'))  22 us
  transfers between devices with their start and end apart: 10, of which 6 were waited for; matrix products, arithmetic and copies ran while one was open for 6% of the time, Pallas kernels for 21%

profile of v4, /device:TPU:11, one launch (start us, length us, event | category | flops | bytes accessed | tf_op | source)
XLA Modules:
  0.0 711.1 jit_solution(5071292452289306161)
XLA Ops:
  7.2 4.7 fusion.25
  11.8 4.6 fusion.24
  16.4 2.7 collective-permute-start.1
  20.6 23.5 %copy.19 = bf16[128,128,512]{1,0,2:T(8,128)(2,1)} copy(bf16[128,128,512]{2,1,0:T(8,128)(2,1)} %param.13) | data formatting | bytes 33554432 | tf_op jit(solution)/shard_map/optimization_barrier | solution.py:396
  44.3 1.5 cholesky.44
  51.2 50.3 %smooth.2 = (bf16[48,512,128]{2,1,0:T(8,128)(2,1)}, bf16[48,512,128]{2,1,0:T(8,128)(2,1)}, f32[512,128]{1,0:T(8,128)S(1)}) custom-call(s32[512]{0:T(512)S(1)} %copy-done.4, f32[48,128]{1,0:T(8,128)S(1)} %slice.64.mask, bf16[16,48,80]{2,1,0:T(8,128)(2,1)S(1)} %copy-done.6, bf16[64,256,128]{2,1,0:T(8,128)(2,1)} %constant.78.clone.col_band, ...), custom_call_target="tpu_custom_call" | custom-call | flops 34359738368 | bytes 80000000 | tf_op jit(solution)/shard_map/smooth/pallas_call | solution.py:196
  101.6 15.2 %delays.4 = bf16[512,48,128]{2,1,0:T(8,128)(2,1)} custom-call(bf16[1024,512]{1,0:T(8,128)(2,1)S(1)} %pad_maximum_fusion.matrix, bf16[48,512,128]{2,1,0:T(8,128)(2,1)} %get-tuple-element.21.high, bf16[48,512,128]{2,1,0:T(8,128)(2,1)} %get-tuple-element.22.low), custom_call_target="tpu_custom_call" | custom-call | flops 9663676416 | bytes 18874368 | tf_op jit(solution)/shard_map/delays/pallas_call | solution.py:243
  116.8 7.2 %all-to-all-start = ((bf16[16,32,48,128]{3,2,1,0:T(8,128)(2,1)}), bf16[16,32,48,128]{3,2,1,0:T(8,128)(2,1)}, u32[]{:S(2)}, u32[]{:S(2)}) async-start(bf16[16,32,48,128]{3,2,1,0:T(8,128)(2,1)} %bitcast.45), calls=%async_computation | async-start | bytes 12582912 | tf_op jit(solution)/shard_map/all_to_all | solution.py:431
  124.0 3.4 collective-permute-start.2
  127.5 2.3 collective-permute-start.3
  130.9 3.0 collective-permute-start.4
  133.9 2.3 collective-permute-start.5
  136.3 167.9 %collective-permute-done.2.refs_0_ = bf16[16,128,512]{2,1,0:T(8,128)(2,1)S(1)} collective-permute-done((bf16[16,128,512]{2,1,0:T(8,128)(2,1)}, bf16[16,128,512]{2,1,0:T(8,128)(2,1)S(1)}, u32[]{:S(2)}, u32[]{:S(2)}) %collective-permute-start.2) | collective-permute-done | bytes 2097184 | tf_op jit(solution)/shard_map/ppermute | solution.py:362
  304.2 1.9 collective-permute-done.3.refs_1_
  306.1 9.2 %collective-permute-done.4.refs_2_ = bf16[16,32,512]{2,1,0:T(8,128)(2,1)S(1)} collective-permute-done((bf16[16,32,512]{2,1,0:T(8,128)(2,1)S(1)}, bf16[16,32,512]{2,1,0:T(8,128)(2,1)S(1)}, u32[]{:S(2)}, u32[]{:S(2)}) %collective-permute-start.4) | collective-permute-done | bytes 524320 | tf_op jit(solution)/shard_map/ppermute | solution.py:362
  315.3 2.0 collective-permute-done.5.refs_3_
  317.4 59.2 %smooth.3 = (bf16[80,512,128]{2,1,0:T(8,128)(2,1)}, bf16[80,512,128]{2,1,0:T(8,128)(2,1)}, f32[512,128]{1,0:T(8,128)S(1)}) custom-call(s32[512]{0:T(512)S(1)} %copy-done.4, f32[80,128]{1,0:T(8,128)S(1)} %pad_maximum_fusion.5.mask, bf16[16,80,144]{2,1,0:T(8,128)(2,1)S(1)} %copy-done.5, bf16[64,256,128]{2,1,0:T(8,128)(2,1)} %constant.78.clone.col_band, ...), custom_call_target="tpu_custom_call" | custom-call | flops 34359738368 | bytes 80000000 | tf_op jit(solution)/shard_map/smooth/pallas_call | solution.py:196
  376.7 22.0 %psum.7 = f32[512]{0:T(512)S(1)} all-reduce(f32[512]{0:T(512)S(1)} %add_reduce_fusion), channel_id=1, replica_groups=mesh['grp'=2,'row'=4,'col'=4] {'row','col'}, use_global_device_ids=true, to_apply=%region_3.6 | all-reduce | flops 512 | bytes 4096 | tf_op jit(solution)/shard_map/psum | solution.py:460
  399.5 1.5 cholesky.55
  406.8 20.4 %delays.7 = bf16[448,80,128]{2,1,0:T(8,128)(2,1)} custom-call(bf16[896,512]{1,0:T(8,128)(2,1)S(1)} %pad_maximum_fusion.1.matrix, bf16[80,512,128]{2,1,0:T(8,128)(2,1)} %get-tuple-element.28.high, bf16[80,512,128]{2,1,0:T(8,128)(2,1)} %get-tuple-element.29.low), custom_call_target="tpu_custom_call" | custom-call | flops 14092861440 | bytes 30146560 | tf_op jit(solution)/shard_map/delays/pallas_call | solution.py:243
  427.2 7.9 %all-to-all-start.2 = ((bf16[16,28,80,128]{3,2,1,0:T(8,128)(2,1)}), bf16[16,28,80,128]{3,2,1,0:T(8,128)(2,1)}, u32[]{:S(2)}, u32[]{:S(2)}) async-start(bf16[16,28,80,128]{3,2,1,0:T(8,128)(2,1)} %bitcast.44), calls=%async_computation.2 | async-start | bytes 18350080 | tf_op jit(solution)/shard_map/all_to_all | solution.py:431
  435.1 6.7 delays.5
  442.9 10.7 %delays.6 = bf16[64,80,128]{2,1,0:T(8,128)(2,1)} custom-call(bf16[128,512]{1,0:T(8,128)(2,1)S(1)} %pad_maximum_fusion.4.matrix, bf16[80,512,128]{2,1,0:T(8,128)(2,1)} %get-tuple-element.28.high, bf16[80,512,128]{2,1,0:T(8,128)(2,1)} %get-tuple-element.29.low), custom_call_target="tpu_custom_call" | custom-call | flops 2013265920 | bytes 22282240 | tf_op jit(solution)/shard_map/delays/pallas_call | solution.py:243
  454.2 147.4 %all-gather.3.cloned.1.call-done = bf16[256,48,128]{2,1,0:T(8,128)(2,1)} async-done(((bf16[16,48,128]{2,1,0:T(8,128)(2,1)}), bf16[256,48,128]{2,1,0:T(8,128)(2,1)}) %all-gather.3.cloned.1.call-update) | async-done | bytes 3145744 | tf_op jit(solution)/shard_map/all_gather | solution.py:467
  601.6 1.9 copy-done
  603.5 19.7 %correct.1.head = bf16[16,32,48,128]{3,2,1,0:T(8,128)(2,1)} custom-call(f32[32,16]{1,0:T(8,128)S(1)} %copy.21.weights, bf16[16,32,48,128]{3,2,1,0:T(8,128)(2,1)} %all-to-all-done.delays, bf16[16,16,48,128]{3,2,1,0:T(8,128)(2,1)S(1)} %bitcast.41), custom_call_target="tpu_custom_call" | custom-call | flops 100663296 | bytes 12582912 | tf_op jit(solution)/shard_map/correct/pallas_call | solution.py:278
  623.2 30.1 %all-to-all-done.2.tail = bf16[16,28,80,128]{3,2,1,0:T(8,128)(2,1)} async-done(((bf16[16,28,80,128]{3,2,1,0:T(8,128)(2,1)}), bf16[16,28,80,128]{3,2,1,0:T(8,128)(2,1)}, u32[]{:S(2)}, u32[]{:S(2)}) %all-to-all-start.2) | async-done | bytes 9175072 | tf_op jit(solution)/shard_map/all_to_all | solution.py:431
  653.3 4.8 all-to-all-start.1
  658.1 1.6 copy-done.2
  659.7 35.9 %spatial.2.refs_0_ = f32[16,2,512,512]{3,2,1,0:T(8,128)} custom-call(bf16[16,32,48,128]{3,2,1,0:T(8,128)(2,1)} %correct.1.head, bf16[16,28,80,128]{3,2,1,0:T(8,128)(2,1)} %all-to-all-done.2.tail, bf16[1024,1024]{1,0:T(8,128)(2,1)S(1)} %copy-done.2, bf16[1024,1024]{1,0:T(8,128)(2,1)S(1)} %copy-done.1), custom_call_target="tpu_custom_call" | custom-call | flops 30064771072 | bytes 44040192 | tf_op jit(solution)/shard_map/spatial/pallas_call | solution.py:337
  695.6 1.6 copy-done.3
  697.2 7.1 spatial.3
  (77 shorter events, 15.9 us)
Async XLA Ops:
  16.4 34.8 %collective-permute-start.1 = (bf16[128,16,512]{2,1,0:T(8,128)(2,1)}, bf16[128,16,512]{2,1,0:T(8,128)(2,1)S(1)}, u32[]{:S(2)}, u32[]{:S(2)}) collective-permute-start(bf16[128,16,512]{2,1,0:T(8,128)(2,1)} %get-tuple-element.32), channel_id=1, source_target_pairs={{1,0},{2,1},{3,2},{5,4},{6,5},{7,6},{9,8},{10,9},{11,10},{13,12},{... | collective-permute-start | bytes 6291464 | tf_op jit(solution)/shard_map/ppermute | solution.py:362
  19.2 24.9 %copy-start.8 = (f32[16,512]{1,0:T(8,128)S(1)}, f32[16,512]{1,0:T(8,128)}, u32[]{:S(2)}) copy-start(f32[16,512]{1,0:T(8,128)} %param.16) | copy-start | bytes 98308
  19.2 29.2 %copy-start.10 = (s32[128,128]{1,0:T(8,128)S(1)}, s32[128,128]{1,0:T(8,128)}, u32[]{:S(2)}) copy-start(s32[128,128]{1,0:T(8,128)} %param.15) | copy-start | bytes 196612
  19.2 29.8 %copy-start.7 = (f32[512,512]{1,0:T(8,128)S(1)}, f32[512,512]{1,0:T(8,128)}, u32[]{:S(2)}) copy-start(f32[512,512]{1,0:T(8,128)} %constant.76.clone) | copy-start | bytes 3145732
  19.2 32.0 %collective-permute-start = (bf16[128,16,512]{2,1,0:T(8,128)(2,1)}, bf16[128,16,512]{2,1,0:T(8,128)(2,1)}, u32[]{:S(2)}, u32[]{:S(2)}) collective-permute-start(bf16[128,16,512]{2,1,0:T(8,128)(2,1)} %get-tuple-element.33), channel_id=1, source_target_pairs={{0,1},{1,2},{2,3},{4,5},{5,6},{6,7},{8,9},{9,10},{10,11},{12,13},{... | collective-permute-start | bytes 6291464 | tf_op jit(solution)/shard_map/ppermute | solution.py:362
  48.4 0.6 copy-start.9
  50.0 1.2 copy-start.4
  50.0 1.2 copy-start.6
  116.8 310.4 %all-to-all-start = ((bf16[16,32,48,128]{3,2,1,0:T(8,128)(2,1)}), bf16[16,32,48,128]{3,2,1,0:T(8,128)(2,1)}, u32[]{:S(2)}, u32[]{:S(2)}) async-start(bf16[16,32,48,128]{3,2,1,0:T(8,128)(2,1)} %bitcast.45), calls=%async_computation | async-start | bytes 12582912 | tf_op jit(solution)/shard_map/all_to_all | solution.py:431
  124.0 12.3 %slice-start = ((f32[128,128]{1,0:T(8,128)}), f32[16,128]{1,0:T(8,128)S(1)}, s32[]{:S(2)}) async-start(f32[128,128]{1,0:T(8,128)} %copy-done.9), calls=%async_computation.4 | async-start | bytes 16384 | tf_op jit(solution)/shard_map/slice | solution.py:451
  124.0 12.3 %slice-start.1 = ((f32[128,128]{1,0:T(8,128)}), f32[64,128]{1,0:T(8,128)S(1)}, s32[]{:S(2)}) async-start(f32[128,128]{1,0:T(8,128)} %copy-done.9), calls=%async_computation.5 | async-start | bytes 65536 | tf_op jit(solution)/shard_map/slice | solution.py:451
  124.0 193.3 %copy-start.5 = (bf16[16,80,144]{2,1,0:T(8,128)(2,1)S(1)}, bf16[16,80,144]{2,1,0:T(8,128)(2,1)}, u32[]{:S(2)}) copy-start(bf16[16,80,144]{2,1,0:T(8,128)(2,1)} %constant.79.clone.row_band) | copy-start | bytes 1105924
  124.0 180.2 %collective-permute-start.2 = (bf16[16,128,512]{2,1,0:T(8,128)(2,1)}, bf16[16,128,512]{2,1,0:T(8,128)(2,1)S(1)}, u32[]{:S(2)}, u32[]{:S(2)}) collective-permute-start(bf16[16,128,512]{2,1,0:T(8,128)(2,1)} %get-tuple-element.24), channel_id=1, source_target_pairs={{0,4},{4,8},{8,12},{1,5},{5,9},{9,13},{2,6},{6,10},{10,14},{3,7},{... | collective-permute-start | bytes 6291464 | tf_op jit(solution)/shard_map/ppermute | solution.py:362
  127.5 178.7 %collective-permute-start.3 = (bf16[16,128,512]{2,1,0:T(8,128)(2,1)}, bf16[16,128,512]{2,1,0:T(8,128)(2,1)S(1)}, u32[]{:S(2)}, u32[]{:S(2)}) collective-permute-start(bf16[16,128,512]{2,1,0:T(8,128)(2,1)} %get-tuple-element.26), channel_id=1, source_target_pairs={{4,0},{8,4},{12,8},{5,1},{9,5},{13,9},{6,2},{10,6},{14,10},{7,3},{... | collective-permute-start | bytes 6291464 | tf_op jit(solution)/shard_map/ppermute | solution.py:362
  130.9 184.4 %collective-permute-start.4 = (bf16[16,32,512]{2,1,0:T(8,128)(2,1)S(1)}, bf16[16,32,512]{2,1,0:T(8,128)(2,1)S(1)}, u32[]{:S(2)}, u32[]{:S(2)}) collective-permute-start(bf16[16,32,512]{2,1,0:T(8,128)(2,1)S(1)} %pad_maximum_fusion.2), channel_id=1, source_target_pairs={{0,4},{4,8},{8,12},{1,5},{5,9},{9,13},{2,6},{6,10},{10,14},{3,7},{... | collective-permute-start | bytes 1572872 | tf_op jit(solution)/shard_map/ppermute | solution.py:362
  133.9 183.4 %collective-permute-start.5 = (bf16[16,32,512]{2,1,0:T(8,128)(2,1)S(1)}, bf16[16,32,512]{2,1,0:T(8,128)(2,1)S(1)}, u32[]{:S(2)}, u32[]{:S(2)}) collective-permute-start(bf16[16,32,512]{2,1,0:T(8,128)(2,1)S(1)} %pad_maximum_fusion.3), channel_id=1, source_target_pairs={{4,0},{8,4},{12,8},{5,1},{9,5},{13,9},{6,2},{10,6},{14,10},{7,3},{... | collective-permute-start | bytes 1572872 | tf_op jit(solution)/shard_map/ppermute | solution.py:362
  304.2 13.1 %copy-start.11 = (bf16[16,128,512]{2,1,0:T(8,128)(2,1)}, bf16[16,128,512]{2,1,0:T(8,128)(2,1)S(1)}, u32[]{:S(2)}) copy-start(bf16[16,128,512]{2,1,0:T(8,128)(2,1)S(1)} %collective-permute-done.2.refs_0_) | copy-start | bytes 6291460
  306.1 11.2 %copy-start.12 = (bf16[16,128,512]{2,1,0:T(8,128)(2,1)}, bf16[16,128,512]{2,1,0:T(8,128)(2,1)S(1)}, u32[]{:S(2)}) copy-start(bf16[16,128,512]{2,1,0:T(8,128)(2,1)S(1)} %collective-permute-done.3.refs_1_) | copy-start | bytes 6291460
  427.2 226.1 %all-to-all-start.2 = ((bf16[16,28,80,128]{3,2,1,0:T(8,128)(2,1)}), bf16[16,28,80,128]{3,2,1,0:T(8,128)(2,1)}, u32[]{:S(2)}, u32[]{:S(2)}) async-start(bf16[16,28,80,128]{3,2,1,0:T(8,128)(2,1)} %bitcast.44), calls=%async_computation.2 | async-start | bytes 18350080 | tf_op jit(solution)/shard_map/all_to_all | solution.py:431
  435.1 166.5 %all-gather.3.cloned.1.call-start = ((), (), s32[]{:S(2)}) async-start(), calls=%async_computation.3 | async-start | bytes 3342336 | tf_op jit(solution)/shard_map/all_gather | solution.py:467
  601.6 1.9 copy-start
  623.2 35.0 %copy-start.1 = (bf16[1024,1024]{1,0:T(8,128)(2,1)S(1)}, bf16[1024,1024]{1,0:T(8,128)(2,1)}, u32[]{:S(2)}) copy-start(bf16[1024,1024]{1,0:T(8,128)(2,1)} %constant.81.clone.row_table) | copy-start | bytes 6291460
  653.3 42.3 %all-to-all-start.1 = ((bf16[16,4,80,128]{3,2,1,0:T(8,128)(2,1)}), bf16[16,4,80,128]{3,2,1,0:T(8,128)(2,1)S(1)}, u32[]{:S(2)}, u32[]{:S(2)}) async-start(bf16[16,4,80,128]{3,2,1,0:T(8,128)(2,1)} %bitcast.9), calls=%async_computation.1 | async-start | bytes 2621440 | tf_op jit(solution)/shard_map/all_to_all | solution.py:431
  658.1 1.6 copy-start.2
  695.6 1.6 copy-start.3
Sparse Core Ops, SparseCore 0:
  442.0 159.5 all-gather.2

commit v5 on v4

--- a/solution.py
+++ b/solution.py
@@ -114,20 +114,19 @@
 def smooth_kernel(spans, capped, widths, mask, row_band, col_band, centre, left, right, *refs):
     if capped:
         top, bottom, top_ends, bottom_ends, *refs = refs
-        high, low, power, staged, sides, caps, corners = refs
+        high, low, power, staged, caps, corners = refs
     else:
-        high, low, power, staged, sides = refs
+        high, low, power, staged = refs
     block = centre.shape[0]
     outputs, columns = mask.shape
-    rows = sides.shape[2]
+    rows = left.shape[2]
     step = pl.program_id(0)
     per_turn = LANES // block
 
-    @pl.when(step % per_turn == 0)
-    def _():
-        sides[:, FIRST] = jnp.transpose(left[...], (2, 1, 0))
-        sides[:, HALF : 2 * HALF] = jnp.transpose(right[...], (2, 1, 0))
-        if capped:
+    if capped:
+
+        @pl.when(step % per_turn == 0)
+        def _():
             caps[:, FIRST] = jnp.transpose(top[...], (2, 0, 1))
             caps[:, HALF : 2 * HALF] = jnp.transpose(bottom[...], (2, 0, 1))
             corners[:, FIRST] = jnp.transpose(top_ends[...], (2, 0, 1))
@@ -139,7 +138,9 @@
     done = []
     for group in range(0, block, PACK):
         members = range(group, group + PACK)
-        flank = sides[pl.ds(lane + group, PACK)].reshape(PACK * 2 * HALF, rows).T
+        chosen = pl.ds(group, PACK)
+        flank = jnp.concatenate([left[chosen], right[chosen]], axis=1)
+        flank = flank.reshape(PACK * 2 * HALF, rows).T
         flank = [flank[a:b] for a, b in spans]
         if capped:
             corner = [corners[lane + j] for j in members]
@@ -184,10 +185,7 @@
     split_spec = pl.BlockSpec((outputs, block, columns), lambda i: (0, i, 0))
     split_shape = jax.ShapeDtypeStruct((outputs, channels, columns), jnp.bfloat16)
     tables = [mask, row_band, col_band]
-    scratch = [
-        pltpu.VMEM((outputs, block, columns), jnp.float32),
-        pltpu.VMEM((LANES, 2 * HALF, tile_rows), jnp.bfloat16),
-    ]
+    scratch = [pltpu.VMEM((outputs, block, columns), jnp.float32)]
     if caps:
         scratch += [
             pltpu.VMEM((LANES, 2 * HALF, columns), jnp.bfloat16),
@@ -198,8 +196,8 @@
         grid=(channels // block,),
         in_specs=[pl.BlockSpec(memory_space=pltpu.SMEM)]
         + [whole(t.shape) for t in tables]
-        + [pl.BlockSpec((block, tile_rows, columns), lambda i: (i, 0, 0))]
-        + [halo(x) for x in sides + caps],
+        + [pl.BlockSpec((block,) + x.shape[1:], lambda i: (i, 0, 0)) for x in [centre] + sides]
+        + [halo(x) for x in caps],
         out_specs=[split_spec, split_spec, pl.BlockSpec((block, columns), lambda i: (i, 0))],
         out_shape=[
             split_shape,
@@ -362,6 +360,20 @@
     return pinned(lax.ppermute(pinned(x), axis, pairs))
 
 
+def gathered(x):
+    shape = x.shape
+    bits = 0
+    for axis in ("row", "col"):
+        size = lax.axis_size(axis)
+        for bit in reversed(range(size.bit_length() - 1)):
+            other = pinned(lax.ppermute(x, axis, [(i, i ^ (1 << bit)) for i in range(size)]))
+            upper = (lax.axis_index(axis) >> bit) % 2 == 1
+            pair = [jnp.where(upper, other, x), jnp.where(upper, x, other)]
+            x = jnp.stack(pair, axis=bits)
+            bits += 1
+    return x.reshape((-1,) + shape)
+
+
 def outside(length):
     return [*range(-HALF, 0), *range(length, length + HALF)]
 
@@ -417,6 +429,9 @@
     head_span = ((0, head_end + HALF),)
     tail_spans = ((0, 2 * HALF), (HEAD_ROWS, tile_rows))
 
+    sides_t = [jnp.transpose(x, (2, 1, 0)) for x in (left, right)]
+    sides_t[0], top, bottom = lax.optimization_barrier((sides_t[0], top, bottom))
+
     modes_t = foreground_modes.T
     delay_table = delay_rows(channels, peers, [per_device])
     mode_delays = exact_dot(delay_table, modes_t)
@@ -434,7 +449,7 @@
         half_widths,
         mask[HALF:head_end],
         centre,
-        [left, right],
+        sides_t,
         [],
         head_span,
         band_table(head_rows, range(head_span[0][1])),
@@ -442,15 +457,15 @@
     )
     plain = stacked(delay_table - exact_dot(mode_delays, plain_fit), 0, per_device)
     head_delays = delay_chunk(plain, head_high, head_low)
+    head_delays, *ends = lax.optimization_barrier((head_delays, top_ends, bottom_ends))
     head = exchange(head_delays, per_device)
-
-    _, top = lax.optimization_barrier((head_delays, top))
+    top_ends, bottom_ends = ends
     tail_in = [r for a, b in tail_spans for r in range(a, b)] + outside(tile_rows)
     tail_high, tail_low, tail_power = smooth(
         half_widths,
         jnp.concatenate([mask[:HALF], mask[head_end:]], axis=0),
         centre,
-        [left, right],
+        sides_t,
         [top, bottom, top_ends, bottom_ends],
         tail_spans,
         band_table(tail_rows, tail_in),
@@ -464,7 +479,7 @@
     weighted_fit = fit(exact_dot(weighted_modes, modes_t), weighted_modes)
     change = jnp.concatenate(split_high_low(weighted_fit - plain_fit), axis=0)
     amplitude = delay_chunk(change, head_high, head_low)
-    amplitude = lax.all_gather(amplitude, ("row", "col"), axis=0, tiled=False)
+    amplitude = gathered(amplitude)
     matrix = delay_table - exact_dot(mode_delays, weighted_fit)
 
     place = lax.axis_index("row") * col_count + lax.axis_index("col")
@@ -556,6 +571,8 @@
 def body(sky_cube, half_widths, pixel_mask, foreground_modes):
     tile_rows, tile_cols, channels = sky_cube.shape
     fits = tile_rows % 128 == 0 and tile_cols % 128 == 0 and channels % 128 == 0
+    for axis in ("row", "col"):
+        fits = fits and lax.axis_size(axis) & (lax.axis_size(axis) - 1) == 0
     run = tiled_body if fits else small_tile_body
     return run(sky_cube, half_widths, pixel_mask, foreground_modes)
 

time: 714 us -> 646 us (0.905)
  waiting for transfers between devices: 359 us -> 226 us
  blocking collectives: 22 us -> 110 us
  Pallas kernels: 225 us -> 186 us
  local copies, waits for them, and re-layouts: 41.2 us -> 55.8 us
  between operations: 15.1 us -> 1.71 us
  starting transfers between devices: 35.1 us -> 43.7 us
    ppermute x0 -> x4, waiting for transfers between devices: none -> 223 us  [gathered(): lax.ppermute(x, axis, [(i, i ^ 1 << bit) for i in range(size)])]
    ppermute x6, waiting for transfers between devices: 181 us -> 3.05 us  [shifted(): return pinned(lax.ppermute(pinned(x), axis, pairs))]
    all_gather x1 -> x0, waiting for transfers between devices: 147 us -> none  [tiled_body(): amplitude = lax.all_gather(amplitude, ('row', 'col'), axis=0, tiled=False)]
    psum x1, blocking collectives: 22 us -> 110 us  [tiled_body(): lax.psum(jnp.sum(head_power + tail_power, axis=1), ('row', 'col'))]
    pallas_call x2, Pallas kernels: 110 us -> 71 us  [smooth(): pl.pallas_call(functools.partial(smooth_kernel, spans, bool(caps)), grid=...]
    all_to_all x3, waiting for transfers between devices: 30.1 us -> 0.01 us  [exchange(): lax.all_to_all(delays, ('row', 'col'), split_axis=0, concat_axis=0, tiled...]
    optimization_barrier x0 -> x2, local copies, waits for them, and re-layouts: none -> 9.35 us  [tiled_body(): left, right, centre = lax.optimization_barrier((left, right, centre))]
    ppermute x0 -> x4, starting transfers between devices: none -> 7.86 us  [gathered(): lax.ppermute(x, axis, [(i, i ^ 1 << bit) for i in range(size)])]
  transfers between devices with their start and end apart: 10 -> 13, of which waited for: 6 -> 5; matrix products, arithmetic and copies ran while one was open for 6% -> 9% of each run, Pallas kernels for 21% -> 28%
where the time goes in v5:
time: 646 us; the launch traced here: 643 us
  waiting for transfers between devices  226 us (35%)
  Pallas kernels  186 us (29%)
  blocking collectives  110 us (17%)
  local copies, waits for them, and re-layouts  55.8 us (9%)
  starting transfers between devices  43.7 us (7%)
  other arithmetic  14.5 us (2%)
    ppermute x4, waiting for transfers between devices, gathered(): lax.ppermute(x, axis, [(i, i ^ 1 << bit) for i in range(size)])  223 us
    psum x1, blocking collectives, tiled_body(): lax.psum(jnp.sum(head_power + tail_power, axis=1), ('row', 'col'))  110 us
    pallas_call x2, Pallas kernels, smooth(): pl.pallas_call(functools.partial(smooth_kernel, spans, bool(caps)), grid=...  71 us
    pallas_call x4, Pallas kernels, delay_chunk(): pl.pallas_call(delay_kernel, grid=(rows // block,), in_specs=[pl.BlockSpe...  52.3 us
    pallas_call x2, Pallas kernels, spatial_chunk(): pl.pallas_call(functools.partial(spatial_kernel, row_count, col_count), g...  42.9 us
    optimization_barrier x1, local copies, waits for them, and re-layouts, tiled_body(): lax.optimization_barrier((sky_cube, sky_cube[LAST], sky_cube[FIRST]))  23.6 us
    pallas_call x1, Pallas kernels, correct(): pl.pallas_call(correct_kernel, grid=(peers,), in_specs=[pl.BlockSpec(memo...  19.7 us
    all_to_all x3, starting transfers between devices, exchange(): lax.all_to_all(delays, ('row', 'col'), split_axis=0, concat_axis=0, tiled...  18.7 us
  transfers between devices with their start and end apart: 13, of which 5 were waited for; matrix products, arithmetic and copies ran while one was open for 9% of the time, Pallas kernels for 28%

profile of v5, /device:TPU:11, one launch (start us, length us, event | category | flops | bytes accessed | tf_op | source)
XLA Modules:
  0.0 643.3 jit_solution(13608381162295026025)
XLA Ops:
  0.6 4.6 fusion.25
  5.3 4.7 fusion.24
  9.9 3.9 collective-permute-start.1
  15.2 3.2 collective-permute-start.2
  18.4 3.4 collective-permute-start.3
  22.0 23.6 %copy.15 = bf16[128,128,512]{1,0,2:T(8,128)(2,1)} copy(bf16[128,128,512]{2,1,0:T(8,128)(2,1)} %param.13) | data formatting | bytes 33554432 | tf_op jit(solution)/shard_map/optimization_barrier | solution.py:408
  52.5 4.2 copy.17
  56.7 5.1 copy.16
  63.4 2.9 collective-permute-done.3.refs_1_
  66.3 3.2 collective-permute-start.4
  69.6 2.1 collective-permute-start.5
  71.7 30.8 %smooth.2 = (bf16[48,512,128]{2,1,0:T(8,128)(2,1)}, bf16[48,512,128]{2,1,0:T(8,128)(2,1)}, f32[512,128]{1,0:T(8,128)S(1)}) custom-call(s32[512]{0:T(512)S(1)} %copy-done.9, f32[48,128]{1,0:T(8,128)S(1)} %slice.64.mask, bf16[16,48,80]{2,1,0:T(8,128)(2,1)S(1)} %copy-done.11, bf16[64,256,128]{2,1,0:T(8,128)(2,1)} %constant.102.clone.col_band, ...), custom_call_target="tpu_custom_call" | custom-call | flops 34359738368 | bytes 80000000 | tf_op jit(solution)/shard_map/smooth/pallas_call | solution.py:194
  102.5 15.3 %delays.4 = bf16[512,48,128]{2,1,0:T(8,128)(2,1)} custom-call(bf16[1024,512]{1,0:T(8,128)(2,1)S(1)} %pad_maximum_fusion.2.matrix, bf16[48,512,128]{2,1,0:T(8,128)(2,1)} %get-tuple-element.29.high, bf16[48,512,128]{2,1,0:T(8,128)(2,1)} %get-tuple-element.30.low), custom_call_target="tpu_custom_call" | custom-call | flops 9663676416 | bytes 18874368 | tf_op jit(solution)/shard_map/delays/pallas_call | solution.py:241
  119.5 7.9 %all-to-all-start = ((bf16[16,32,48,128]{3,2,1,0:T(8,128)(2,1)}), bf16[16,32,48,128]{3,2,1,0:T(8,128)(2,1)}, u32[]{:S(2)}, u32[]{:S(2)}) async-start(bf16[16,32,48,128]{3,2,1,0:T(8,128)(2,1)} %bitcast.71), calls=%async_computation | async-start | bytes 12582912 | tf_op jit(solution)/shard_map/all_to_all | solution.py:446
  131.1 40.2 %smooth.3 = (bf16[80,512,128]{2,1,0:T(8,128)(2,1)}, bf16[80,512,128]{2,1,0:T(8,128)(2,1)}, f32[512,128]{1,0:T(8,128)S(1)}) custom-call(s32[512]{0:T(512)S(1)} %copy-done.9, f32[80,128]{1,0:T(8,128)S(1)} %pad_maximum_fusion.9.mask, bf16[16,80,144]{2,1,0:T(8,128)(2,1)S(1)} %copy-done.10, bf16[64,256,128]{2,1,0:T(8,128)(2,1)} %constant.102.clone.col_band, ...), custom_call_target="tpu_custom_call" | custom-call | flops 34359738368 | bytes 80000000 | tf_op jit(solution)/shard_map/smooth/pallas_call | solution.py:194
  171.5 109.9 %psum.7 = f32[512]{0:T(512)S(1)} all-reduce(f32[512]{0:T(512)S(1)} %add_reduce_fusion), channel_id=1, replica_groups=mesh['grp'=2,'row'=4,'col'=4] {'row','col'}, use_global_device_ids=true, to_apply=%region_3.6 | all-reduce | flops 512 | bytes 4096 | tf_op jit(solution)/shard_map/psum | solution.py:475
  286.7 2.3 convolution_subtract_fusion
  290.8 20.4 %delays.7 = bf16[448,80,128]{2,1,0:T(8,128)(2,1)} custom-call(bf16[896,512]{1,0:T(8,128)(2,1)S(1)} %pad_maximum_fusion.3.matrix, bf16[80,512,128]{2,1,0:T(8,128)(2,1)} %get-tuple-element.38.high, bf16[80,512,128]{2,1,0:T(8,128)(2,1)} %get-tuple-element.39.low), custom_call_target="tpu_custom_call" | custom-call | flops 14092861440 | bytes 30146560 | tf_op jit(solution)/shard_map/delays/pallas_call | solution.py:241
  311.1 6.0 all-to-all-start.2
  317.1 6.1 delays.5
  323.2 2.2 collective-permute-start.6
  325.3 197.1 %collective-permute-done.6 = bf16[16,48,128]{2,1,0:T(8,128)(2,1)S(1)} collective-permute-done((bf16[16,48,128]{2,1,0:T(8,128)(2,1)S(1)}, bf16[16,48,128]{2,1,0:T(8,128)(2,1)S(1)}, u32[]{:S(2)}, u32[]{:S(2)}) %collective-permute-start.6) | collective-permute-done | bytes 196640 | tf_op jit(solution)/shard_map/ppermute | solution.py:369
  522.5 3.3 collective-permute-start.7
  525.8 8.6 %collective-permute-done.7 = bf16[2,16,48,128]{3,2,1,0:T(8,128)(2,1)S(1)} collective-permute-done((bf16[2,16,48,128]{3,2,1,0:T(8,128)(2,1)S(1)}, bf16[2,16,48,128]{3,2,1,0:T(8,128)(2,1)S(1)}, u32[]{:S(2)}, u32[]{:S(2)}) %collective-permute-start.7) | collective-permute-done | bytes 393248 | tf_op jit(solution)/shard_map/ppermute | solution.py:369
  534.6 17.7 %collective-permute-done.8 = bf16[2,2,16,48,128]{4,3,2,1,0:T(8,128)(2,1)} collective-permute-done((bf16[2,2,16,48,128]{4,3,2,1,0:T(8,128)(2,1)S(1)}, bf16[2,2,16,48,128]{4,3,2,1,0:T(8,128)(2,1)}, u32[]{:S(2)}, u32[]{:S(2)}) %collective-permute-start.8) | collective-permute-done | bytes 786464 | tf_op jit(solution)/shard_map/ppermute | solution.py:369
  554.9 2.4 collective-permute-start.9
  558.9 10.5 %delays.6 = bf16[64,80,128]{2,1,0:T(8,128)(2,1)} custom-call(bf16[128,512]{1,0:T(8,128)(2,1)S(1)} %pad_maximum_fusion.8.matrix, bf16[80,512,128]{2,1,0:T(8,128)(2,1)} %get-tuple-element.38.high, bf16[80,512,128]{2,1,0:T(8,128)(2,1)} %get-tuple-element.39.low), custom_call_target="tpu_custom_call" | custom-call | flops 2013265920 | bytes 22282240 | tf_op jit(solution)/shard_map/delays/pallas_call | solution.py:241
  569.9 1.6 select_bitcast_fusion.1
  572.6 19.7 %correct.1.head = bf16[16,32,48,128]{3,2,1,0:T(8,128)(2,1)} custom-call(f32[32,16]{1,0:T(8,128)S(1)} %copy.22.weights, bf16[16,32,48,128]{3,2,1,0:T(8,128)(2,1)} %all-to-all-done.delays, bf16[16,16,48,128]{3,2,1,0:T(8,128)(2,1)S(1)} %bitcast.63), custom_call_target="tpu_custom_call" | custom-call | flops 100663296 | bytes 12582912 | tf_op jit(solution)/shard_map/correct/pallas_call | solution.py:276
  592.3 4.9 all-to-all-start.1
  598.8 35.9 %spatial.2.refs_0_ = f32[16,2,512,512]{3,2,1,0:T(8,128)} custom-call(bf16[16,32,48,128]{3,2,1,0:T(8,128)(2,1)} %correct.1.head, bf16[16,28,80,128]{3,2,1,0:T(8,128)(2,1)} %all-to-all-done.2.tail, bf16[1024,1024]{1,0:T(8,128)(2,1)S(1)} %copy-done.1, bf16[1024,1024]{1,0:T(8,128)(2,1)S(1)} %copy-done), custom_call_target="tpu_custom_call" | custom-call | flops 30064771072 | bytes 44040192 | tf_op jit(solution)/shard_map/spatial/pallas_call | solution.py:335
  636.2 7.1 %spatial.3 = f32[16,2,512,512]{3,2,1,0:T(8,128)} custom-call(bf16[16,32,48,128]{3,2,1,0:T(8,128)(2,1)} %correct.1.head, bf16[16,4,80,128]{3,2,1,0:T(8,128)(2,1)S(1)} %all-to-all-done.1.tail, bf16[1024,1024]{1,0:T(8,128)(2,1)S(1)} %copy-done.2, bf16[1024,1024]{1,0:T(8,128)(2,1)S(1)} %copy-done, ...), custom_call_target="tpu_custom_call", output_to_operand_aliasing={{}: (4, {})} | custom-call | flops 4294967296 | bytes 6291456 | tf_op jit(solution)/shard_map/spatial/pallas_call | solution.py:335
  (105 shorter events, 31.1 us)
Async XLA Ops:
  5.2 16.6 %copy-start.13 = (f32[16,512]{1,0:T(8,128)S(1)}, f32[16,512]{1,0:T(8,128)}, u32[]{:S(2)}) copy-start(f32[16,512]{1,0:T(8,128)} %param.16) | copy-start | bytes 98308
  9.9 42.5 %collective-permute-start.1 = (bf16[128,16,512]{2,1,0:T(8,128)(2,1)}, bf16[128,16,512]{2,1,0:T(8,128)(2,1)}, u32[]{:S(2)}, u32[]{:S(2)}) collective-permute-start(bf16[128,16,512]{2,1,0:T(8,128)(2,1)} %get-tuple-element.42), channel_id=1, source_target_pairs={{1,0},{2,1},{3,2},{5,4},{6,5},{7,6},{9,8},{10,9},{11,10},{13,12},{... | collective-permute-start | bytes 6291464 | tf_op jit(solution)/shard_map/ppermute | solution.py:360
  13.9 38.6 %collective-permute-start = (bf16[128,16,512]{2,1,0:T(8,128)(2,1)}, bf16[128,16,512]{2,1,0:T(8,128)(2,1)}, u32[]{:S(2)}, u32[]{:S(2)}) collective-permute-start(bf16[128,16,512]{2,1,0:T(8,128)(2,1)} %get-tuple-element.43), channel_id=1, source_target_pairs={{0,1},{1,2},{2,3},{4,5},{5,6},{6,7},{8,9},{9,10},{10,11},{12,13},{... | collective-permute-start | bytes 6291464 | tf_op jit(solution)/shard_map/ppermute | solution.py:360
  15.2 48.2 %collective-permute-start.2 = (bf16[16,128,512]{2,1,0:T(8,128)(2,1)}, bf16[16,128,512]{2,1,0:T(8,128)(2,1)}, u32[]{:S(2)}, u32[]{:S(2)}) collective-permute-start(bf16[16,128,512]{2,1,0:T(8,128)(2,1)} %get-tuple-element.25), channel_id=1, source_target_pairs={{0,4},{4,8},{8,12},{1,5},{5,9},{9,13},{2,6},{6,10},{10,14},{3,7},{... | collective-permute-start | bytes 6291464 | tf_op jit(solution)/shard_map/ppermute | solution.py:360
  18.4 47.9 %collective-permute-start.3 = (bf16[16,128,512]{2,1,0:T(8,128)(2,1)}, bf16[16,128,512]{2,1,0:T(8,128)(2,1)}, u32[]{:S(2)}, u32[]{:S(2)}) collective-permute-start(bf16[16,128,512]{2,1,0:T(8,128)(2,1)} %get-tuple-element.26), channel_id=1, source_target_pairs={{4,0},{8,4},{12,8},{5,1},{9,5},{13,9},{6,2},{10,6},{14,10},{7,3},{... | collective-permute-start | bytes 6291464 | tf_op jit(solution)/shard_map/ppermute | solution.py:360
  22.0 27.7 %copy-start.16 = (s32[128,128]{1,0:T(8,128)S(1)}, s32[128,128]{1,0:T(8,128)}, u32[]{:S(2)}) copy-start(s32[128,128]{1,0:T(8,128)} %param.15) | copy-start | bytes 196612
  22.0 28.3 %copy-start.12 = (f32[512,512]{1,0:T(8,128)S(1)}, f32[512,512]{1,0:T(8,128)}, u32[]{:S(2)}) copy-start(f32[512,512]{1,0:T(8,128)} %constant.100.clone) | copy-start | bytes 3145732
  51.3 235.4 %copy-start.14 = (f32[512,16]{0,1:T(8,128)}, f32[512,16]{0,1:T(8,128)S(1)}, u32[]{:S(2)}) copy-start(f32[512,16]{0,1:T(8,128)S(1)} %fusion.28) | copy-start | bytes 98308
  61.8 9.9 %copy-start.3 = (bf16[128,16,512]{0,1,2:T(8,128)(2,1)S(1)}, bf16[128,16,512]{0,1,2:T(8,128)(2,1)}, u32[]{:S(2)}) copy-start(bf16[128,16,512]{0,1,2:T(8,128)(2,1)} %copy.16) | copy-start | bytes 6291460
  61.8 9.9 %copy-start.9 = (s32[512]{0:T(512)S(1)}, s32[512]{0:T(512)}, u32[]{:S(2)}) copy-start(s32[512]{0:T(512)} %widths.3) | copy-start | bytes 6148
  61.9 9.9 %copy-start.11 = (bf16[16,48,80]{2,1,0:T(8,128)(2,1)S(1)}, bf16[16,48,80]{2,1,0:T(8,128)(2,1)}, u32[]{:S(2)}) copy-start(bf16[16,48,80]{2,1,0:T(8,128)(2,1)} %constant.101.clone.row_band) | copy-start | bytes 368644
  66.3 51.5 %collective-permute-start.4 = (bf16[16,32,512]{2,1,0:T(8,128)(2,1)S(1)}, bf16[16,32,512]{2,1,0:T(8,128)(2,1)S(1)}, u32[]{:S(2)}, u32[]{:S(2)}) collective-permute-start(bf16[16,32,512]{2,1,0:T(8,128)(2,1)S(1)} %pad_maximum_fusion.5), channel_id=1, source_target_pairs={{0,4},{4,8},{8,12},{1,5},{5,9},{9,13},{2,6},{6,10},{10,14},{3,7},{... | collective-permute-start | bytes 1572872 | tf_op jit(solution)/shard_map/ppermute | solution.py:360
  69.6 49.1 %collective-permute-start.5 = (bf16[16,32,512]{2,1,0:T(8,128)(2,1)S(1)}, bf16[16,32,512]{2,1,0:T(8,128)(2,1)S(1)}, u32[]{:S(2)}, u32[]{:S(2)}) collective-permute-start(bf16[16,32,512]{2,1,0:T(8,128)(2,1)S(1)} %pad_maximum_fusion.6), channel_id=1, source_target_pairs={{4,0},{8,4},{12,8},{5,1},{9,5},{13,9},{6,2},{10,6},{14,10},{7,3},{... | collective-permute-start | bytes 1572872 | tf_op jit(solution)/shard_map/ppermute | solution.py:360
  117.8 0.8 copy-start.5
  118.7 0.8 copy-start.7
  119.5 7.9 %slice-start = ((f32[128,128]{1,0:T(8,128)}), f32[16,128]{1,0:T(8,128)S(1)}, s32[]{:S(2)}) async-start(f32[128,128]{1,0:T(8,128)} %copy-done.15), calls=%async_computation.3 | async-start | bytes 16384 | tf_op jit(solution)/shard_map/slice | solution.py:466
  119.5 7.9 %slice-start.1 = ((f32[128,128]{1,0:T(8,128)}), f32[64,128]{1,0:T(8,128)S(1)}, s32[]{:S(2)}) async-start(f32[128,128]{1,0:T(8,128)} %copy-done.15), calls=%async_computation.4 | async-start | bytes 65536 | tf_op jit(solution)/shard_map/slice | solution.py:466
  119.5 7.9 %copy-start.6 = (bf16[16,32,512]{2,1,0:T(8,128)(2,1)S(1)}, bf16[16,32,512]{2,1,0:T(8,128)(2,1)}, u32[]{:S(2)}) copy-start(bf16[16,32,512]{2,1,0:T(8,128)(2,1)} %copy-done.5) | copy-start | bytes 1572868
  119.5 191.6 %all-to-all-start = ((bf16[16,32,48,128]{3,2,1,0:T(8,128)(2,1)}), bf16[16,32,48,128]{3,2,1,0:T(8,128)(2,1)}, u32[]{:S(2)}, u32[]{:S(2)}) async-start(bf16[16,32,48,128]{3,2,1,0:T(8,128)(2,1)} %bitcast.71), calls=%async_computation | async-start | bytes 12582912 | tf_op jit(solution)/shard_map/all_to_all | solution.py:446
  127.4 1.6 copy-start.4
  129.0 1.0 copy-start.8
  130.0 1.1 copy-start.10
  311.1 281.1 %all-to-all-start.2 = ((bf16[16,28,80,128]{3,2,1,0:T(8,128)(2,1)}), bf16[16,28,80,128]{3,2,1,0:T(8,128)(2,1)}, u32[]{:S(2)}, u32[]{:S(2)}) async-start(bf16[16,28,80,128]{3,2,1,0:T(8,128)(2,1)} %bitcast.70), calls=%async_computation.2 | async-start | bytes 18350080 | tf_op jit(solution)/shard_map/all_to_all | solution.py:446
  323.2 199.2 %collective-permute-start.6 = (bf16[16,48,128]{2,1,0:T(8,128)(2,1)S(1)}, bf16[16,48,128]{2,1,0:T(8,128)(2,1)S(1)}, u32[]{:S(2)}, u32[]{:S(2)}) collective-permute-start(bf16[16,48,128]{2,1,0:T(8,128)(2,1)S(1)} %delays.5), channel_id=1, source_target_pairs={{0,8},{4,12},{8,0},{12,4},{1,9},{5,13},{9,1},{13,5},{2,10},{6,14},... | collective-permute-start | bytes 589832 | tf_op jit(solution)/shard_map/ppermute | solution.py:369
  522.5 11.9 %collective-permute-start.7 = (bf16[2,16,48,128]{3,2,1,0:T(8,128)(2,1)S(1)}, bf16[2,16,48,128]{3,2,1,0:T(8,128)(2,1)S(1)}, u32[]{:S(2)}, u32[]{:S(2)}) collective-permute-start(bf16[2,16,48,128]{3,2,1,0:T(8,128)(2,1)S(1)} %pad_maximum_fusion.7), channel_id=1, source_target_pairs={{0,4},{4,0},{8,12},{12,8},{1,5},{5,1},{9,13},{13,9},{2,6},{6,2},{1... | collective-permute-start | bytes 1179656 | tf_op jit(solution)/shard_map/ppermute | solution.py:369
  534.5 17.8 %collective-permute-start.8 = (bf16[2,2,16,48,128]{4,3,2,1,0:T(8,128)(2,1)S(1)}, bf16[2,2,16,48,128]{4,3,2,1,0:T(8,128)(2,1)}, u32[]{:S(2)}, u32[]{:S(2)}) collective-permute-start(bf16[2,2,16,48,128]{4,3,2,1,0:T(8,128)(2,1)S(1)} %pad_maximum_fusion.4), channel_id=1, source_target_pairs={{0,2},{1,3},{2,0},{3,1},{4,6},{5,7},{6,4},{7,5},{8,10},{9,11},{10,... | collective-permute-start | bytes 2359304 | tf_op jit(solution)/shard_map/ppermute | solution.py:369
  554.9 15.1 %collective-permute-start.9 = (bf16[2,2,2,16,48,128]{5,4,3,2,1,0:T(8,128)(2,1)}, bf16[2,2,2,16,48,128]{5,4,3,2,1,0:T(8,128)(2,1)}, u32[]{:S(2)}, u32[]{:S(2)}) collective-permute-start(bf16[2,2,2,16,48,128]{5,4,3,2,1,0:T(8,128)(2,1)} %pad_maximum_fusion.1), channel_id=1, source_target_pairs={{0,1},{1,0},{2,3},{3,2},{4,5},{5,4},{6,7},{7,6},{8,9},{9,8},{10,11... | collective-permute-start | bytes 4718600 | tf_op jit(solution)/shard_map/ppermute | solution.py:369
  558.9 10.5 %copy-start.18 = (f32[512]{0:T(512)S(1)}, f32[512]{0:T(512)}, u32[]{:S(2)}) copy-start(f32[512]{0:T(512)} %copy-done.17) | copy-start | bytes 6148
  592.3 4.9 copy-start
  592.3 42.3 %all-to-all-start.1 = ((bf16[16,4,80,128]{3,2,1,0:T(8,128)(2,1)}), bf16[16,4,80,128]{3,2,1,0:T(8,128)(2,1)S(1)}, u32[]{:S(2)}, u32[]{:S(2)}) async-start(bf16[16,4,80,128]{3,2,1,0:T(8,128)(2,1)} %bitcast.21), calls=%async_computation.1 | async-start | bytes 2621440 | tf_op jit(solution)/shard_map/all_to_all | solution.py:446
  597.2 1.6 copy-start.1
  634.6 1.6 copy-start.2
  (2 other events, 1.3 us)

commit v6 on v5

--- a/solution.py
+++ b/solution.py
@@ -14,7 +14,7 @@
 VMEM_LIMIT = 48 * 1024 * 1024
 PACK = 4
 TURN = 8
-HEAD_ROWS = 48
+HEAD_ROWS = 16
 LANES = 128
 FIRST, LAST = slice(0, HALF), slice(-HALF, None)
 END_DELAYS = 2
@@ -234,10 +234,10 @@
     out[...] = staged[...].astype(jnp.bfloat16)
 
 
-def delay_chunk(matrix, high, low, block=16):
-    rows, channels, columns = high.shape
+def delay_chunk(matrix, high, low, begin, rows, block=16):
+    _, channels, columns = high.shape
     count = matrix.shape[0] // 2
-    spec = pl.BlockSpec((block, channels, columns), lambda i: (i, 0, 0))
+    spec = pl.BlockSpec((block, channels, columns), lambda i: (begin // block + i, 0, 0))
     return pl.pallas_call(
         delay_kernel,
         grid=(rows // block,),
@@ -253,38 +253,6 @@
         ),
         name="delays",
     )(matrix, high, low)
-
-
-def correct_kernel(weights, delays, modes, out):
-    _, count, rows, _ = delays.shape
-    mode_count = modes.shape[1]
-
-    @pl.loop(0, rows // HALF)
-    def _(part):
-        here = pl.ds(pl.multiple_of(part * HALF, HALF), HALF)
-        values = [modes[0, m, here].astype(jnp.float32) for m in range(mode_count)]
-        for d in range(count):
-            total = delays[0, d, here].astype(jnp.float32)
-            for m in range(mode_count):
-                total = total - weights[d, m] * values[m]
-            out[0, d, here] = total.astype(jnp.bfloat16)
-
-
-def correct(weights, delays, modes):
-    peers = delays.shape[0]
-    piece = lambda x: pl.BlockSpec((1,) + x.shape[1:], lambda i: (i, 0, 0, 0))
-    return pl.pallas_call(
-        correct_kernel,
-        grid=(peers,),
-        in_specs=[pl.BlockSpec(memory_space=pltpu.SMEM), piece(delays), piece(modes)],
-        out_specs=piece(delays),
-        out_shape=jax.ShapeDtypeStruct(delays.shape, delays.dtype),
-        compiler_params=pltpu.CompilerParams(vmem_limit_bytes=VMEM_LIMIT),
-        cost_estimate=pl.CostEstimate(
-            flops=32 * delays.size, bytes_accessed=4 * delays.size, transcendentals=0
-        ),
-        name="correct",
-    )(weights, delays, modes)
 
 
 def spatial_kernel(row_count, col_count, head, tail, col_table, row_table, *refs):
@@ -360,20 +328,6 @@
     return pinned(lax.ppermute(pinned(x), axis, pairs))
 
 
-def gathered(x):
-    shape = x.shape
-    bits = 0
-    for axis in ("row", "col"):
-        size = lax.axis_size(axis)
-        for bit in reversed(range(size.bit_length() - 1)):
-            other = pinned(lax.ppermute(x, axis, [(i, i ^ (1 << bit)) for i in range(size)]))
-            upper = (lax.axis_index(axis) >> bit) % 2 == 1
-            pair = [jnp.where(upper, other, x), jnp.where(upper, x, other)]
-            x = jnp.stack(pair, axis=bits)
-            bits += 1
-    return x.reshape((-1,) + shape)
-
-
 def outside(length):
     return [*range(-HALF, 0), *range(length, length + HALF)]
 
@@ -421,84 +375,50 @@
         begin = tile_cols + member * 2 * HALF
         col_band[:, member, begin : begin + 2 * HALF] = narrow[:, tile_cols:]
     col_band = col_band.reshape((HALF * PACK,) + col_band.shape[2:])
-    mask = pixel_mask.astype(jnp.float32)
-
-    head_end = HALF + HEAD_ROWS
-    head_rows = list(range(HALF, head_end))
-    tail_rows = [*range(HALF), *range(head_end, tile_rows)]
-    head_span = ((0, head_end + HALF),)
-    tail_spans = ((0, 2 * HALF), (HEAD_ROWS, tile_rows))
-
-    sides_t = [jnp.transpose(x, (2, 1, 0)) for x in (left, right)]
-    sides_t[0], top, bottom = lax.optimization_barrier((sides_t[0], top, bottom))
+    high, low, power = smooth(
+        half_widths,
+        pixel_mask.astype(jnp.float32),
+        centre,
+        [jnp.transpose(x, (2, 1, 0)) for x in (left, right)],
+        [top, bottom, top_ends, bottom_ends],
+        ((0, tile_rows),),
+        band_table(range(tile_rows), [*range(tile_rows), *outside(tile_rows)]),
+        col_band,
+    )
+
+    def exchange(x):
+        return lax.all_to_all(x, ("row", "col"), split_axis=0, concat_axis=0, tiled=True)
 
     modes_t = foreground_modes.T
     delay_table = delay_rows(channels, peers, [per_device])
     mode_delays = exact_dot(delay_table, modes_t)
-    plain_fit = fit(exact_dot(foreground_modes, modes_t), foreground_modes)
-
-    def stacked(matrix, begin, end):
-        matrix = matrix.reshape(peers, per_device, 2, channels)[:, begin:end]
-        return jnp.concatenate(split_high_low(matrix.reshape(-1, channels)), axis=0)
-
-    def exchange(delays, items):
-        delays = delays.reshape(peers, 2 * items, -1, tile_cols)
-        return lax.all_to_all(delays, ("row", "col"), split_axis=0, concat_axis=0, tiled=True)
-
-    head_high, head_low, head_power = smooth(
-        half_widths,
-        mask[HALF:head_end],
-        centre,
-        sides_t,
-        [],
-        head_span,
-        band_table(head_rows, range(head_span[0][1])),
-        col_band,
-    )
-    plain = stacked(delay_table - exact_dot(mode_delays, plain_fit), 0, per_device)
-    head_delays = delay_chunk(plain, head_high, head_low)
-    head_delays, *ends = lax.optimization_barrier((head_delays, top_ends, bottom_ends))
-    head = exchange(head_delays, per_device)
-    top_ends, bottom_ends = ends
-    tail_in = [r for a, b in tail_spans for r in range(a, b)] + outside(tile_rows)
-    tail_high, tail_low, tail_power = smooth(
-        half_widths,
-        jnp.concatenate([mask[:HALF], mask[head_end:]], axis=0),
-        centre,
-        sides_t,
-        [top, bottom, top_ends, bottom_ends],
-        tail_spans,
-        band_table(tail_rows, tail_in),
-        col_band,
-    )
-
-    power_sum = lax.psum(jnp.sum(head_power + tail_power, axis=1), ("row", "col"))
+    tile_power = jnp.broadcast_to(jnp.sum(power, axis=1)[None], (peers, channels))
+    power_sum = jnp.sum(exchange(tile_power), axis=0)
     weights = 1.0 / (power_sum / (sides * columns) + 1e-05)
     channel_weights = weights / jnp.mean(weights)
     weighted_modes = foreground_modes * weights[None, :]
     weighted_fit = fit(exact_dot(weighted_modes, modes_t), weighted_modes)
-    change = jnp.concatenate(split_high_low(weighted_fit - plain_fit), axis=0)
-    amplitude = delay_chunk(change, head_high, head_low)
-    amplitude = gathered(amplitude)
-    matrix = delay_table - exact_dot(mode_delays, weighted_fit)
-
-    place = lax.axis_index("row") * col_count + lax.axis_index("col")
-    own = lax.dynamic_slice_in_dim(mode_delays, place * 2 * per_device, 2 * per_device, axis=0)
-    head = correct(own, head, amplitude)
+    matrix = split_high_low(delay_table - exact_dot(mode_delays, weighted_fit))
+
+    def send(begin, end, first_row, rows):
+        parts = [
+            x.reshape(peers, per_device, 2, channels)[:, begin:end].reshape(-1, channels)
+            for x in matrix
+        ]
+        delays = delay_chunk(jnp.concatenate(parts, axis=0), high, low, first_row, rows)
+        return exchange(delays.reshape(peers, 2 * (end - begin), rows, tile_cols))
 
     cos_c, sin_c = dft_parts(columns)
     col_table = np.block([[cos_c, sin_c], [-sin_c, cos_c]])
     cos_r, sin_r = dft_parts(sides)
-    order = [a * tile_rows + r for a in range(row_count) for r in head_rows + tail_rows]
-    cos_r, sin_r = cos_r[:, order], sin_r[:, order]
     row_table = np.block([[cos_r, -sin_r], [sin_r, cos_r]])
 
     shape = (per_device, 2, sides, columns)
+    head = send(0, per_device, 0, HEAD_ROWS)
     spectrum = None
     start = 0
     for size in chunk_sizes(per_device):
-        delays = delay_chunk(stacked(matrix, start, start + size), tail_high, tail_low)
-        tail = exchange(delays, size)
+        tail = send(start, start + size, HEAD_ROWS, tile_rows - HEAD_ROWS)
         spectrum = spatial_chunk(head, tail, col_table, row_table, shape, start, spectrum)
         start += size
     return (spectrum, channel_weights)
@@ -571,8 +491,6 @@
 def body(sky_cube, half_widths, pixel_mask, foreground_modes):
     tile_rows, tile_cols, channels = sky_cube.shape
     fits = tile_rows % 128 == 0 and tile_cols % 128 == 0 and channels % 128 == 0
-    for axis in ("row", "col"):
-        fits = fits and lax.axis_size(axis) & (lax.axis_size(axis) - 1) == 0
     run = tiled_body if fits else small_tile_body
     return run(sky_cube, half_widths, pixel_mask, foreground_modes)
 

time: 646 us -> 548 us (0.85)
  blocking collectives: 110 us -> 0 us
  waiting for transfers between devices: 226 us -> 301 us
  Pallas kernels: 186 us -> 139 us
  other arithmetic: 14.5 us -> 7.25 us
    all_to_all x3 -> x4, waiting for transfers between devices: 0.01 us -> 285 us  [exchange(): lax.all_to_all(x, ('row', 'col'), split_axis=0, concat_axis=0, tiled=True)]
    ppermute x4 -> x0, waiting for transfers between devices: 223 us -> none  [gathered(): lax.ppermute(x, axis, [(i, i ^ 1 << bit) for i in range(size)])]
    psum x1 -> x0, blocking collectives: 110 us -> none  [tiled_body(): lax.psum(jnp.sum(head_power + tail_power, axis=1), ('row', 'col'))]
    pallas_call x2 -> x1, Pallas kernels: 71 us -> 48.5 us  [smooth(): pl.pallas_call(functools.partial(smooth_kernel, spans, bool(caps)), grid=...]
    pallas_call x1 -> x0, Pallas kernels: 19.7 us -> none  [correct(): pl.pallas_call(correct_kernel, grid=(peers,), in_specs=[pl.BlockSpec(memo...]
    ppermute x6, waiting for transfers between devices: 3.05 us -> 15.8 us  [shifted(): return pinned(lax.ppermute(pinned(x), axis, pairs))]
    ppermute x4 -> x0, starting transfers between devices: 7.86 us -> none  [gathered(): lax.ppermute(x, axis, [(i, i ^ 1 << bit) for i in range(size)])]
    pallas_call x4 -> x3, Pallas kernels: 52.3 us -> 46.1 us  [delay_chunk(): pl.pallas_call(delay_kernel, grid=(rows // block,), in_specs=[pl.BlockSpe...]
  transfers between devices with their start and end apart: 13 -> 10, of which waited for: 5 -> 8; matrix products, arithmetic and copies ran while one was open for 9% -> 7% of each run, Pallas kernels for 28% -> 14%
where the time goes in v6:
time: 548 us; the launch traced here: 546 us
  waiting for transfers between devices  301 us (55%)
  Pallas kernels  139 us (25%)
  local copies, waits for them, and re-layouts  53.1 us (10%)
  starting transfers between devices  40.7 us (7%)
  other arithmetic  7.25 us (1%)
    all_to_all x4, waiting for transfers between devices, exchange(): lax.all_to_all(x, ('row', 'col'), split_axis=0, concat_axis=0, tiled=True)  285 us
    pallas_call x1, Pallas kernels, smooth(): pl.pallas_call(functools.partial(smooth_kernel, spans, bool(caps)), grid=...  48.5 us
    pallas_call x3, Pallas kernels, delay_chunk(): pl.pallas_call(delay_kernel, grid=(rows // block,), in_specs=[pl.BlockSpe...  46.1 us
    pallas_call x2, Pallas kernels, spatial_chunk(): pl.pallas_call(functools.partial(spatial_kernel, row_count, col_count), g...  44.6 us
    all_to_all x4, starting transfers between devices, exchange(): lax.all_to_all(x, ('row', 'col'), split_axis=0, concat_axis=0, tiled=True)  24.8 us
    optimization_barrier x1, local copies, waits for them, and re-layouts, tiled_body(): lax.optimization_barrier((sky_cube, sky_cube[LAST], sky_cube[FIRST]))  23.5 us
    ppermute x6, starting transfers between devices, shifted(): return pinned(lax.ppermute(pinned(x), axis, pairs))  15.8 us
    ppermute x6, waiting for transfers between devices, shifted(): return pinned(lax.ppermute(pinned(x), axis, pairs))  15.8 us
  transfers between devices with their start and end apart: 10, of which 8 were waited for; matrix products, arithmetic and copies ran while one was open for 7% of the time, Pallas kernels for 14%

profile of v6, /device:TPU:11, one launch (start us, length us, event | category | flops | bytes accessed | tf_op | source)
XLA Modules:
  0.0 546.4 jit_solution(7840821312879785135)
XLA Ops:
  0.6 4.6 fusion.16
  5.2 4.7 fusion.15
  10.0 2.7 collective-permute-start.1
  14.0 3.2 collective-permute-start.2
  17.2 3.4 collective-permute-start.3
  20.6 23.5 %copy.20 = bf16[128,128,512]{1,0,2:T(8,128)(2,1)} copy(bf16[128,128,512]{2,1,0:T(8,128)(2,1)} %param.9) | data formatting | bytes 33554432 | tf_op jit(solution)/shard_map/optimization_barrier | solution.py:362
  46.0 1.9 collective-permute-start.4
  48.8 3.4 collective-permute-start.5
  52.2 3.9 copy.22
  56.1 4.2 copy.21
  60.4 1.8 collective-permute-done.2.refs_0_
  62.2 2.9 collective-permute-done.3.refs_1_
  65.1 8.2 %collective-permute-done.4.refs_2_ = bf16[16,32,512]{2,1,0:T(8,128)(2,1)S(1)} collective-permute-done((bf16[16,32,512]{2,1,0:T(8,128)(2,1)}, bf16[16,32,512]{2,1,0:T(8,128)(2,1)S(1)}, u32[]{:S(2)}, u32[]{:S(2)}) %collective-permute-start.4) | collective-permute-done | bytes 524320 | tf_op jit(solution)/shard_map/ppermute | solution.py:328
  73.3 2.9 collective-permute-done.5.refs_3_
  77.5 48.5 %smooth.1 = (bf16[128,512,128]{2,1,0:T(8,128)(2,1)}, bf16[128,512,128]{2,1,0:T(8,128)(2,1)}, f32[512,128]{1,0:T(8,128)S(1)}) custom-call(s32[512]{0:T(512)S(1)} %copy-done.4, f32[128,128]{1,0:T(8,128)S(1)} %convert_element_type.9.mask, bf16[16,128,160]{2,1,0:T(8,128)(2,1)S(1)} %copy-done.5, bf16[64,256,128]{2,1,0:T(8,128)(2,1)} %constant.71.clone.col_band, ...), custom_call_target="tpu_custom_call" | custom-call | flops 34359738368 | bytes 80000000 | tf_op jit(solution)/shard_map/smooth/pallas_call | solution.py:194
  126.7 8.6 %all-to-all-start = ((f32[16,1,512]{2,1,0:T(1,128)}), f32[16,1,512]{2,1,0:T(1,128)S(1)}, u32[]{:S(2)}, u32[]{:S(2)}) async-start(f32[16,1,512]{2,1,0:T(1,128)} %broadcast_in_dim.3), calls=%async_computation | async-start | bytes 65536 | tf_op jit(solution)/shard_map/all_to_all | solution.py:390
  135.4 2.2 fusion.19
  137.6 2.0 all-to-all-done
  140.4 1.5 cholesky.16
  146.1 6.1 %delays.3 = bf16[512,16,128]{2,1,0:T(8,128)(2,1)S(1)} custom-call(bf16[1024,512]{1,0:T(8,128)(2,1)S(1)} %pad_maximum_fusion.matrix, bf16[128,512,128]{2,1,0:T(8,128)(2,1)} %get-tuple-element.18.high, bf16[128,512,128]{2,1,0:T(8,128)(2,1)} %get-tuple-element.19.low), custom_call_target="tpu_custom_call" | custom-call | flops 3221225472 | bytes 6291456 | tf_op jit(solution)/shard_map/delays/pallas_call | solution.py:241
  153.4 6.3 %all-to-all-start.1 = ((bf16[16,32,16,128]{3,2,1,0:T(8,128)(2,1)}), bf16[16,32,16,128]{3,2,1,0:T(8,128)(2,1)S(1)}, u32[]{:S(2)}, u32[]{:S(2)}) async-start(bf16[16,32,16,128]{3,2,1,0:T(8,128)(2,1)} %bitcast.23), calls=%async_computation.1 | async-start | bytes 4194304 | tf_op jit(solution)/shard_map/all_to_all | solution.py:390
  163.0 27.2 %delays.5 = bf16[448,112,128]{2,1,0:T(8,128)(2,1)} custom-call(bf16[896,512]{1,0:T(8,128)(2,1)S(1)} %pad_maximum_fusion.1.matrix, bf16[128,512,128]{2,1,0:T(8,128)(2,1)} %get-tuple-element.18.high, bf16[128,512,128]{2,1,0:T(8,128)(2,1)} %get-tuple-element.19.low), custom_call_target="tpu_custom_call" | custom-call | flops 19730006016 | bytes 42205184 | tf_op jit(solution)/shard_map/delays/pallas_call | solution.py:241
  190.2 17.0 %all-to-all-done.1.head = bf16[16,32,16,128]{3,2,1,0:T(8,128)(2,1)S(1)} async-done(((bf16[16,32,16,128]{3,2,1,0:T(8,128)(2,1)}), bf16[16,32,16,128]{3,2,1,0:T(8,128)(2,1)S(1)}, u32[]{:S(2)}, u32[]{:S(2)}) %all-to-all-start.1) | async-done | bytes 2097184 | tf_op jit(solution)/shard_map/all_to_all | solution.py:390
  207.2 5.0 all-to-all-start.3
  212.3 12.8 %delays.4 = bf16[64,112,128]{2,1,0:T(8,128)(2,1)S(1)} custom-call(bf16[128,512]{1,0:T(8,128)(2,1)S(1)} %pad_maximum_fusion.4.matrix, bf16[128,512,128]{2,1,0:T(8,128)(2,1)} %get-tuple-element.18.high, bf16[128,512,128]{2,1,0:T(8,128)(2,1)} %get-tuple-element.19.low), custom_call_target="tpu_custom_call" | custom-call | flops 2818572288 | bytes 31195136 | tf_op jit(solution)/shard_map/delays/pallas_call | solution.py:241
  226.3 263.7 %all-to-all-done.3.tail = bf16[16,28,112,128]{3,2,1,0:T(8,128)(2,1)} async-done(((bf16[16,28,112,128]{3,2,1,0:T(8,128)(2,1)}), bf16[16,28,112,128]{3,2,1,0:T(8,128)(2,1)}, u32[]{:S(2)}, u32[]{:S(2)}) %all-to-all-start.3) | async-done | bytes 12845088 | tf_op jit(solution)/shard_map/all_to_all | solution.py:390
  490.0 4.9 all-to-all-start.2
  496.2 1.6 copy-done.2
  497.8 36.6 %spatial.2.refs_0_ = f32[16,2,512,512]{3,2,1,0:T(8,128)} custom-call(bf16[16,32,16,128]{3,2,1,0:T(8,128)(2,1)S(1)} %all-to-all-done.1.head, bf16[16,28,112,128]{3,2,1,0:T(8,128)(2,1)} %all-to-all-done.3.tail, bf16[1024,1024]{1,0:T(8,128)(2,1)S(1)} %copy-done.2, bf16[1024,1024]{1,0:T(8,128)(2,1)} %constant.74.clone.row_table), custom_call_target="tpu_custom_call" | custom-call | flops 30064771072 | bytes 44040192 | tf_op jit(solution)/shard_map/spatial/pallas_call | solution.py:303
  534.4 2.5 all-to-all-done.2.tail
  536.8 1.6 copy-done.3
  538.4 8.0 %spatial.3 = f32[16,2,512,512]{3,2,1,0:T(8,128)} custom-call(bf16[16,32,16,128]{3,2,1,0:T(8,128)(2,1)S(1)} %all-to-all-done.1.head, bf16[16,4,112,128]{3,2,1,0:T(8,128)(2,1)} %all-to-all-done.2.tail, bf16[1024,1024]{1,0:T(8,128)(2,1)S(1)} %copy-done.3, bf16[1024,1024]{1,0:T(8,128)(2,1)} %constant.74.clone.row_table, ...), custom_call_target="tpu_custom_call", output_to_operand_aliasing={{}: (4, {})} | custom-call | flops 4294967296 | bytes 6291456 | tf_op jit(solution)/shard_map/spatial/pallas_call | solution.py:303
  (55 shorter events, 17.6 us)
Async XLA Ops:
  10.0 34.1 %collective-permute-start.1 = (bf16[128,16,512]{2,1,0:T(8,128)(2,1)}, bf16[128,16,512]{2,1,0:T(8,128)(2,1)S(1)}, u32[]{:S(2)}, u32[]{:S(2)}) collective-permute-start(bf16[128,16,512]{2,1,0:T(8,128)(2,1)} %get-tuple-element.22), channel_id=1, source_target_pairs={{1,0},{2,1},{3,2},{5,4},{6,5},{7,6},{9,8},{10,9},{11,10},{13,12},{... | collective-permute-start | bytes 6291464 | tf_op jit(solution)/shard_map/ppermute | solution.py:328
  12.7 31.4 %collective-permute-start = (bf16[128,16,512]{2,1,0:T(8,128)(2,1)}, bf16[128,16,512]{2,1,0:T(8,128)(2,1)}, u32[]{:S(2)}, u32[]{:S(2)}) collective-permute-start(bf16[128,16,512]{2,1,0:T(8,128)(2,1)} %get-tuple-element.23), channel_id=1, source_target_pairs={{0,1},{1,2},{2,3},{4,5},{5,6},{6,7},{8,9},{9,10},{10,11},{12,13},{... | collective-permute-start | bytes 6291464 | tf_op jit(solution)/shard_map/ppermute | solution.py:328
  14.0 48.2 %collective-permute-start.2 = (bf16[16,128,512]{2,1,0:T(8,128)(2,1)}, bf16[16,128,512]{2,1,0:T(8,128)(2,1)}, u32[]{:S(2)}, u32[]{:S(2)}) collective-permute-start(bf16[16,128,512]{2,1,0:T(8,128)(2,1)} %get-tuple-element.15), channel_id=1, source_target_pairs={{0,4},{4,8},{8,12},{1,5},{5,9},{9,13},{2,6},{6,10},{10,14},{3,7},{... | collective-permute-start | bytes 6291464 | tf_op jit(solution)/shard_map/ppermute | solution.py:328
  17.2 47.9 %collective-permute-start.3 = (bf16[16,128,512]{2,1,0:T(8,128)(2,1)}, bf16[16,128,512]{2,1,0:T(8,128)(2,1)}, u32[]{:S(2)}, u32[]{:S(2)}) collective-permute-start(bf16[16,128,512]{2,1,0:T(8,128)(2,1)} %get-tuple-element.16), channel_id=1, source_target_pairs={{4,0},{8,4},{12,8},{5,1},{9,5},{13,9},{6,2},{10,6},{14,10},{7,3},{... | collective-permute-start | bytes 6291464 | tf_op jit(solution)/shard_map/ppermute | solution.py:328
  44.0 8.2 %copy-start.8 = (s32[128,128]{1,0:T(8,128)S(1)}, s32[128,128]{1,0:T(8,128)}, u32[]{:S(2)}) copy-start(s32[128,128]{1,0:T(8,128)} %param.11) | copy-start | bytes 196612
  46.0 27.3 %collective-permute-start.4 = (bf16[16,32,512]{2,1,0:T(8,128)(2,1)}, bf16[16,32,512]{2,1,0:T(8,128)(2,1)S(1)}, u32[]{:S(2)}, u32[]{:S(2)}) collective-permute-start(bf16[16,32,512]{2,1,0:T(8,128)(2,1)} %pad_maximum_fusion.2), channel_id=1, source_target_pairs={{0,4},{4,8},{8,12},{1,5},{5,9},{9,13},{2,6},{6,10},{10,14},{3,7},{... | collective-permute-start | bytes 1572872 | tf_op jit(solution)/shard_map/ppermute | solution.py:328
  48.8 27.4 %collective-permute-start.5 = (bf16[16,32,512]{2,1,0:T(8,128)(2,1)}, bf16[16,32,512]{2,1,0:T(8,128)(2,1)S(1)}, u32[]{:S(2)}, u32[]{:S(2)}) collective-permute-start(bf16[16,32,512]{2,1,0:T(8,128)(2,1)} %pad_maximum_fusion.3), channel_id=1, source_target_pairs={{4,0},{8,4},{12,8},{5,1},{9,5},{13,9},{6,2},{10,6},{14,10},{7,3},{... | collective-permute-start | bytes 1572872 | tf_op jit(solution)/shard_map/ppermute | solution.py:328
  56.1 20.1 %copy-start.4 = (s32[512]{0:T(512)S(1)}, s32[512]{0:T(512)}, u32[]{:S(2)}) copy-start(s32[512]{0:T(512)} %widths.1) | copy-start | bytes 6148
  76.2 1.2 copy-start.5
  77.5 57.9 %copy-start.7 = (f32[16,512]{1,0:T(8,128)S(1)}, f32[16,512]{1,0:T(8,128)}, u32[]{:S(2)}) copy-start(f32[16,512]{1,0:T(8,128)} %param.12) | copy-start | bytes 98308
  126.0 18.9 %copy-start.6 = (f32[512,512]{1,0:T(8,128)S(1)}, f32[512,512]{1,0:T(8,128)}, u32[]{:S(2)}) copy-start(f32[512,512]{1,0:T(8,128)} %constant.72.clone) | copy-start | bytes 3145732
  126.7 12.8 %all-to-all-start = ((f32[16,1,512]{2,1,0:T(1,128)}), f32[16,1,512]{2,1,0:T(1,128)S(1)}, u32[]{:S(2)}, u32[]{:S(2)}) async-start(f32[16,1,512]{2,1,0:T(1,128)} %broadcast_in_dim.3), calls=%async_computation | async-start | bytes 65536 | tf_op jit(solution)/shard_map/all_to_all | solution.py:390
  152.1 1.3 copy-start
  153.4 53.7 %all-to-all-start.1 = ((bf16[16,32,16,128]{3,2,1,0:T(8,128)(2,1)}), bf16[16,32,16,128]{3,2,1,0:T(8,128)(2,1)S(1)}, u32[]{:S(2)}, u32[]{:S(2)}) async-start(bf16[16,32,16,128]{3,2,1,0:T(8,128)(2,1)} %bitcast.23), calls=%async_computation.1 | async-start | bytes 4194304 | tf_op jit(solution)/shard_map/all_to_all | solution.py:390
  160.7 1.0 slice-start
  161.7 1.0 slice-start.2
  207.2 5.0 slice-start.1
  207.2 5.1 slice-start.3
  207.2 282.9 %all-to-all-start.3 = ((bf16[16,28,112,128]{3,2,1,0:T(8,128)(2,1)}), bf16[16,28,112,128]{3,2,1,0:T(8,128)(2,1)}, u32[]{:S(2)}, u32[]{:S(2)}) async-start(bf16[16,28,112,128]{3,2,1,0:T(8,128)(2,1)} %bitcast.27), calls=%async_computation.3 | async-start | bytes 25690112 | tf_op jit(solution)/shard_map/all_to_all | solution.py:390
  225.1 1.2 copy-start.1
  490.0 46.8 %all-to-all-start.2 = ((bf16[16,4,112,128]{3,2,1,0:T(8,128)(2,1)}), bf16[16,4,112,128]{3,2,1,0:T(8,128)(2,1)}, u32[]{:S(2)}, u32[]{:S(2)}) async-start(bf16[16,4,112,128]{3,2,1,0:T(8,128)(2,1)} %bitcast.24), calls=%async_computation.2 | async-start | bytes 3670016 | tf_op jit(solution)/shard_map/all_to_all | solution.py:390
  496.2 1.6 copy-start.2
  536.8 1.6 copy-start.3

commit v7 on v6

--- a/solution.py
+++ b/solution.py
@@ -346,10 +346,20 @@
     return rounded.astype(jnp.bfloat16), (x - rounded).astype(jnp.bfloat16)
 
 
-def chunk_sizes(per_device):
-    if per_device <= 4 * END_DELAYS:
-        return [per_device]
-    return [per_device - END_DELAYS, END_DELAYS]
+def exchange_by_pairs(x):
+    rows, cols = lax.axis_size("row"), lax.axis_size("col")
+    place = lax.axis_index("row") * cols + lax.axis_index("col")
+    far = [k for k in range(1, rows * cols) if k // cols >= rows // 2]
+    near = [k for k in range(1, rows * cols) if k // cols < rows // 2]
+    order = [k for pair in zip(far, near) for k in pair] + far[len(near) :]
+    brought = []
+    for k in order:
+        piece = lax.dynamic_slice_in_dim(x, place ^ k, 1, axis=0)
+        pairs = [(i, i ^ k) for i in range(rows * cols)]
+        brought.append(lax.ppermute(piece, ("row", "col"), pairs))
+    for k, piece in zip(order, brought):
+        x = lax.dynamic_update_slice_in_dim(x, piece, place ^ k, axis=0)
+    return x, brought[-4]
 
 
 def tiled_body(sky_cube, half_widths, pixel_mask, foreground_modes):
@@ -363,7 +373,7 @@
     top, bottom = shifted(last, "row", 1), shifted(initial, "row", -1)
     left, right = shifted(sky_cube[:, LAST], "col", 1), shifted(sky_cube[:, FIRST], "col", -1)
     centre = jnp.transpose(sky_cube, (2, 0, 1))
-    left, right, centre = lax.optimization_barrier((left, right, centre))
+    left, right, centre, top, bottom = lax.optimization_barrier((left, right, centre, top, bottom))
     ends = [jnp.concatenate([left[rows], right[rows]], axis=1) for rows in (LAST, FIRST)]
     top_ends, bottom_ends = shifted(ends[0], "row", 1), shifted(ends[1], "row", -1)
 
@@ -400,13 +410,13 @@
     weighted_fit = fit(exact_dot(weighted_modes, modes_t), weighted_modes)
     matrix = split_high_low(delay_table - exact_dot(mode_delays, weighted_fit))
 
-    def send(begin, end, first_row, rows):
+    def delays(begin, end, first_row, rows):
         parts = [
             x.reshape(peers, per_device, 2, channels)[:, begin:end].reshape(-1, channels)
             for x in matrix
         ]
-        delays = delay_chunk(jnp.concatenate(parts, axis=0), high, low, first_row, rows)
-        return exchange(delays.reshape(peers, 2 * (end - begin), rows, tile_cols))
+        part = delay_chunk(jnp.concatenate(parts, axis=0), high, low, first_row, rows)
+        return part.reshape(peers, 2 * (end - begin), rows, tile_cols)
 
     cos_c, sin_c = dft_parts(columns)
     col_table = np.block([[cos_c, sin_c], [-sin_c, cos_c]])
@@ -414,13 +424,15 @@
     row_table = np.block([[cos_r, -sin_r], [sin_r, cos_r]])
 
     shape = (per_device, 2, sides, columns)
-    head = send(0, per_device, 0, HEAD_ROWS)
-    spectrum = None
-    start = 0
-    for size in chunk_sizes(per_device):
-        tail = send(start, start + size, HEAD_ROWS, tile_rows - HEAD_ROWS)
-        spectrum = spatial_chunk(head, tail, col_table, row_table, shape, start, spectrum)
-        start += size
+    rest = tile_rows - HEAD_ROWS
+    split = per_device - END_DELAYS
+    head = exchange(delays(0, per_device, 0, HEAD_ROWS))
+    middle, near_end = exchange_by_pairs(delays(0, split, HEAD_ROWS, rest))
+    last = delays(split, per_device, HEAD_ROWS, rest)
+    last, _ = lax.optimization_barrier((last, near_end))
+    last = exchange(last)
+    spectrum = spatial_chunk(head, middle, col_table, row_table, shape, 0, None)
+    spectrum = spatial_chunk(head, last, col_table, row_table, shape, split, spectrum)
     return (spectrum, channel_weights)
 
 
@@ -491,6 +503,8 @@
 def body(sky_cube, half_widths, pixel_mask, foreground_modes):
     tile_rows, tile_cols, channels = sky_cube.shape
     fits = tile_rows % 128 == 0 and tile_cols % 128 == 0 and channels % 128 == 0
+    for axis in ("row", "col"):
+        fits = fits and lax.axis_size(axis) & (lax.axis_size(axis) - 1) == 0
     run = tiled_body if fits else small_tile_body
     return run(sky_cube, half_widths, pixel_mask, foreground_modes)
 

time: 548 us -> 571 us (1.042)
  waiting for transfers between devices: 301 us -> 255 us
  local copies, waits for them, and re-layouts: 53.1 us -> 89.9 us
  starting transfers between devices: 40.7 us -> 69.7 us
    all_to_all x4 -> x3, waiting for transfers between devices: 285 us -> 1.95 us  [exchange(): lax.all_to_all(x, ('row', 'col'), split_axis=0, concat_axis=0, tiled=True)]
    ppermute x0 -> x15, waiting for transfers between devices: none -> 238 us  [exchange_by_pairs(): brought.append(lax.ppermute(piece, ('row', 'col'), pairs))]
    ppermute x0 -> x15, starting transfers between devices: none -> 32.8 us  [exchange_by_pairs(): brought.append(lax.ppermute(piece, ('row', 'col'), pairs))]
    dynamic_update_slice x0 -> x14, local copies, waits for them, and re-layouts: none -> 26.9 us  [exchange_by_pairs(): x = lax.dynamic_update_slice_in_dim(x, piece, place ^ k, axis=0)]
    dynamic_slice x0 -> x2, local copies, waits for them, and re-layouts: none -> 10 us  [exchange_by_pairs(): piece = lax.dynamic_slice_in_dim(x, place ^ k, 1, axis=0)]
    all_to_all x4 -> x3, starting transfers between devices: 24.8 us -> 20.3 us  [exchange(): lax.all_to_all(x, ('row', 'col'), split_axis=0, concat_axis=0, tiled=True)]
  transfers between devices with their start and end apart: 10 -> 24, of which waited for: 8 -> 13; matrix products, arithmetic and copies ran while one was open for 7% -> 14% of each run, Pallas kernels for 14% -> 13%
where the time goes in v7:
time: 571 us; the launch traced here: 569 us
  waiting for transfers between devices  255 us (45%)
  Pallas kernels  139 us (24%)
  local copies, waits for them, and re-layouts  89.9 us (16%)
  starting transfers between devices  69.7 us (12%)
  other arithmetic  8.4 us (1%)
    ppermute x15, waiting for transfers between devices, exchange_by_pairs(): brought.append(lax.ppermute(piece, ('row', 'col'), pairs))  238 us
    pallas_call x1, Pallas kernels, smooth(): pl.pallas_call(functools.partial(smooth_kernel, spans, bool(caps)), grid=...  48.5 us
    pallas_call x3, Pallas kernels, delay_chunk(): pl.pallas_call(delay_kernel, grid=(rows // block,), in_specs=[pl.BlockSpe...  46.1 us
    pallas_call x2, Pallas kernels, spatial_chunk(): pl.pallas_call(functools.partial(spatial_kernel, row_count, col_count), g...  44.6 us
    ppermute x15, starting transfers between devices, exchange_by_pairs(): brought.append(lax.ppermute(piece, ('row', 'col'), pairs))  32.8 us
    dynamic_update_slice x14, local copies, waits for them, and re-layouts, exchange_by_pairs(): x = lax.dynamic_update_slice_in_dim(x, piece, place ^ k, axis=0)  26.9 us
    optimization_barrier x1, local copies, waits for them, and re-layouts, tiled_body(): lax.optimization_barrier((sky_cube, sky_cube[LAST], sky_cube[FIRST]))  23.5 us
    all_to_all x3, starting transfers between devices, exchange(): lax.all_to_all(x, ('row', 'col'), split_axis=0, concat_axis=0, tiled=True)  20.3 us
  transfers between devices with their start and end apart: 24, of which 13 were waited for; matrix products, arithmetic and copies ran while one was open for 14% of the time, Pallas kernels for 13%

profile of v7, /device:TPU:11, one launch (start us, length us, event | category | flops | bytes accessed | tf_op | source)
XLA Modules:
  0.0 568.6 jit_solution(13850290744931319785)
XLA Ops:
  0.6 4.7 fusion.16
  5.3 3.2 collective-permute-start.2
  8.5 3.4 collective-permute-start.3
  11.9 4.8 fusion.15
  16.6 3.3 collective-permute-start.1
  21.3 23.5 %copy.20 = bf16[128,128,512]{1,0,2:T(8,128)(2,1)} copy(bf16[128,128,512]{2,1,0:T(8,128)(2,1)} %param.9) | data formatting | bytes 33554432 | tf_op jit(solution)/shard_map/optimization_barrier | solution.py:372
  44.8 9.2 %collective-permute-done.2.refs_0_ = bf16[16,128,512]{2,1,0:T(8,128)(2,1)} collective-permute-done((bf16[16,128,512]{2,1,0:T(8,128)(2,1)}, bf16[16,128,512]{2,1,0:T(8,128)(2,1)}, u32[]{:S(2)}, u32[]{:S(2)}) %collective-permute-start.2) | collective-permute-done | bytes 2097184 | tf_op jit(solution)/shard_map/ppermute | solution.py:328
  58.9 3.2 collective-permute-start.4
  65.0 3.9 copy.22
  69.0 4.2 copy.21
  77.5 48.5 %smooth.1 = (bf16[128,512,128]{2,1,0:T(8,128)(2,1)}, bf16[128,512,128]{2,1,0:T(8,128)(2,1)}, f32[512,128]{1,0:T(8,128)S(1)}) custom-call(s32[512]{0:T(512)S(1)} %copy-done.4, f32[128,128]{1,0:T(8,128)S(1)} %convert_element_type.9.mask, bf16[16,128,160]{2,1,0:T(8,128)(2,1)S(1)} %copy-done.5, bf16[64,256,128]{2,1,0:T(8,128)(2,1)} %constant.112.clone.col_band, ...), custom_call_target="tpu_custom_call" | custom-call | flops 34359738368 | bytes 80000000 | tf_op jit(solution)/shard_map/smooth/pallas_call | solution.py:194
  126.8 6.9 %all-to-all-start = ((f32[16,1,512]{2,1,0:T(1,128)}), f32[16,1,512]{2,1,0:T(1,128)S(1)}, u32[]{:S(2)}, u32[]{:S(2)}) async-start(f32[16,1,512]{2,1,0:T(1,128)} %broadcast_in_dim.3), calls=%async_computation | async-start | bytes 65536 | tf_op jit(solution)/shard_map/all_to_all | solution.py:400
  148.6 6.1 %delays.3 = bf16[512,16,128]{2,1,0:T(8,128)(2,1)S(1)} custom-call(bf16[1024,512]{1,0:T(8,128)(2,1)S(1)} %pad_maximum_fusion.matrix, bf16[128,512,128]{2,1,0:T(8,128)(2,1)} %get-tuple-element.23.high, bf16[128,512,128]{2,1,0:T(8,128)(2,1)} %get-tuple-element.24.low), custom_call_target="tpu_custom_call" | custom-call | flops 3221225472 | bytes 6291456 | tf_op jit(solution)/shard_map/delays/pallas_call | solution.py:241
  156.0 6.1 %all-to-all-start.1 = ((bf16[16,32,16,128]{3,2,1,0:T(8,128)(2,1)}), bf16[16,32,16,128]{3,2,1,0:T(8,128)(2,1)S(1)}, u32[]{:S(2)}, u32[]{:S(2)}) async-start(bf16[16,32,16,128]{3,2,1,0:T(8,128)(2,1)} %bitcast.23), calls=%async_computation.1 | async-start | bytes 4194304 | tf_op jit(solution)/shard_map/all_to_all | solution.py:400
  163.3 27.3 %delays.5 = bf16[448,112,128]{2,1,0:T(8,128)(2,1)} custom-call(bf16[896,512]{1,0:T(8,128)(2,1)S(1)} %pad_maximum_fusion.1.matrix, bf16[128,512,128]{2,1,0:T(8,128)(2,1)} %get-tuple-element.23.high, bf16[128,512,128]{2,1,0:T(8,128)(2,1)} %get-tuple-element.24.low), custom_call_target="tpu_custom_call" | custom-call | flops 19730006016 | bytes 42205184 | tf_op jit(solution)/shard_map/delays/pallas_call | solution.py:241
  194.1 47.7 %collective-permute-done.7 = bf16[1,28,112,128]{3,2,1,0:T(8,128)(2,1)} collective-permute-done((bf16[1,28,112,128]{3,2,1,0:T(8,128)(2,1)S(1)}, bf16[1,28,112,128]{3,2,1,0:T(8,128)(2,1)}, u32[]{:S(2)}, u32[]{:S(2)}) %collective-permute-start.7) | collective-permute-done | bytes 802848 | tf_op jit(solution)/shard_map/ppermute | solution.py:359
  241.7 8.8 %constant_dynamic-slice_fusion = (bf16[1,28,112,128]{3,2,1,0:T(8,128)(2,1)S(1)}, bf16[1,28,112,128]{3,2,1,0:T(8,128)(2,1)}, bf16[1,28,112,128]{3,2,1,0:T(8,128)(...) fusion(bf16[16,28,112,128]{3,2,1,0:T(8,128)(2,1)} %bitcast.28, ...), kind=kLoop, calls=%fused_computation.26 | loop fusion | bytes 24084540 | tf_op jit(solution)/shard_map/dynamic_slice | solution.py:357
  259.0 27.6 %collective-permute-done.15 = bf16[1,28,112,128]{3,2,1,0:T(8,128)(2,1)} collective-permute-done((bf16[1,28,112,128]{3,2,1,0:T(8,128)(2,1)}, bf16[1,28,112,128]{3,2,1,0:T(8,128)(2,1)}, u32[]{:S(2)}, u32[]{:S(2)}) %collective-permute-start.15) | collective-permute-done | bytes 802848 | tf_op jit(solution)/shard_map/ppermute | solution.py:359
  286.9 6.3 %collective-permute-done.14 = bf16[1,28,112,128]{3,2,1,0:T(8,128)(2,1)} collective-permute-done((bf16[1,28,112,128]{3,2,1,0:T(8,128)(2,1)}, bf16[1,28,112,128]{3,2,1,0:T(8,128)(2,1)}, u32[]{:S(2)}, u32[]{:S(2)}) %collective-permute-start.14) | collective-permute-done | bytes 802848 | tf_op jit(solution)/shard_map/ppermute | solution.py:359
  294.8 12.8 %delays.4 = bf16[64,112,128]{2,1,0:T(8,128)(2,1)S(1)} custom-call(bf16[128,512]{1,0:T(8,128)(2,1)S(1)} %pad_maximum_fusion.4.matrix, bf16[128,512,128]{2,1,0:T(8,128)(2,1)} %get-tuple-element.23.high, bf16[128,512,128]{2,1,0:T(8,128)(2,1)} %get-tuple-element.24.low), custom_call_target="tpu_custom_call" | custom-call | flops 2818572288 | bytes 31195136 | tf_op jit(solution)/shard_map/delays/pallas_call | solution.py:241
  309.5 27.9 %collective-permute-done.11 = bf16[1,28,112,128]{3,2,1,0:T(8,128)(2,1)} collective-permute-done((bf16[1,28,112,128]{3,2,1,0:T(8,128)(2,1)}, bf16[1,28,112,128]{3,2,1,0:T(8,128)(2,1)}, u32[]{:S(2)}, u32[]{:S(2)}) %collective-permute-start.11) | collective-permute-done | bytes 802848 | tf_op jit(solution)/shard_map/ppermute | solution.py:359
  337.3 7.1 %collective-permute-start.13 = (bf16[1,28,112,128]{3,2,1,0:T(8,128)(2,1)}, bf16[1,28,112,128]{3,2,1,0:T(8,128)(2,1)S(1)}, u32[]{:S(2)}, u32[]{:S(2)}) collective-permute-start(bf16[1,28,112,128]{3,2,1,0:T(8,128)(2,1)} %get-tuple-element.39), channel_id=1, source_target_pairs={{0,11},{1,10},{2,9},{3,8},{4,15},{5,14},{6,13},{7,12},{8,3},{9,2},... | collective-permute-start | bytes 2408456 | tf_op jit(solution)/shard_map/ppermute | solution.py:359
  347.1 24.7 %collective-permute-done.9 = bf16[1,28,112,128]{3,2,1,0:T(8,128)(2,1)} collective-permute-done((bf16[1,28,112,128]{3,2,1,0:T(8,128)(2,1)}, bf16[1,28,112,128]{3,2,1,0:T(8,128)(2,1)}, u32[]{:S(2)}, u32[]{:S(2)}) %collective-permute-start.9) | collective-permute-done | bytes 802848 | tf_op jit(solution)/shard_map/ppermute | solution.py:359
  376.4 3.8 collective-permute-start.17
  389.0 3.3 collective-permute-start.19
  393.3 3.4 collective-permute-start.20
  400.9 43.0 %collective-permute-done.16 = bf16[1,28,112,128]{3,2,1,0:T(8,128)(2,1)S(1)} collective-permute-done((bf16[1,28,112,128]{3,2,1,0:T(8,128)(2,1)}, bf16[1,28,112,128]{3,2,1,0:T(8,128)(2,1)S(1)}, u32[]{:S(2)}, u32[]{:S(2)}) %collective-permute-start.16) | collective-permute-done | bytes 802848 | tf_op jit(solution)/shard_map/ppermute | solution.py:359
  444.8 7.3 %all-to-all-start.2 = ((bf16[16,4,112,128]{3,2,1,0:T(8,128)(2,1)}), bf16[16,4,112,128]{3,2,1,0:T(8,128)(2,1)}, u32[]{:S(2)}, u32[]{:S(2)}) async-start(bf16[16,4,112,128]{3,2,1,0:T(8,128)(2,1)} %bitcast.24), calls=%async_computation.2 | async-start | bytes 3670016 | tf_op jit(solution)/shard_map/all_to_all | solution.py:400
  456.3 42.8 %collective-permute-done.18 = bf16[1,28,112,128]{3,2,1,0:T(8,128)(2,1)} collective-permute-done((bf16[1,28,112,128]{3,2,1,0:T(8,128)(2,1)}, bf16[1,28,112,128]{3,2,1,0:T(8,128)(2,1)}, u32[]{:S(2)}, u32[]{:S(2)}) %collective-permute-start.18) | collective-permute-done | bytes 802848 | tf_op jit(solution)/shard_map/ppermute | solution.py:359
  503.3 15.4 %collective-permute-done.20 = bf16[1,28,112,128]{3,2,1,0:T(8,128)(2,1)} collective-permute-done((bf16[1,28,112,128]{3,2,1,0:T(8,128)(2,1)S(1)}, bf16[1,28,112,128]{3,2,1,0:T(8,128)(2,1)}, u32[]{:S(2)}, u32[]{:S(2)}) %collective-permute-start.20) | collective-permute-done | bytes 802848 | tf_op jit(solution)/shard_map/ppermute | solution.py:359
  522.4 36.6 %spatial.2.refs_0_ = f32[16,2,512,512]{3,2,1,0:T(8,128)} custom-call(bf16[16,32,16,128]{3,2,1,0:T(8,128)(2,1)S(1)} %all-to-all-done.1.head, bf16[16,28,112,128]{3,2,1,0:T(8,128)(2,1)} %constant_dynamic-update-slice_fusion.tail, bf16[1024,1024]{1,0:T(8,128)(2,1)S(1)} %copy-done.2, bf16[1024,1024]{1,0:T(8,128)(2,1)} %constant.115.clone.row_table), custom_call_target="tpu_custom_call" | custom-call | flops 30064771072 | bytes 44040192 | tf_op jit(solution)/shard_map/spatial/pallas_call | solution.py:303
  560.6 8.0 %spatial.3 = f32[16,2,512,512]{3,2,1,0:T(8,128)} custom-call(bf16[16,32,16,128]{3,2,1,0:T(8,128)(2,1)S(1)} %all-to-all-done.1.head, bf16[16,4,112,128]{3,2,1,0:T(8,128)(2,1)} %all-to-all-done.2.tail, bf16[1024,1024]{1,0:T(8,128)(2,1)S(1)} %copy-done.3, bf16[1024,1024]{1,0:T(8,128)(2,1)} %constant.115.clone.row_table, ...), custom_call_target="tpu_custom_call", output_to_operand_aliasing={{}: (4, {})} | custom-call | flops 4294967296 | bytes 6291456 | tf_op jit(solution)/shard_map/spatial/pallas_call | solution.py:303
  (101 shorter events, 82.4 us)
Async XLA Ops:
  5.3 48.7 %collective-permute-start.2 = (bf16[16,128,512]{2,1,0:T(8,128)(2,1)}, bf16[16,128,512]{2,1,0:T(8,128)(2,1)}, u32[]{:S(2)}, u32[]{:S(2)}) collective-permute-start(bf16[16,128,512]{2,1,0:T(8,128)(2,1)} %get-tuple-element.15), channel_id=1, source_target_pairs={{0,4},{4,8},{8,12},{1,5},{5,9},{9,13},{2,6},{6,10},{10,14},{3,7},{... | collective-permute-start | bytes 6291464 | tf_op jit(solution)/shard_map/ppermute | solution.py:328
  8.5 48.4 %collective-permute-start.3 = (bf16[16,128,512]{2,1,0:T(8,128)(2,1)}, bf16[16,128,512]{2,1,0:T(8,128)(2,1)}, u32[]{:S(2)}, u32[]{:S(2)}) collective-permute-start(bf16[16,128,512]{2,1,0:T(8,128)(2,1)} %get-tuple-element.16), channel_id=1, source_target_pairs={{4,0},{8,4},{12,8},{5,1},{9,5},{13,9},{6,2},{10,6},{14,10},{7,3},{... | collective-permute-start | bytes 6291464 | tf_op jit(solution)/shard_map/ppermute | solution.py:328
  16.6 40.3 %collective-permute-start.1 = (bf16[128,16,512]{2,1,0:T(8,128)(2,1)}, bf16[128,16,512]{2,1,0:T(8,128)(2,1)S(1)}, u32[]{:S(2)}, u32[]{:S(2)}) collective-permute-start(bf16[128,16,512]{2,1,0:T(8,128)(2,1)} %get-tuple-element.28), channel_id=1, source_target_pairs={{1,0},{2,1},{3,2},{5,4},{6,5},{7,6},{9,8},{10,9},{11,10},{13,12},{... | collective-permute-start | bytes 6291464 | tf_op jit(solution)/shard_map/ppermute | solution.py:328
  19.9 45.1 %copy-start.10 = (s32[128,128]{1,0:T(8,128)S(1)}, s32[128,128]{1,0:T(8,128)}, u32[]{:S(2)}) copy-start(s32[128,128]{1,0:T(8,128)} %param.11) | copy-start | bytes 196612
  19.9 56.4 %copy-start.4 = (s32[512]{0:T(512)S(1)}, s32[512]{0:T(512)}, u32[]{:S(2)}) copy-start(s32[512]{0:T(512)} %widths.1) | copy-start | bytes 6148
  19.9 37.0 %collective-permute-start = (bf16[128,16,512]{2,1,0:T(8,128)(2,1)}, bf16[128,16,512]{2,1,0:T(8,128)(2,1)}, u32[]{:S(2)}, u32[]{:S(2)}) collective-permute-start(bf16[128,16,512]{2,1,0:T(8,128)(2,1)} %get-tuple-element.29), channel_id=1, source_target_pairs={{0,1},{1,2},{2,3},{4,5},{5,6},{6,7},{8,9},{9,10},{10,11},{12,13},{... | collective-permute-start | bytes 6291464 | tf_op jit(solution)/shard_map/ppermute | solution.py:328
  58.9 14.4 %collective-permute-start.4 = (bf16[16,32,512]{2,1,0:T(8,128)(2,1)}, bf16[16,32,512]{2,1,0:T(8,128)(2,1)S(1)}, u32[]{:S(2)}, u32[]{:S(2)}) collective-permute-start(bf16[16,32,512]{2,1,0:T(8,128)(2,1)} %pad_maximum_fusion.2), channel_id=1, source_target_pairs={{0,4},{4,8},{8,12},{1,5},{5,9},{9,13},{2,6},{6,10},{10,14},{3,7},{... | collective-permute-start | bytes 1572872 | tf_op jit(solution)/shard_map/ppermute | solution.py:328
  62.9 13.4 %collective-permute-start.5 = (bf16[16,32,512]{2,1,0:T(8,128)(2,1)}, bf16[16,32,512]{2,1,0:T(8,128)(2,1)S(1)}, u32[]{:S(2)}, u32[]{:S(2)}) collective-permute-start(bf16[16,32,512]{2,1,0:T(8,128)(2,1)} %pad_maximum_fusion.3), channel_id=1, source_target_pairs={{4,0},{8,4},{12,8},{5,1},{9,5},{13,9},{6,2},{10,6},{14,10},{7,3},{... | collective-permute-start | bytes 1572872 | tf_op jit(solution)/shard_map/ppermute | solution.py:328
  77.5 56.2 %copy-start.9 = (f32[16,512]{1,0:T(8,128)S(1)}, f32[16,512]{1,0:T(8,128)}, u32[]{:S(2)}) copy-start(f32[16,512]{1,0:T(8,128)} %param.12) | copy-start | bytes 98308
  126.8 11.1 %all-to-all-start = ((f32[16,1,512]{2,1,0:T(1,128)}), f32[16,1,512]{2,1,0:T(1,128)S(1)}, u32[]{:S(2)}, u32[]{:S(2)}) async-start(f32[16,1,512]{2,1,0:T(1,128)} %broadcast_in_dim.3), calls=%async_computation | async-start | bytes 65536 | tf_op jit(solution)/shard_map/all_to_all | solution.py:400
  145.7 2.9 copy-start.6
  146.0 2.7 copy-start.7
  156.0 288.8 %all-to-all-start.1 = ((bf16[16,32,16,128]{3,2,1,0:T(8,128)(2,1)}), bf16[16,32,16,128]{3,2,1,0:T(8,128)(2,1)S(1)}, u32[]{:S(2)}, u32[]{:S(2)}) async-start(bf16[16,32,16,128]{3,2,1,0:T(8,128)(2,1)} %bitcast.23), calls=%async_computation.1 | async-start | bytes 4194304 | tf_op jit(solution)/shard_map/all_to_all | solution.py:400
  190.6 68.3 %slice-start = ((bf16[16,16,2,512]{3,2,1,0:T(2,128)(2,1)}), bf16[16,2,2,512]{3,2,1,0:T(2,128)(2,1)S(1)}, s32[]{:S(2)}) async-start(bf16[16,16,2,512]{3,2,1,0:T(2,128)(2,1)} %copy-done.6), calls=%async_computation.3 | async-start | bytes 131072 | tf_op jit(solution)/shard_map/slice | solution.py:415
  190.6 68.4 %slice-start.1 = ((bf16[16,16,2,512]{3,2,1,0:T(2,128)(2,1)}), bf16[16,2,2,512]{3,2,1,0:T(2,128)(2,1)S(1)}, s32[]{:S(2)}) async-start(bf16[16,16,2,512]{3,2,1,0:T(2,128)(2,1)} %copy-done.7), calls=%async_computation.4 | async-start | bytes 131072 | tf_op jit(solution)/shard_map/slice | solution.py:415
  191.9 49.9 %collective-permute-start.7 = (bf16[1,28,112,128]{3,2,1,0:T(8,128)(2,1)S(1)}, bf16[1,28,112,128]{3,2,1,0:T(8,128)(2,1)}, u32[]{:S(2)}, u32[]{:S(2)}) collective-permute-start(bf16[1,28,112,128]{3,2,1,0:T(8,128)(2,1)S(1)} %constant_dynamic-slice_fusion.13), channel_id=1, source_target_pairs={{0,8},{1,9},{2,10},{3,11},{4,12},{5,13},{6,14},{7,15},{8,0},{9,1},... | collective-permute-start | bytes 2408456 | tf_op jit(solution)/shard_map/ppermute | solution.py:359
  250.5 36.1 %collective-permute-start.15 = (bf16[1,28,112,128]{3,2,1,0:T(8,128)(2,1)}, bf16[1,28,112,128]{3,2,1,0:T(8,128)(2,1)}, u32[]{:S(2)}, u32[]{:S(2)}) collective-permute-start(bf16[1,28,112,128]{3,2,1,0:T(8,128)(2,1)} %get-tuple-element.37), channel_id=1, source_target_pairs={{0,12},{1,13},{2,14},{3,15},{4,8},{5,9},{6,10},{7,11},{8,4},{9,5},... | collective-permute-start | bytes 2408456 | tf_op jit(solution)/shard_map/ppermute | solution.py:359
  251.9 41.3 %collective-permute-start.14 = (bf16[1,28,112,128]{3,2,1,0:T(8,128)(2,1)}, bf16[1,28,112,128]{3,2,1,0:T(8,128)(2,1)}, u32[]{:S(2)}, u32[]{:S(2)}) collective-permute-start(bf16[1,28,112,128]{3,2,1,0:T(8,128)(2,1)} %get-tuple-element.38), channel_id=1, source_target_pairs={{0,4},{1,5},{2,6},{3,7},{4,0},{5,1},{6,2},{7,3},{8,12},{9,13},{10,... | collective-permute-start | bytes 2408456 | tf_op jit(solution)/shard_map/ppermute | solution.py:359
  254.9 82.4 %collective-permute-start.11 = (bf16[1,28,112,128]{3,2,1,0:T(8,128)(2,1)}, bf16[1,28,112,128]{3,2,1,0:T(8,128)(2,1)}, u32[]{:S(2)}, u32[]{:S(2)}) collective-permute-start(bf16[1,28,112,128]{3,2,1,0:T(8,128)(2,1)} %get-tuple-element.41), channel_id=1, source_target_pairs={{0,10},{1,11},{2,8},{3,9},{4,14},{5,15},{6,12},{7,13},{8,2},{9,3},... | collective-permute-start | bytes 2408456 | tf_op jit(solution)/shard_map/ppermute | solution.py:359
  255.9 88.5 %collective-permute-start.8 = (bf16[1,28,112,128]{3,2,1,0:T(8,128)(2,1)}, bf16[1,28,112,128]{3,2,1,0:T(8,128)(2,1)}, u32[]{:S(2)}, u32[]{:S(2)}) collective-permute-start(bf16[1,28,112,128]{3,2,1,0:T(8,128)(2,1)} %get-tuple-element.44), channel_id=1, source_target_pairs={{0,1},{1,0},{2,3},{3,2},{4,5},{5,4},{6,7},{7,6},{8,9},{9,8},{10,11... | collective-permute-start | bytes 2408456 | tf_op jit(solution)/shard_map/ppermute | solution.py:359
  257.4 114.4 %collective-permute-start.9 = (bf16[1,28,112,128]{3,2,1,0:T(8,128)(2,1)}, bf16[1,28,112,128]{3,2,1,0:T(8,128)(2,1)}, u32[]{:S(2)}, u32[]{:S(2)}) collective-permute-start(bf16[1,28,112,128]{3,2,1,0:T(8,128)(2,1)} %get-tuple-element.43), channel_id=1, source_target_pairs={{0,9},{1,8},{2,11},{3,10},{4,13},{5,12},{6,15},{7,14},{8,1},{9,0},... | collective-permute-start | bytes 2408456 | tf_op jit(solution)/shard_map/ppermute | solution.py:359
  286.7 89.7 %collective-permute-start.10 = (bf16[1,28,112,128]{3,2,1,0:T(8,128)(2,1)}, bf16[1,28,112,128]{3,2,1,0:T(8,128)(2,1)}, u32[]{:S(2)}, u32[]{:S(2)}) collective-permute-start(bf16[1,28,112,128]{3,2,1,0:T(8,128)(2,1)} %get-tuple-element.42), channel_id=1, source_target_pairs={{0,2},{1,3},{2,0},{3,1},{4,6},{5,7},{6,4},{7,5},{8,10},{9,11},{10,... | collective-permute-start | bytes 2408456 | tf_op jit(solution)/shard_map/ppermute | solution.py:359
  293.2 91.1 %collective-permute-start.12 = (bf16[1,28,112,128]{3,2,1,0:T(8,128)(2,1)}, bf16[1,28,112,128]{3,2,1,0:T(8,128)(2,1)}, u32[]{:S(2)}, u32[]{:S(2)}) collective-permute-start(bf16[1,28,112,128]{3,2,1,0:T(8,128)(2,1)} %get-tuple-element.40), channel_id=1, source_target_pairs={{0,3},{1,2},{2,1},{3,0},{4,7},{5,6},{6,5},{7,4},{8,11},{9,10},{10,... | collective-permute-start | bytes 2408456 | tf_op jit(solution)/shard_map/ppermute | solution.py:359
  337.3 51.7 %collective-permute-start.13 = (bf16[1,28,112,128]{3,2,1,0:T(8,128)(2,1)}, bf16[1,28,112,128]{3,2,1,0:T(8,128)(2,1)S(1)}, u32[]{:S(2)}, u32[]{:S(2)}) collective-permute-start(bf16[1,28,112,128]{3,2,1,0:T(8,128)(2,1)} %get-tuple-element.39), channel_id=1, source_target_pairs={{0,11},{1,10},{2,9},{3,8},{4,15},{5,14},{6,13},{7,12},{8,3},{9,2},... | collective-permute-start | bytes 2408456 | tf_op jit(solution)/shard_map/ppermute | solution.py:359
  344.4 48.8 %collective-permute-start.6 = (bf16[1,28,112,128]{3,2,1,0:T(8,128)(2,1)}, bf16[1,28,112,128]{3,2,1,0:T(8,128)(2,1)S(1)}, u32[]{:S(2)}, u32[]{:S(2)}) collective-permute-start(bf16[1,28,112,128]{3,2,1,0:T(8,128)(2,1)} %get-tuple-element.46), channel_id=1, source_target_pairs={{0,6},{1,7},{2,4},{3,5},{4,2},{5,3},{6,0},{7,1},{8,14},{9,15},{10,... | collective-permute-start | bytes 2408456 | tf_op jit(solution)/shard_map/ppermute | solution.py:359
  371.8 72.1 %collective-permute-start.16 = (bf16[1,28,112,128]{3,2,1,0:T(8,128)(2,1)}, bf16[1,28,112,128]{3,2,1,0:T(8,128)(2,1)S(1)}, u32[]{:S(2)}, u32[]{:S(2)}) collective-permute-start(bf16[1,28,112,128]{3,2,1,0:T(8,128)(2,1)} %get-tuple-element.36), channel_id=1, source_target_pairs={{0,5},{1,4},{2,7},{3,6},{4,1},{5,0},{6,3},{7,2},{8,13},{9,12},{10,... | collective-permute-start | bytes 2408456 | tf_op jit(solution)/shard_map/ppermute | solution.py:359
  376.4 75.7 %collective-permute-start.17 = (bf16[1,28,112,128]{3,2,1,0:T(8,128)(2,1)}, bf16[1,28,112,128]{3,2,1,0:T(8,128)(2,1)}, u32[]{:S(2)}, u32[]{:S(2)}) collective-permute-start(bf16[1,28,112,128]{3,2,1,0:T(8,128)(2,1)} %get-tuple-element.35), channel_id=1, source_target_pairs={{0,13},{1,12},{2,15},{3,14},{4,9},{5,8},{6,11},{7,10},{8,5},{9,4},... | collective-permute-start | bytes 2408456 | tf_op jit(solution)/shard_map/ppermute | solution.py:359
  384.4 114.7 %collective-permute-start.18 = (bf16[1,28,112,128]{3,2,1,0:T(8,128)(2,1)}, bf16[1,28,112,128]{3,2,1,0:T(8,128)(2,1)}, u32[]{:S(2)}, u32[]{:S(2)}) collective-permute-start(bf16[1,28,112,128]{3,2,1,0:T(8,128)(2,1)} %get-tuple-element.34), channel_id=1, source_target_pairs={{0,14},{1,15},{2,12},{3,13},{4,10},{5,11},{6,8},{7,9},{8,6},{9,7},... | collective-permute-start | bytes 2408456 | tf_op jit(solution)/shard_map/ppermute | solution.py:359
  389.0 112.3 %collective-permute-start.19 = (bf16[1,28,112,128]{3,2,1,0:T(8,128)(2,1)}, bf16[1,28,112,128]{3,2,1,0:T(8,128)(2,1)}, u32[]{:S(2)}, u32[]{:S(2)}) collective-permute-start(bf16[1,28,112,128]{3,2,1,0:T(8,128)(2,1)} %get-tuple-element.33), channel_id=1, source_target_pairs={{0,7},{1,6},{2,5},{3,4},{4,3},{5,2},{6,1},{7,0},{8,15},{9,14},{10,... | collective-permute-start | bytes 2408456 | tf_op jit(solution)/shard_map/ppermute | solution.py:359
  393.2 50.6 %copy-start.8 = (bf16[1,28,112,128]{3,2,1,0:T(8,128)(2,1)}, bf16[1,28,112,128]{3,2,1,0:T(8,128)(2,1)S(1)}, u32[]{:S(2)}) copy-start(bf16[1,28,112,128]{3,2,1,0:T(8,128)(2,1)S(1)} %collective-permute-done.6) | copy-start | bytes 2408452
  393.3 125.5 %collective-permute-start.20 = (bf16[1,28,112,128]{3,2,1,0:T(8,128)(2,1)S(1)}, bf16[1,28,112,128]{3,2,1,0:T(8,128)(2,1)}, u32[]{:S(2)}, u32[]{:S(2)}) collective-permute-start(bf16[1,28,112,128]{3,2,1,0:T(8,128)(2,1)S(1)} %get-tuple-element.32), channel_id=1, source_target_pairs={{0,15},{1,14},{2,13},{3,12},{4,11},{5,10},{6,9},{7,8},{8,7},{9,6},... | collective-permute-start | bytes 2408456 | tf_op jit(solution)/shard_map/ppermute | solution.py:359
  444.8 114.3 %all-to-all-start.2 = ((bf16[16,4,112,128]{3,2,1,0:T(8,128)(2,1)}), bf16[16,4,112,128]{3,2,1,0:T(8,128)(2,1)}, u32[]{:S(2)}, u32[]{:S(2)}) async-start(bf16[16,4,112,128]{3,2,1,0:T(8,128)(2,1)} %bitcast.24), calls=%async_computation.2 | async-start | bytes 3670016 | tf_op jit(solution)/shard_map/all_to_all | solution.py:400
  (5 other events, 7.0 us)
